TPU v7x, 128 devices: a whole 4x4x4 slice. The times are simulated.
128 devices in a mesh: lat: 16 (over z_hi, y, core), lon: 8 (over x, z_lo).
Axes of the slice: x: 4, y: 4, z: 4 (z_hi: 2, z_lo: 2; z = z_hi * 2 + z_lo), core: 2. Of those that a mesh axis runs over, the one named last changes fastest.
Arguments:
- inputs: bfloat16 [96, 384, 384], P('lat', 'lon'), may hold values from -16 to 16
- cotangent: bfloat16 [96, 384, 384], P('lat', 'lon'), may hold values from -6 to 6
- norm_gains: float32 [2, 2, 192], replicated, may hold values from 0.25 to 1.75
- qkv_weight: bfloat16 [2, 192, 576], replicated, may hold values from -0.4375 to 0.4375
- out_weight: bfloat16 [2, 192, 192], replicated, may hold values from -0.4375 to 0.4375
- up_weight: bfloat16 [2, 192, 768], replicated, may hold values from -0.4375 to 0.4375
- down_weight: bfloat16 [2, 768, 192], replicated, may hold values from -0.21875 to 0.21875
- bias_table: float32 [2, 16, 6, 3312], P(None, 'lat'), may hold values from -3 to 3
Outputs:
- output: bfloat16 [96, 384, 384], P('lat', 'lon')
- grad_inputs: bfloat16 [96, 384, 384], P('lat', 'lon')
- grad_gains: float32 [2, 2, 192], replicated
- grad_qkv: float32 [2, 192, 576], replicated
- grad_out: float32 [2, 192, 192], replicated
- grad_up: float32 [2, 192, 768], replicated
- grad_down: float32 [2, 768, 192], replicated
- grad_table: float32 [2, 16, 6, 3312], P(None, 'lat')
All inputs are finite; a program needn't handle non-finite values.
Results may differ from a plain program's by a relative error of at most 0.033.
Values may be sent and summed in bfloat16 or wider, within the bound.
No kernel may reach another device: no remote copies, remote signals or barrier semaphores. Data moves between devices by JAX's collectives and lax.ppermute only.
A program may use at most 128 MiB of HBM per device.

v0:
```python
import math

import jax
import jax.numpy as jnp
import numpy as np
from jax import lax
from jax.sharding import PartitionSpec as P

DIM = 192
HEADS = 6
LEVELS = 2
WIN_LAT = 6
WIN_LON = 12
SHIFT_LAT = 3
SHIFT_LON = 6
WIN_TOK = 144
TABLE = 3312


MASK_VALUE = -100.0
NORM_EPS = 1e-05


def passed_along(block, axis, distance):
    devices = range(lax.axis_size(axis))
    route = [((i - distance) % len(devices), i) for i in devices]
    return lax.ppermute(block, axis, route)


def offset_table():
    col_ids = np.arange(WIN_LON)
    offsets = col_ids[:, None] - col_ids[None, :] + WIN_LON - 1
    picked = (np.arange(2 * WIN_LON - 1)[:, None, None] == offsets[None]).astype(np.float32)
    return jnp.asarray(picked.reshape(2 * WIN_LON - 1, WIN_LON * WIN_LON))


def group_mask():
    upper_rows = np.arange(WIN_TOK) // WIN_LON % WIN_LAT >= WIN_LAT - SHIFT_LAT
    return np.where(upper_rows[:, None] != upper_rows[None, :], MASK_VALUE, 0.0).astype(np.float32)


def expand_table(bias_table):
    lat_wins = bias_table.shape[0]
    flat = bias_table.reshape(-1, 2 * WIN_LON - 1)
    spread = jnp.dot(flat, offset_table(), precision=lax.Precision.HIGHEST)
    spread = spread.reshape(lat_wins, HEADS, LEVELS, LEVELS, WIN_LAT, WIN_LAT, WIN_LON, WIN_LON)
    spread = spread.transpose(0, 1, 3, 5, 6, 2, 4, 7)
    return spread.reshape(lat_wins, HEADS, WIN_TOK, WIN_TOK)


def table_sum(grad_bias):
    lat_wins = grad_bias.shape[0]
    shaped = grad_bias.reshape(lat_wins, HEADS, LEVELS, WIN_LAT, WIN_LON, LEVELS, WIN_LAT, WIN_LON)
    shaped = shaped.transpose(0, 1, 5, 2, 6, 3, 4, 7).reshape(-1, WIN_LON * WIN_LON)
    summed = lax.dot_general(
        shaped, offset_table(), (((1,), (1,)), ((), ())), precision=lax.Precision.HIGHEST
    )
    return summed.reshape(lat_wins, HEADS, TABLE)


def to_windows(tokens):
    row_count, col_count = (tokens.shape[0], tokens.shape[1])
    shaped = tokens.reshape(
        row_count // WIN_LAT, WIN_LAT, col_count // WIN_LON, WIN_LON, LEVELS, DIM
    )
    shaped = shaped.transpose(0, 2, 4, 1, 3, 5)
    return shaped.reshape(row_count // WIN_LAT, col_count // WIN_LON, WIN_TOK, DIM)


def from_windows(windows):
    lat_wins, lon_wins = (windows.shape[0], windows.shape[1])
    shaped = windows.reshape(lat_wins, lon_wins, LEVELS, WIN_LAT, WIN_LON, DIM)
    shaped = shaped.transpose(0, 3, 1, 4, 2, 5)
    return shaped.reshape(lat_wins * WIN_LAT, lon_wins * WIN_LON, LEVELS * DIM)


def layer_norm(widened, gain_row):
    shaped = widened.reshape(widened.shape[0], widened.shape[1], LEVELS, DIM)
    centre = jnp.mean(shaped, axis=-1, keepdims=True)
    spread = jnp.mean(jnp.square(shaped - centre), axis=-1, keepdims=True)
    normed = (shaped - centre) * lax.rsqrt(spread + NORM_EPS) * gain_row
    return normed.reshape(widened.shape).astype(jnp.bfloat16)


def prepare_mlp(widened, branch, gain_row):
    hidden_state = widened + branch.astype(jnp.float32)
    return (layer_norm(hidden_state, gain_row), hidden_state)


def activate(pre_act):
    return jax.nn.gelu(pre_act, approximate=False).astype(jnp.bfloat16)


def matmul(left_side, right_side):
    return jnp.dot(left_side, right_side, preferred_element_type=jnp.float32)


def outer_sum(left_side, right_side):
    return lax.dot_general(
        left_side, right_side, (((0,), (0,)), ((), ())), preferred_element_type=jnp.float32
    )


def times_transposed(left_side, right_side):
    return lax.dot_general(
        left_side, right_side, (((1,), (1,)), ((), ())), preferred_element_type=jnp.float32
    )


def split_heads(projections):
    shaped = projections.reshape(projections.shape[:3] + (3, HEADS, DIM // HEADS))
    return (shaped[:, :, :, 0], shaped[:, :, :, 1], shaped[:, :, :, 2])


def attend_forward(projections, bias_full):
    score_scale = 1.0 / math.sqrt(DIM // HEADS)
    queries, key_heads, values = split_heads(projections)
    scores = (
        jnp.einsum("abqhd,abkhd->abhqk", queries, key_heads, preferred_element_type=jnp.float32)
        * score_scale
    )
    scores = scores + bias_full[:, None]
    weights = jnp.exp(scores)
    soft_weights = weights / jnp.sum(weights, axis=-1, keepdims=True)
    rounded = soft_weights.astype(jnp.bfloat16)
    context = jnp.einsum("abhqk,abkhd->abqhd", rounded, values, preferred_element_type=jnp.float32)
    return (
        context.astype(jnp.bfloat16).reshape(projections.shape[:3] + (DIM,)),
        soft_weights,
        rounded,
    )


def attend_backward(projections, soft_weights, rounded, grad_context):
    head_dim = DIM // HEADS
    score_scale = 1.0 / math.sqrt(head_dim)
    queries, key_heads, values = split_heads(projections)
    grad_heads = grad_context.reshape(grad_context.shape[:3] + (HEADS, head_dim))
    grad_values = jnp.einsum(
        "abhqk,abqhd->abkhd", rounded, grad_heads, preferred_element_type=jnp.float32
    ).astype(jnp.bfloat16)
    grad_probs = jnp.einsum(
        "abqhd,abkhd->abhqk", grad_heads, values, preferred_element_type=jnp.float32
    )
    grad_scores = soft_weights * (
        grad_probs - jnp.sum(grad_probs * soft_weights, axis=-1, keepdims=True)
    )
    grad_bias = jnp.sum(grad_scores, axis=1)
    scaled = grad_scores.astype(jnp.bfloat16)
    grad_queries = (
        jnp.einsum("abhqk,abkhd->abqhd", scaled, key_heads, preferred_element_type=jnp.float32)
        * score_scale
    ).astype(jnp.bfloat16)
    grad_keys = (
        jnp.einsum("abhqk,abqhd->abkhd", scaled, queries, preferred_element_type=jnp.float32)
        * score_scale
    ).astype(jnp.bfloat16)
    grad_mixed = jnp.stack([grad_queries, grad_keys, grad_values], axis=3).reshape(
        projections.shape
    )
    return (grad_mixed, grad_bias)


def lat_roll(tokens, upward):
    row_count = tokens.shape[0]
    if upward:
        edge_strip = tokens[:SHIFT_LAT]
        source_step = -1
    else:
        edge_strip = tokens[row_count - SHIFT_LAT :]
        source_step = 1
    arrived = passed_along(edge_strip, "lat", source_step)
    if upward:
        return jnp.concatenate([tokens[SHIFT_LAT:], arrived], axis=0)
    return jnp.concatenate([arrived, tokens[: row_count - SHIFT_LAT]], axis=0)


def lon_roll(tokens, upward):
    col_count = tokens.shape[1]
    if upward:
        edge_strip = tokens[:, :SHIFT_LON]
        source_step = -1
    else:
        edge_strip = tokens[:, col_count - SHIFT_LON :]
        source_step = 1
    arrived = passed_along(edge_strip, "lon", source_step)
    if upward:
        return jnp.concatenate([tokens[:, SHIFT_LON:], arrived], axis=1)
    return jnp.concatenate([arrived, tokens[:, : col_count - SHIFT_LON]], axis=1)


def roll_tokens(tokens, upward):
    return lon_roll(lat_roll(tokens, upward), upward)


def reduce_weights(weight_grads):
    return lax.psum(
        (weight_grads[0], weight_grads[1], weight_grads[2], weight_grads[3], weight_grads[4]),
        ("lat", "lon"),
    )


def block_forward(
    inputs, gains, qkv_weight, out_weight, up_weight, down_weight, bias_table, mask_flags, shifted
):
    widened = inputs.astype(jnp.float32)
    normed, norm_back = jax.vjp(layer_norm, widened, gains[0])
    if shifted:
        normed = roll_tokens(normed, True)
    windows = to_windows(normed)
    flat_in = windows.reshape(-1, DIM)
    projections = (
        matmul(flat_in, qkv_weight).astype(jnp.bfloat16).reshape(windows.shape[:3] + (3 * DIM,))
    )
    bias_full = expand_table(bias_table) + mask_flags[:, None, None, None] * group_mask()
    context, soft_weights, rounded = attend_forward(projections, bias_full)
    flat_ctx = context.reshape(-1, DIM)
    branch = from_windows(matmul(flat_ctx, out_weight).astype(jnp.bfloat16).reshape(windows.shape))
    if shifted:
        branch = roll_tokens(branch, False)
    (normed_mlp, hidden_state), mlp_back = jax.vjp(prepare_mlp, widened, branch, gains[1])
    flat_mlp = normed_mlp.reshape(-1, DIM)
    pre_act = matmul(flat_mlp, up_weight)
    expanded, gelu_back = jax.vjp(activate, pre_act)
    output = (hidden_state + matmul(expanded, down_weight).reshape(hidden_state.shape)).astype(
        jnp.bfloat16
    )

    def backward(grad_output):
        flat_grad = grad_output.reshape(-1, DIM)
        grad_down = outer_sum(expanded, flat_grad)
        grad_pre = gelu_back(times_transposed(flat_grad, down_weight).astype(jnp.bfloat16))[
            0
        ].astype(jnp.bfloat16)
        grad_up = outer_sum(flat_mlp, grad_pre)
        grad_normed = (
            times_transposed(grad_pre, up_weight).astype(jnp.bfloat16).reshape(normed_mlp.shape)
        )
        grad_wide, grad_branch, grad_gain_mlp = mlp_back(
            (grad_normed, grad_output.astype(jnp.float32))
        )
        if shifted:
            grad_branch = roll_tokens(grad_branch, True)
        grad_proj_in = to_windows(grad_branch).reshape(-1, DIM)
        grad_out = outer_sum(flat_ctx, grad_proj_in)
        grad_context = (
            times_transposed(grad_proj_in, out_weight).astype(jnp.bfloat16).reshape(context.shape)
        )
        grad_mixed, grad_bias = attend_backward(projections, soft_weights, rounded, grad_context)
        grad_table = table_sum(grad_bias)
        flat_gm = grad_mixed.reshape(-1, 3 * DIM)
        grad_qkv = outer_sum(flat_in, flat_gm)
        grad_windows = (
            times_transposed(flat_gm, qkv_weight).astype(jnp.bfloat16).reshape(windows.shape)
        )
        grad_attn_in = from_windows(grad_windows)
        if shifted:
            grad_attn_in = roll_tokens(grad_attn_in, False)
        grad_first, grad_gain_attn = norm_back(grad_attn_in)
        grad_inputs = (grad_first + grad_wide).astype(jnp.bfloat16)
        stacked_gains = jnp.stack([grad_gain_attn, grad_gain_mlp])
        return (grad_inputs, (stacked_gains, grad_qkv, grad_out, grad_up, grad_down, grad_table))

    return (output, backward)


def on_device(
    inputs, cotangent, norm_gains, qkv_weight, out_weight, up_weight, down_weight, bias_table
):
    lat_wins = bias_table.shape[1]
    first_flags = jnp.zeros((lat_wins,), jnp.float32)
    window_rows = lax.axis_index("lat") * lat_wins + jnp.arange(lat_wins, dtype=jnp.int32)
    last_flags = (window_rows == lat_wins * lax.axis_size("lat") - 1).astype(jnp.float32)
    first_out, first_back = block_forward(
        inputs,
        norm_gains[0],
        qkv_weight[0],
        out_weight[0],
        up_weight[0],
        down_weight[0],
        bias_table[0],
        first_flags,
        False,
    )
    output, last_back = block_forward(
        first_out,
        norm_gains[1],
        qkv_weight[1],
        out_weight[1],
        up_weight[1],
        down_weight[1],
        bias_table[1],
        last_flags,
        True,
    )
    grad_middle, last_grads = last_back(cotangent)
    grad_inputs, first_grads = first_back(grad_middle)
    stacked_weights = tuple(
        (
            jnp.stack([first_part, last_part])
            for first_part, last_part in zip(first_grads[:5], last_grads[:5])
        )
    )
    summed = reduce_weights(stacked_weights)
    table_terms = jnp.stack([first_grads[5], last_grads[5]])
    table_total = lax.psum(table_terms.astype(jnp.bfloat16), "lon").astype(jnp.float32)
    return (output, grad_inputs, summed[0], summed[1], summed[2], summed[3], summed[4], table_total)


def solution(mesh):
    return jax.shard_map(
        on_device,
        mesh=mesh,
        in_specs=(
            P("lat", "lon", None),
            P("lat", "lon", None),
            P(),
            P(),
            P(),
            P(),
            P(),
            P(None, "lat", None, None),
        ),
        out_specs=(
            P("lat", "lon", None),
            P("lat", "lon", None),
            P(),
            P(),
            P(),
            P(),
            P(),
            P(None, "lat", None, None),
        ),
        check_vma=False,
    )
```

profile of v0, /device:TPU:0, one launch (start us, length us, event | category | flops | bytes accessed | tf_op | source)
XLA Modules:
  0.0 562.1 jit_solution(13438405598810433599)
XLA Ops:
  18.3 5.8 %convolution_bitcast_fusion.1 = f32[1,6,2,6,12,2,6,12]{7,3,6,2,5,1,4,0:T(8,128)S(1)} fusion(f32[12,12,23,1,1,1,1]{2,1,6,5,4,3,0:T(8,128)S(1)} %copy-done.93, f32[6,2,2,6,6,23,1]{5,4,3,2,1,0,6:T(8,128)S(1)} %reshape.616), kind=kOutput, calls=%fused_computation.11 | convolution fusion | flops 34338816 | bytes 590400 | tf_op jit(solution)/shard_map/dot_general | solution.py:45
  24.1 4.4 copy.231
  28.5 5.0 reshape.580
  45.4 5.7 %multiply_convert_fusion.1 = (bf16[576,768]{1,0:T(8,128)(2,1)S(1)}, f32[576,768]{1,0:T(8,128)}, f32[576,768]{1,0:T(8,128)}) fusion(bf16[576,192]{1,0:T(8,128)(2,1)S(1)} %reshape.582, bf16[2,192,768]{2,1,0:T(8,128)(2,1)S(1)} %copy-done.126), kind=kOutput, calls=%fused_computation.47 | convolution fusion | flops 198623232 | bytes 5013504 | tf_op jit(solution)/shard_map/dot_general | solution.py:95
  59.1 5.8 %collective-permute-start = (bf16[3,48,384]{2,1,0:T(8,128)(2,1)}, bf16[3,48,384]{2,1,0:T(8,128)(2,1)S(1)}, u32[]{:S(2)}, u32[]{:S(2)}) collective-permute-start(bf16[3,48,384]{2,1,0:T(8,128)(2,1)} %get-tuple-element.88), channel_id=1, source_target_pairs={{8,0},{16,8},{24,16},{32,24},{40,32},{48,40},{56,48},{64,56},{72,6... | collective-permute-start | bytes 331784 | tf_op jit(solution)/shard_map/ppermute | solution.py:27
  65.2 6.7 %convolution_bitcast_fusion = f32[1,6,2,6,12,2,6,12]{7,3,6,2,5,1,4,0:T(8,128)S(1)} fusion(f32[12,12,23,1,1,1,1]{2,1,6,5,4,3,0:T(8,128)} %constant.116, f32[6,2,2,6,6,23,1]{5,4,3,2,1,0,6:T(8,128)S(1)} %reshape.617), kind=kOutput, calls=%fused_computation.10 | convolution fusion | flops 34338816 | bytes 590400 | tf_op jit(solution)/shard_map/dot_general | solution.py:45
  72.0 4.2 copy.243
  76.2 5.1 reshape.590
  83.9 3.3 collective-permute-start.1
  92.7 2.3 convolution_convert_fusion.2
  95.0 2.3 copy.239
  97.3 3.8 reshape_reshape.46
  120.3 4.7 collective-permute-done.2
  132.3 2.0 collective-permute-done.3
  142.7 2.1 mul.492
  144.8 2.3 mul.493
  147.1 2.1 sub.106
  149.2 2.3 sub.107
  151.5 2.2 multiply_convert_fusion.2
  155.5 5.9 %multiply_convert_fusion = (bf16[576,768]{1,0:T(8,128)(2,1)}, f32[576,768]{1,0:T(8,128)S(1)}, f32[576,768]{1,0:T(8,128)S(1)}) fusion(bf16[576,192]{1,0:T(8,128)(2,1)} %reshape.592, bf16[2,192,768]{2,1,0:T(8,128)(2,1)} %param.19), kind=kOutput, calls=%fused_computation.34 | convolution fusion | flops 198623232 | bytes 5013504 | tf_op jit(solution)/shard_map/dot_general | solution.py:95
  165.2 2.1 copy.251
  167.2 2.2 reshape.606
  171.5 2.6 convolution_bitcast_fusion.2
  176.3 2.3 multiply_reduce_fusion.9
  180.9 2.3 broadcast_in_dim.17
  184.3 2.3 mul.519
  186.6 2.5 fusion.116
  192.8 2.5 convolution_bitcast_fusion.4
  202.7 3.7 multiply_reduce_fusion.1
  206.4 2.2 fusion.30
  225.1 5.9 %reshape.602 = f32[1,6,2,6,12,2,6,12]{7,6,5,4,3,2,1,0:T(8,128)} reshape(f32[6,144,144]{2,1,0:T(8,128)} %copy.282) | data formatting | bytes 995328 | tf_op jit(solution)/shard_map/reshape | solution.py:53
  231.0 7.7 %copy.283 = f32[1,6,2,2,6,6,12,12]{7,6,5,4,3,2,1,0:T(8,128)} copy(f32[1,6,2,2,6,6,12,12]{7,4,2,6,5,3,1,0:T(8,128)} %bitcast.260) | data formatting | bytes 995328 | tf_op jit(solution)/shard_map/transpose | solution.py:54
  238.7 5.0 reshape.603
  243.7 2.3 convolution_convert_fusion.16
  250.6 3.8 collective-permute-done.7
  260.8 3.1 fusion.16
  266.5 2.3 convolution_bitcast_fusion.3
  274.2 2.0 fusion.115
  276.3 2.0 reshape.598
  283.9 2.0 convolution_bitcast_fusion.9
  287.8 2.8 multiply_reduce_fusion
  290.6 2.2 fusion.32
  298.6 4.9 reshape.600
  303.5 7.7 %copy.280 = f32[1,6,2,2,6,6,12,12]{7,6,5,4,3,2,1,0:T(8,128)} copy(f32[1,6,2,2,6,6,12,12]{7,4,2,6,5,3,1,0:T(8,128)} %bitcast.261) | data formatting | bytes 995328 | tf_op jit(solution)/shard_map/transpose | solution.py:54
  311.2 5.0 reshape.601
  334.6 65.4 %psum.42 = f32[2,2,192]{2,1,0:T(2,128)} all-reduce(f32[2,2,192]{2,1,0:T(2,128)S(1)} %pad_maximum_fusion.13), channel_id=1, replica_groups=mesh['lat'=16,'lon'=8] {'lat','lon'}, use_global_device_ids=true, to_apply=%region_32.0 | all-reduce | flops 768 | bytes 6144 | tf_op jit(solution)/shard_map/psum | solution.py:197
  401.6 148.0 %all-reduce.6.cloned.1.call-done = (f32[2,192,576]{2,1,0:T(8,128)}, f32[2,192,192]{2,1,0:T(8,128)}, f32[2,192,768]{2,1,0:T(8,128)}, f32[2,768,192]{1,2,0:T(8,128)}) async-done(((f32[2,192,576]{2,1,0:T(8,128)}, f32[2,192,192]{2,1,0:T(8,128)}, f32[2,192,768]{2,1,0:T(8,128)}, f32[2,768,192]{1,2,0:T(8,128)}), (f32[2,192,576]{2,1,0:T(8,128)}, f32[2,192,192]{2,1,0:T(8,128)}, f32[2,192,768]{2,1,0:T(8,128)}, ...) | async-done | bytes 3538960 | tf_op jit(solution)/shard_map/psum | solution.py:197
  549.7 2.3 copy.360
  (502 shorter events, 168.2 us)
Async XLA Ops:
  7.2 392.8 %all-reduce.4.cloned.1.call-start = ((), (), s32[]{:S(2)}) async-start(), calls=%async_computation | async-start | bytes 212992 | tf_op jit(solution)/shard_map/psum | solution.py:306
  12.8 44.5 %copy-start.116 = (f32[1,1,192]{2,1,0:T(1,128)}, f32[1,1,192]{2,1,0:T(1,128)S(1)}, u32[]{:S(2)}) copy-start(f32[1,1,192]{2,1,0:T(1,128)S(1)} %get-tuple-element.92) | copy-start | bytes 2308
  12.8 116.8 %copy-start.118 = (f32[1,1,192]{2,1,0:T(1,128)}, f32[1,1,192]{2,1,0:T(1,128)S(1)}, u32[]{:S(2)}) copy-start(f32[1,1,192]{2,1,0:T(1,128)S(1)} %get-tuple-element.89) | copy-start | bytes 2308
  16.9 17.2 %copy-start.23 = (bf16[1,4,144,1,6,32]{2,1,5,4,3,0:T(4,128)(2,1)}, bf16[1,4,144,1,6,32]{2,1,5,4,3,0:T(4,128)(2,1)S(1)}, u32[]{:S(2)}) copy-start(bf16[1,4,144,1,6,32]{2,1,5,4,3,0:T(4,128)(2,1)S(1)} %get-tuple-element.75) | copy-start | bytes 663556
  16.9 17.2 %copy-start.25 = (bf16[1,4,144,1,6,32]{2,1,5,4,3,0:T(4,128)(2,1)}, bf16[1,4,144,1,6,32]{2,1,5,4,3,0:T(4,128)(2,1)S(1)}, u32[]{:S(2)}) copy-start(bf16[1,4,144,1,6,32]{2,1,5,4,3,0:T(4,128)(2,1)S(1)} %get-tuple-element.74) | copy-start | bytes 663556
  16.9 18.2 %copy-start.94 = (bf16[1,4,144,1,6,32]{2,1,5,4,3,0:T(4,128)(2,1)}, bf16[1,4,144,1,6,32]{2,1,5,4,3,0:T(4,128)(2,1)S(1)}, u32[]{:S(2)}) copy-start(bf16[1,4,144,1,6,32]{2,1,5,4,3,0:T(4,128)(2,1)S(1)} %get-tuple-element.76) | copy-start | bytes 663556
  28.5 5.0 copy-start.104
  45.3 5.8 %copy-start.74 = (bf16[576,192]{1,0:T(8,128)(2,1)}, bf16[576,192]{1,0:T(8,128)(2,1)S(1)}, u32[]{:S(2)}) copy-start(bf16[576,192]{1,0:T(8,128)(2,1)S(1)} %reshape.582) | copy-start | bytes 663556
  45.4 6.7 %copy-start.88 = (bf16[2,768,192]{1,2,0:T(8,128)(2,1)S(1)}, bf16[2,768,192]{1,2,0:T(8,128)(2,1)}, u32[]{:S(2)}) copy-start(bf16[2,768,192]{1,2,0:T(8,128)(2,1)} %param.20) | copy-start | bytes 1769476
  57.2 7.7 %copy-start.92 = (f32[6,3312]{1,0:T(8,128)S(1)}, f32[6,3312]{1,0:T(8,128)}, u32[]{:S(2)}) copy-start(f32[6,3312]{1,0:T(8,128)} %get-tuple-element.42) | copy-start | bytes 238468
  59.1 24.8 %collective-permute-start = (bf16[3,48,384]{2,1,0:T(8,128)(2,1)}, bf16[3,48,384]{2,1,0:T(8,128)(2,1)S(1)}, u32[]{:S(2)}, u32[]{:S(2)}) collective-permute-start(bf16[3,48,384]{2,1,0:T(8,128)(2,1)} %get-tuple-element.88), channel_id=1, source_target_pairs={{8,0},{16,8},{24,16},{32,24},{40,32},{48,40},{56,48},{64,56},{72,6... | collective-permute-start | bytes 331784 | tf_op jit(solution)/shard_map/ppermute | solution.py:27
  76.2 5.1 copy-start.103
  83.9 4.9 collective-permute-start.1
  92.7 4.6 copy-start.39
  103.9 4.1 copy-start.84
  108.0 10.6 %copy-start.49 = (bf16[576,192]{0,1:T(8,128)(2,1)}, bf16[576,192]{0,1:T(8,128)(2,1)S(1)}, u32[]{:S(2)}) copy-start(bf16[576,192]{0,1:T(8,128)(2,1)S(1)} %reshape_reshape.47) | copy-start | bytes 663556
  109.0 19.7 %copy-start.71 = (f32[6,48,2]{2,1,0:T(8,128)S(1)}, f32[6,48,2]{2,1,0:T(8,128)}, u32[]{:S(2)}) copy-start(f32[6,48,2]{2,1,0:T(8,128)} %copy-done.70) | copy-start | bytes 6916
  110.9 18.6 %copy-start.69 = (f32[6,48,2]{2,1,0:T(8,128)S(1)}, f32[6,48,2]{2,1,0:T(8,128)}, u32[]{:S(2)}) copy-start(f32[6,48,2]{2,1,0:T(8,128)} %copy-done.68) | copy-start | bytes 6916
  116.9 8.1 %collective-permute-start.2 = (bf16[3,48,384]{2,1,0:T(8,128)(2,1)}, bf16[3,48,384]{2,1,0:T(8,128)(2,1)}, u32[]{:S(2)}, u32[]{:S(2)}) collective-permute-start(bf16[3,48,384]{2,1,0:T(8,128)(2,1)} %slice.158), channel_id=1, source_target_pairs={{120,0},{0,8},{8,16},{16,24},{24,32},{32,40},{40,48},{48,56},{56,6... | collective-permute-start | bytes 331784 | tf_op jit(solution)/shard_map/ppermute | solution.py:27
  126.8 7.5 %copy-start.87 = (bf16[6,48,384]{2,1,0:T(8,128)(2,1)}, bf16[6,48,384]{2,1,0:T(8,128)(2,1)S(1)}, u32[]{:S(2)}) copy-start(bf16[6,48,384]{2,1,0:T(8,128)(2,1)S(1)} %constant_dynamic-update-slice_fusion) | copy-start | bytes 663556
  127.5 6.8 %collective-permute-start.3 = (bf16[6,6,384]{2,1,0:T(8,128)(2,1)}, bf16[6,6,384]{2,1,0:T(8,128)(2,1)S(1)}, u32[]{:S(2)}, u32[]{:S(2)}) collective-permute-start(bf16[6,6,384]{2,1,0:T(8,128)(2,1)} %slice.188), channel_id=1, source_target_pairs={{7,0},{0,1},{1,2},{2,3},{3,4},{4,5},{5,6},{6,7},{15,8},{8,9},{9,10... | collective-permute-start | bytes 82952 | tf_op jit(solution)/shard_map/ppermute | solution.py:27
  155.5 6.0 %copy-start.76 = (bf16[576,192]{1,0:T(8,128)(2,1)S(1)}, bf16[576,192]{1,0:T(8,128)(2,1)}, u32[]{:S(2)}) copy-start(bf16[576,192]{1,0:T(8,128)(2,1)} %reshape.594) | copy-start | bytes 663556
  155.5 6.0 %copy-start.89 = (bf16[2,768,192]{1,2,0:T(8,128)(2,1)S(1)}, bf16[2,768,192]{1,2,0:T(8,128)(2,1)}, u32[]{:S(2)}) copy-start(bf16[2,768,192]{1,2,0:T(8,128)(2,1)} %param.20) | copy-start | bytes 1769476
  171.5 3.9 copy-start.22
  171.5 3.9 copy-start.47
  178.6 4.6 copy-start.73
  179.7 6.9 %copy-start.14 = (f32[6,48,384]{2,1,0:T(8,128)S(1)}, f32[6,48,384]{2,1,0:T(8,128)}, u32[]{:S(2)}) copy-start(f32[6,48,384]{2,1,0:T(8,128)} %mul.493) | copy-start | bytes 1327108
  189.8 5.5 collective-permute-start.4
  196.0 4.0 collective-permute-start.5
  198.7 4.1 copy-start.108
  200.4 6.0 %copy-start.41 = (bf16[576,192]{1,0:T(8,128)(2,1)}, bf16[576,192]{1,0:T(8,128)(2,1)S(1)}, u32[]{:S(2)}) copy-start(bf16[576,192]{1,0:T(8,128)(2,1)S(1)} %reshape_reshape.49) | copy-start | bytes 663556
  215.6 8.2 %copy-start.36 = (f32[6,144,144]{1,2,0:T(8,128)S(1)}, f32[6,144,144]{1,2,0:T(8,128)}, u32[]{:S(2)}) copy-start(f32[6,144,144]{1,2,0:T(8,128)} %get-tuple-element.67) | copy-start | bytes 1492996
  221.1 26.2 %collective-permute-start.6 = (bf16[3,48,384]{2,1,0:T(8,128)(2,1)}, bf16[3,48,384]{2,1,0:T(8,128)(2,1)}, u32[]{:S(2)}, u32[]{:S(2)}) collective-permute-start(bf16[3,48,384]{2,1,0:T(8,128)(2,1)} %slice.171), channel_id=1, source_target_pairs={{120,0},{0,8},{8,16},{16,24},{24,32},{32,40},{40,48},{48,56},{56,6... | collective-permute-start | bytes 331784 | tf_op jit(solution)/shard_map/ppermute | solution.py:27
  238.7 7.3 %copy-start.40 = (bf16[576,192]{1,0:T(8,128)(2,1)S(1)}, bf16[576,192]{1,0:T(8,128)(2,1)}, u32[]{:S(2)}) copy-start(bf16[576,192]{1,0:T(8,128)(2,1)} %copy-done.39) | copy-start | bytes 663556
  243.7 4.6 copy-start.91
  243.7 4.7 copy-start.42
  243.7 4.7 copy-start.50
  246.0 8.5 %copy-start.20 = (f32[6,48,2]{2,1,0:T(8,128)S(1)}, f32[6,48,2]{2,1,0:T(8,128)}, u32[]{:S(2)}) copy-start(f32[6,48,2]{2,1,0:T(8,128)} %copy-done.19) | copy-start | bytes 6916
  246.0 8.5 %copy-start.65 = (f32[6,48,2]{2,1,0:T(8,128)S(1)}, f32[6,48,2]{2,1,0:T(8,128)}, u32[]{:S(2)}) copy-start(f32[6,48,2]{2,1,0:T(8,128)} %copy-done.64) | copy-start | bytes 6916
  246.0 8.5 %copy-start.117 = (f32[1,1,192]{2,1,0:T(1,128)S(1)}, f32[1,1,192]{2,1,0:T(1,128)}, u32[]{:S(2)}) copy-start(f32[1,1,192]{2,1,0:T(1,128)} %copy-done.116) | copy-start | bytes 2308
  248.3 8.1 %copy-start.63 = (f32[6,48,2]{2,1,0:T(8,128)S(1)}, f32[6,48,2]{2,1,0:T(8,128)}, u32[]{:S(2)}) copy-start(f32[6,48,2]{2,1,0:T(8,128)} %copy-done.62) | copy-start | bytes 6916
  248.3 6.1 %collective-permute-start.7 = (bf16[6,6,384]{2,1,0:T(8,128)(2,1)S(1)}, bf16[6,6,384]{2,1,0:T(8,128)(2,1)S(1)}, u32[]{:S(2)}, u32[]{:S(2)}) collective-permute-start(bf16[6,6,384]{2,1,0:T(8,128)(2,1)S(1)} %slice.196), channel_id=1, source_target_pairs={{7,0},{0,1},{1,2},{2,3},{3,4},{4,5},{5,6},{6,7},{15,8},{8,9},{9,10... | collective-permute-start | bytes 82952 | tf_op jit(solution)/shard_map/ppermute | solution.py:27
  260.8 4.0 copy-start.121
  260.8 4.0 copy-start.128
  276.3 11.6 %copy-start.3 = (f32[4,6,144,144]{2,3,1,0:T(8,128)S(1)}, f32[4,6,144,144]{2,3,1,0:T(8,128)}, u32[]{:S(2)}) copy-start(f32[4,6,144,144]{2,3,1,0:T(8,128)} %copy-done.2) | copy-start | bytes 5971972
  311.2 5.0 copy-start.110
  311.2 6.3 %copy-start.100 = (bf16[1,1,6,3312]{3,2,1,0:T(8,128)(2,1)S(1)}, bf16[1,1,6,3312]{3,2,1,0:T(8,128)(2,1)}, u32[]{:S(2)}) copy-start(bf16[1,1,6,3312]{3,2,1,0:T(8,128)(2,1)} %stack.124) | copy-start | bytes 119236
  318.3 231.4 %all-reduce.6.cloned.1.call-start = ((), (), s32[]{:S(2)}) async-start(), calls=%async_computation.1 | async-start | bytes 7471104 | tf_op jit(solution)/shard_map/psum | solution.py:197
  (91 other events, 164.2 us)
Sparse Core Ops, SparseCore 0:
  318.4 70.7 all-reduce.3
  396.1 153.5 all-reduce.5
where the time goes:
time: 573 us; the launch traced here: 562 us
  local copies, waits for them, and re-layouts  185 us (32%)
  waiting for transfers between devices  162 us (28%)
  matrix products  74.7 us (13%)
  blocking collectives  65.4 us (11%)
  other arithmetic  46.3 us (8%)
  between operations  16.8 us (3%)
  starting transfers between devices  13 us (2%)
    psum x1, waiting for transfers between devices, reduce_weights(): lax.psum((weight_grads[0], weight_grads[1], weight_grads[2], weight_grads...  148 us
    psum x1, blocking collectives, reduce_weights(): lax.psum((weight_grads[0], weight_grads[1], weight_grads[2], weight_grads...  65.4 us
    unnamed x265, local copies, waits for them, and re-layouts  23.7 us
    dot_general x8, matrix products, matmul(): return jnp.dot(left_side, right_side, preferred_element_type=jnp.float32)  17.3 us
    transpose x2, local copies, waits for them, and re-layouts, table_sum(): shaped.transpose(0, 1, 5, 2, 6, 3, 4, 7).reshape(-1, WIN_LON * WIN_LON)  15.3 us
    ppermute x8, waiting for transfers between devices, passed_along(): return lax.ppermute(block, axis, route)  13.4 us
    dot_general x8, matrix products, outer_sum(): lax.dot_general(left_side, right_side, (((0,), (0,)), ((), ())), preferre...  13.4 us
    ppermute x8, starting transfers between devices, passed_along(): return lax.ppermute(block, axis, route)  12.7 us
  transfers between devices with their start and end apart: 10, of which 6 were waited for; matrix products, arithmetic and copies ran while one was open for 14% of the time, Pallas kernels for 0%

commit v1 on v0

v1 whole, which is shorter than its diff:
```python
import math

import jax
import jax.numpy as jnp
import numpy as np
from jax import lax
from jax.experimental import pallas as pl
from jax.experimental.pallas import tpu as pltpu
from jax.sharding import PartitionSpec as P

DIM = 192
HEADS = 6
HEAD_DIM = 32
UNITS = 768
ROWS = 6
COLS = 48
WIN_COLS = 12
WINDOWS = 4
WIN_TOK = 144
TOKENS = 576
GRID = ROWS * COLS
GROUP = 12
SPAN = 23
WIDE = SPAN * GROUP
QLANES = HEADS * WIN_TOK
STRIP = 32
SOURCE = 288 + 2 * STRIP
NORM_EPS = 1e-05
MASK_VALUE = -100.0
LOG2E = math.log2(math.e)
SCALE = 1.0 / math.sqrt(HEAD_DIM)
WBLOCK = 18 * DIM

F32 = jnp.float32
BF16 = jnp.bfloat16


def token_places():
    t = np.arange(TOKENS)
    w, rest = t // WIN_TOK, t % WIN_TOK
    c, l, r = rest // GROUP, rest % GROUP // ROWS, rest % ROWS
    return r, w * WIN_COLS + c, l


def one_hot(places, size):
    return (places[:, None] == np.arange(size)[None, :]).astype(np.float32)


def grid_picker():
    r, j, _ = token_places()
    return one_hot(r * COLS + j, GRID)


def shifted_picker():
    r, j, _ = token_places()
    half = np.where(r < 3, r, r - 3)
    inner = np.where(r < 3, 0, 144) + half * COLS + j + 6
    edge = np.where(r < 3, 288, 288 + STRIP) + half * 6 + j - 42
    return one_hot(np.where(j < 42, inner, edge), SOURCE)


def returned_picker():
    r, j, _ = token_places()
    half = np.where(r >= 3, r - 3, r)
    inner = np.where(r >= 3, 0, 144) + half * COLS + j
    edge = np.where(r >= 3, 288, 288 + STRIP) + half * 6 + j
    return one_hot(np.where(j >= 6, inner, edge), SOURCE)


def strip_picker():
    picked = np.zeros((2 * STRIP, GRID), np.float32)
    for i in range(3):
        for j in range(6):
            picked[i * 6 + j, (i + 3) * COLS + j] = 1
            picked[STRIP + i * 6 + j, i * COLS + j] = 1
    return picked


def table_rows():
    picked = np.zeros((2, HEADS * 16, HEADS * 24), np.float32)
    for h in range(HEADS):
        for lq in range(2):
            for lp in range(2):
                for rq in range(6):
                    picked[lp, h * 16 + lq * 6 + rq, ((h * 2 + lq) * 2 + lp) * 6 + rq] = 1
    return picked


def table_cols():
    picked = np.zeros((2, 6 * SPAN, WIDE), np.float32)
    for lp in range(2):
        for rp in range(6):
            for d in range(SPAN):
                picked[lp, rp * SPAN + d, d * GROUP + lp * 6 + rp] = 1
    return picked


def nn(a, b):
    return jnp.dot(a, b, preferred_element_type=F32)


def nt(a, b):
    return lax.dot_general(a, b, (((1,), (1,)), ((), ())), preferred_element_type=F32)


def tn(a, b):
    return lax.dot_general(a, b, (((0,), (0,)), ((), ())), preferred_element_type=F32)


def level_mask():
    t = lax.broadcasted_iota(jnp.int32, (TOKENS, DIM), 0)
    return (lax.div(t, 6) & 1) == 1


def gather_tokens(picker, source):
    both = nn(picker, source)
    return jnp.where(level_mask(), both[:, DIM:], both[:, :DIM])


def scatter_tokens(picker, tokens):
    upper = level_mask()
    zero = jnp.zeros_like(tokens)
    both = jnp.concatenate([jnp.where(upper, zero, tokens), jnp.where(upper, tokens, zero)], axis=1)
    return tn(picker, both.astype(BF16))


def normalize(x):
    centre = jnp.mean(x, axis=-1, keepdims=True)
    off = x - centre
    spread = jnp.mean(off * off, axis=-1, keepdims=True)
    inv = lax.rsqrt(spread + NORM_EPS)
    return off * inv, inv


def norm_backward(grad, gain, hat, inv):
    scaled = grad * gain
    mean_one = jnp.mean(scaled, axis=-1, keepdims=True)
    mean_two = jnp.mean(scaled * hat, axis=-1, keepdims=True)
    return inv * (scaled - mean_one - hat * mean_two)


def gelu_parts(x):
    bell = jnp.exp2(x * x * (-0.5 * LOG2E))
    t = 1.0 / (1.0 + (0.3275911 * math.sqrt(0.5)) * jnp.abs(x))
    poly = t * (0.254829592 + t * (-0.284496736 + t * (1.421413741 + t * (-1.453152027 + t * 1.061405429))))
    tail = 0.5 * poly * bell
    below = jnp.where(x >= 0, 1.0 - tail, tail)
    return below, bell * (1.0 / math.sqrt(2.0 * math.pi))


def head_rows():
    lane = lax.div(lax.broadcasted_iota(jnp.int32, (1, DIM), 1), HEAD_DIM)
    return [(lane == h) for h in range(HEADS)]


def stack_heads(x, masks):
    return jnp.concatenate([jnp.where(m, x, jnp.zeros_like(x)) for m in masks], axis=0)


def fold_heads(x, masks):
    folded = x[:WIN_TOK]
    for h in range(1, HEADS):
        folded = jnp.where(masks[h], x[h * WIN_TOK : (h + 1) * WIN_TOK], folded)
    return folded


def expand_table(table_ref, trows_ref, tcols_ref, bias_ref):
    table = table_ref[...] * LOG2E
    high = table.astype(BF16)
    low = (table - high.astype(F32)).astype(BF16)
    wide = jnp.zeros((HEADS * 16, WIDE), F32)
    for lp in range(2):
        for part in (high, low):
            wide += nn(nn(trows_ref[lp], part).astype(BF16), tcols_ref[lp])
    for cq in range(WIN_COLS):
        start = GROUP * (WIN_COLS - 1 - cq)
        row = jnp.concatenate(
            [wide[h * 16 : h * 16 + GROUP, start : start + WIN_TOK] for h in range(HEADS)], axis=1
        )
        bias_ref[cq * GROUP : (cq + 1) * GROUP, :] = row


def add_mask(bias_ref, flag):
    key = lax.broadcasted_iota(jnp.int32, (WIN_TOK, 1), 0)
    query = lax.broadcasted_iota(jnp.int32, (1, QLANES), 1)
    key_up = (lax.div(key, 3) & 1).astype(F32)
    query_up = (lax.div(query, 3) & 1).astype(F32)
    apart = jnp.abs(key_up - query_up)
    bias_ref[...] += apart * (flag * (MASK_VALUE * LOG2E))


def collapse_table(grad_ref, trows_ref, tcols_ref):
    parts = []
    for h in range(HEADS):
        total = None
        for cq in range(WIN_COLS):
            start = GROUP * (WIN_COLS - 1 - cq)
            piece = grad_ref[cq * GROUP : (cq + 1) * GROUP, h * WIN_TOK : (h + 1) * WIN_TOK]
            pads = [jnp.zeros((GROUP, start), F32)] if start else []
            tail = WIDE - start - WIN_TOK
            pads_after = [jnp.zeros((GROUP, tail), F32)] if tail else []
            piece = jnp.concatenate(pads + [piece] + pads_after, axis=1)
            total = piece if total is None else total + piece
        parts.append(jnp.concatenate([total, jnp.zeros((16 - GROUP, WIDE), F32)], axis=0))
    wide = jnp.concatenate(parts, axis=0).astype(BF16)
    result = jnp.zeros((HEADS * 24, 6 * SPAN), F32)
    for lp in range(2):
        narrow = nt(wide, tcols_ref[lp]).astype(BF16)
        result += tn(trows_ref[lp], narrow)
    return result


def attention(q_ref, k_ref, v_ref, bias_ref, probs_ref, ctx_ref, masks):
    for w in range(WINDOWS):
        rows = pl.ds(w * WIN_TOK, WIN_TOK)
        stacked = stack_heads(q_ref[rows, :], masks)
        scores = nt(k_ref[rows, :], stacked) * (SCALE * LOG2E) + bias_ref[...]
        weights = jnp.exp2(scores)
        inverse = 1.0 / jnp.sum(weights, axis=0, keepdims=True)
        probs = (weights * inverse).astype(BF16)
        probs_ref[w] = probs
        ctx_ref[rows, :] = fold_heads(tn(probs, v_ref[rows, :]), masks).astype(BF16)


def attention_back(q_ref, k_ref, v_ref, probs_ref, gctx_ref, dq_ref, dk_ref, dv_ref, grad_ref, masks):
    for w in range(WINDOWS):
        rows = pl.ds(w * WIN_TOK, WIN_TOK)
        stacked_g = stack_heads(gctx_ref[rows, :], masks)
        stacked_q = stack_heads(q_ref[rows, :], masks)
        probs_half = probs_ref[w]
        probs = probs_half.astype(F32)
        grad_probs = nt(v_ref[rows, :], stacked_g)
        inner = jnp.sum(grad_probs * probs, axis=0, keepdims=True)
        grad_scores = probs * (grad_probs - inner)
        if w == 0:
            grad_ref[...] = grad_scores
        else:
            grad_ref[...] += grad_scores
        half = grad_scores.astype(BF16)
        dv_ref[rows, :] = nn(probs_half, stacked_g).astype(BF16)
        dk_ref[rows, :] = (nn(half, stacked_q) * SCALE).astype(BF16)
        dq_ref[rows, :] = (fold_heads(tn(half, k_ref[rows, :]), masks) * SCALE).astype(BF16)


def project(normed, qkv_ref, q_ref, k_ref, v_ref):
    for i, ref in enumerate((q_ref, k_ref, v_ref)):
        ref[...] = nn(normed, qkv_ref[:, i * DIM : (i + 1) * DIM]).astype(BF16)


def put_weights(wbuf_ref, offset, value):
    tiles = value.shape[1] // 128
    for j in range(tiles):
        wbuf_ref[(offset + j) * DIM : (offset + j + 1) * DIM, :] = value[:, j * 128 : (j + 1) * 128].astype(BF16)


def weight_grads(wbuf_ref, normed, dq, dk, dv, ctx, gbranch, normed_mlp, gpre_ref, expanded_ref, g):
    for j in range(3):
        cols = slice(j * 256, (j + 1) * 256)
        put_weights(wbuf_ref, 2 * j, tn(normed_mlp, gpre_ref[:, cols]))
        put_weights(wbuf_ref, 6 + 2 * j, tn(g, expanded_ref[:, cols]))
    put_weights(wbuf_ref, 12, tn(normed, jnp.concatenate([dq, dk], axis=1)))
    put_weights(wbuf_ref, 15, jnp.concatenate([tn(normed, dv), tn(ctx, gbranch)], axis=1))


def attention_backward_part(
    x, gain, qkv_ref, out_ref, ghid, q_ref, k_ref, v_ref, probs_ref, ctx_ref, gctx_ref, dq_ref, dk_ref, dv_ref, grad_ref, masks
):
    gbranch = ghid.astype(BF16)
    gctx_ref[...] = nt(gbranch, out_ref[...]).astype(BF16)
    attention_back(q_ref, k_ref, v_ref, probs_ref, gctx_ref, dq_ref, dk_ref, dv_ref, grad_ref, masks)
    gnormed = nt(dq_ref[...], qkv_ref[:, :DIM])
    gnormed += nt(dk_ref[...], qkv_ref[:, DIM : 2 * DIM])
    gnormed += nt(dv_ref[...], qkv_ref[:, 2 * DIM :])
    gnormed = gnormed.astype(BF16).astype(F32)
    hat, inv = normalize(x)
    gain_grad = jnp.sum(gnormed * hat, axis=0, keepdims=True)
    gblock = norm_backward(gnormed, gain, hat, inv) + ghid
    normed = (hat * gain).astype(BF16)
    return gblock, normed, gbranch, gain_grad


def first_forward(
    x_ref, cot_ref, gains_ref, qkv_ref, out_ref, up_ref, down_ref, table_ref, trows_ref, tcols_ref, pick_ref, strips_ref,
    xw_ref, q_ref, k_ref, v_ref, probs_ref, ctx_ref, hidden_ref, expanded_ref, slope_ref, grid_ref, edges_ref, cot_edges_ref,
    bias_ref,
):
    masks = head_rows()
    cot_edges_ref[...] = nn(strips_ref[...], cot_ref[...]).astype(BF16)
    x = gather_tokens(pick_ref[...], x_ref[...])
    xw_ref[...] = x.astype(BF16)
    hat, _ = normalize(x)
    normed = (hat * gains_ref[0:1, :]).astype(BF16)
    project(normed, qkv_ref, q_ref, k_ref, v_ref)
    expand_table(table_ref, trows_ref, tcols_ref, bias_ref)
    attention(q_ref, k_ref, v_ref, bias_ref, probs_ref, ctx_ref, masks)
    branch = nn(ctx_ref[...], out_ref[...]).astype(BF16)
    hidden = xw_ref[...].astype(F32) + branch.astype(F32)
    hidden_ref[...] = hidden
    hat, _ = normalize(hidden)
    normed_mlp = (hat * gains_ref[1:2, :]).astype(BF16)
    total = hidden
    for j in range(3):
        cols = slice(j * 256, (j + 1) * 256)
        pre = nn(normed_mlp, up_ref[:, cols])
        below, density = gelu_parts(pre)
        expanded = (pre * below).astype(BF16)
        expanded_ref[:, cols] = expanded
        slope_ref[:, cols] = (below + pre * density).astype(BF16)
        total = total + nn(expanded, down_ref[cols, :])
    grid = scatter_tokens(pick_ref[...], total.astype(BF16)).astype(BF16)
    grid_ref[...] = grid
    edges_ref[...] = nn(strips_ref[...], grid).astype(BF16)


def second_both(
    flag_ref, grid_ref, above_ref, edges_ref, cot_ref, cot_above_ref, cot_edges_ref,
    gains_ref, qkv_ref, out_ref, up_ref, down_ref, table_ref, trows_ref, tcols_ref, pick_ref,
    y_ref, back_ref, wbuf_ref, gain_grad_ref, table_grad_ref,
    source_ref, x_ref, q_ref, k_ref, v_ref, probs_ref, ctx_ref, bias_ref, gctx_ref, dq_ref, dk_ref, dv_ref, gpre_ref, expanded_ref,
):
    masks = head_rows()

    def assemble(grid, above, edges):
        source_ref[0:144, :] = grid[144:288, :]
        source_ref[144:288, :] = above[...]
        source_ref[288:SOURCE, :] = edges[...]
        return gather_tokens(pick_ref[...], source_ref[...])

    x_ref[...] = assemble(grid_ref, above_ref, edges_ref)
    hat, _ = normalize(x_ref[...])
    normed = (hat * gains_ref[0:1, :]).astype(BF16)
    project(normed, qkv_ref, q_ref, k_ref, v_ref)
    expand_table(table_ref, trows_ref, tcols_ref, bias_ref)
    add_mask(bias_ref, flag_ref[0])
    attention(q_ref, k_ref, v_ref, bias_ref, probs_ref, ctx_ref, masks)
    branch = nn(ctx_ref[...], out_ref[...]).astype(BF16)
    hidden = x_ref[...] + branch.astype(F32)
    hat_mlp, inv_mlp = normalize(hidden)
    normed_mlp = (hat_mlp * gains_ref[1:2, :]).astype(BF16)
    g32 = assemble(cot_ref, cot_above_ref, cot_edges_ref)
    g = g32.astype(BF16)
    total = hidden
    gnormed = jnp.zeros((TOKENS, DIM), F32)
    for j in range(3):
        cols = slice(j * 256, (j + 1) * 256)
        pre = nn(normed_mlp, up_ref[:, cols])
        below, density = gelu_parts(pre)
        expanded = (pre * below).astype(BF16)
        expanded_ref[:, cols] = expanded
        total = total + nn(expanded, down_ref[cols, :])
        gact = nt(g, down_ref[cols, :]).astype(BF16).astype(F32)
        gpre = ((below + pre * density) * gact).astype(BF16)
        gpre_ref[:, cols] = gpre
        gnormed = gnormed + nt(gpre, up_ref[:, cols])
    y_ref[...] = scatter_tokens(pick_ref[...], total.astype(BF16)).astype(BF16)
    gnormed = gnormed.astype(BF16).astype(F32)
    gain_grad_ref[1:2, :] = jnp.sum(gnormed * hat_mlp, axis=0, keepdims=True)
    ghid = g32 + norm_backward(gnormed, gains_ref[1:2, :], hat_mlp, inv_mlp)
    gblock, normed, gbranch, gain_grad = attention_backward_part(
        x_ref[...], gains_ref[0:1, :], qkv_ref, out_ref, ghid,
        q_ref, k_ref, v_ref, probs_ref, ctx_ref, gctx_ref, dq_ref, dk_ref, dv_ref, bias_ref, masks,
    )
    gain_grad_ref[0:1, :] = gain_grad
    back_ref[...] = scatter_tokens(pick_ref[...], gblock.astype(BF16)).astype(BF16)
    weight_grads(
        wbuf_ref, normed, dq_ref[...], dk_ref[...], dv_ref[...], ctx_ref[...], gbranch, normed_mlp, gpre_ref, expanded_ref, g
    )
    table_grad_ref[...] = collapse_table(bias_ref, trows_ref, tcols_ref).astype(BF16)


def first_backward(
    back_ref, above_ref, edges_ref, xw_ref, q_ref, k_ref, v_ref, probs_ref, ctx_ref, hidden_ref, expanded_ref, slope_ref,
    gains_ref, qkv_ref, out_ref, up_ref, down_ref, trows_ref, tcols_ref, pick_ref, returned_ref,
    gin_ref, wbuf_ref, gain_grad_ref, table_grad_ref,
    source_ref, gctx_ref, dq_ref, dk_ref, dv_ref, gpre_ref, grad_ref,
):
    masks = head_rows()
    source_ref[0:144, :] = back_ref[0:144, :]
    source_ref[144:288, :] = above_ref[...]
    source_ref[288:SOURCE, :] = edges_ref[...]
    g32 = gather_tokens(returned_ref[...], source_ref[...])
    g = g32.astype(BF16)
    hat_mlp, inv_mlp = normalize(hidden_ref[...])
    normed_mlp = (hat_mlp * gains_ref[1:2, :]).astype(BF16)
    gnormed = jnp.zeros((TOKENS, DIM), F32)
    for j in range(3):
        cols = slice(j * 256, (j + 1) * 256)
        gact = nt(g, down_ref[cols, :]).astype(BF16).astype(F32)
        gpre = (slope_ref[:, cols].astype(F32) * gact).astype(BF16)
        gpre_ref[:, cols] = gpre
        gnormed = gnormed + nt(gpre, up_ref[:, cols])
    gnormed = gnormed.astype(BF16).astype(F32)
    gain_grad_ref[1:2, :] = jnp.sum(gnormed * hat_mlp, axis=0, keepdims=True)
    ghid = g32 + norm_backward(gnormed, gains_ref[1:2, :], hat_mlp, inv_mlp)
    gblock, normed, gbranch, gain_grad = attention_backward_part(
        xw_ref[...].astype(F32), gains_ref[0:1, :], qkv_ref, out_ref, ghid,
        q_ref, k_ref, v_ref, probs_ref, ctx_ref, gctx_ref, dq_ref, dk_ref, dv_ref, grad_ref, masks,
    )
    gain_grad_ref[0:1, :] = gain_grad
    gin_ref[...] = scatter_tokens(pick_ref[...], gblock.astype(BF16)).astype(BF16)
    weight_grads(
        wbuf_ref, normed, dq_ref[...], dk_ref[...], dv_ref[...], ctx_ref[...], gbranch, normed_mlp, gpre_ref, expanded_ref, g
    )
    table_grad_ref[...] = collapse_table(grad_ref, trows_ref, tcols_ref).astype(BF16)


def whole(array):
    return pl.BlockSpec(array.shape, lambda i: (0,) * array.ndim)


def picked(array, index):
    rest = array.shape[1:]
    return pl.BlockSpec((None,) + rest, lambda i: (index,) + (0,) * len(rest))


def call(kernel, operands, specs, outs, scratch):
    shapes = [jax.ShapeDtypeStruct(shape, dtype) for shape, dtype in outs]
    return pl.pallas_call(
        kernel,
        grid=(1,),
        out_shape=shapes,
        in_specs=specs,
        out_specs=[whole(s) for s in shapes],
        scratch_shapes=[pltpu.VMEM(shape, dtype) for shape, dtype in scratch],
        compiler_params=pltpu.CompilerParams(vmem_limit_bytes=56 * 1024 * 1024),
    )(*operands)


def neighbour(axes, sizes, steps):
    pairs = []
    for a in range(sizes[0]):
        for b in range(sizes[1]):
            source = ((a + steps[0]) % sizes[0]) * sizes[1] + (b + steps[1]) % sizes[1]
            pairs.append((source, a * sizes[1] + b))
    return pairs


def exchange(rows, edges, sizes, step):
    both = ("lat", "lon")
    above = lax.ppermute(rows, both, neighbour(both, sizes, (step, 0)))
    side = lax.ppermute(edges[:STRIP], both, neighbour(both, sizes, (0, step)))
    corner = lax.ppermute(edges[STRIP:], both, neighbour(both, sizes, (step, step)))
    return above, jnp.concatenate([side, corner], axis=0)


def total_sum(wbuf_first, wbuf_last, gains_first, gains_last):
    gains = jnp.concatenate([gains_first, gains_last]).reshape(-1).astype(BF16)
    flat = jnp.concatenate([wbuf_first, wbuf_last, jnp.pad(gains, (0, 256 * 128 - 768)).reshape(256, 128)])
    parts = lax.all_to_all(flat.reshape(128, 56, 128), ("lat", "lon"), 0, 0, tiled=False)
    mine = jnp.sum(parts.astype(F32), axis=0).astype(BF16)
    spread = jnp.broadcast_to(mine[None], (128, 56, 128))
    full = lax.all_to_all(spread, ("lat", "lon"), 0, 0, tiled=False)
    return full.reshape(128 * 56, 128)


def on_device(sizes, inputs, cotangent, norm_gains, qkv_weight, out_weight, up_weight, down_weight, bias_table):
    x = inputs.reshape(GRID, 2 * DIM)
    cot = cotangent.reshape(GRID, 2 * DIM)
    tables = bias_table.reshape(2, HEADS * 24, 6 * SPAN)
    trows, tcols = jnp.asarray(table_rows(), BF16), jnp.asarray(table_cols(), BF16)
    pick_grid, pick_shift, pick_back = (
        jnp.asarray(m, BF16) for m in (grid_picker(), shifted_picker(), returned_picker())
    )
    strips = jnp.asarray(strip_picker(), BF16)
    last = (lax.axis_index("lat") == sizes[0] - 1).astype(F32).reshape(1)
    weights = (norm_gains, qkv_weight, out_weight, up_weight, down_weight)
    tok = (TOKENS, DIM)

    operands = [x, cot, *weights, tables, trows, tcols, pick_grid, strips]
    specs = [whole(x), whole(cot)] + [picked(a, 0) for a in (*weights, tables)]
    specs += [whole(a) for a in (trows, tcols, pick_grid, strips)]
    outs = [(tok, BF16), (tok, BF16), (tok, BF16), (tok, BF16), ((WINDOWS, WIN_TOK, QLANES), BF16), (tok, BF16), (tok, F32)]
    outs += [((TOKENS, UNITS), BF16), ((TOKENS, UNITS), BF16), ((GRID, 2 * DIM), BF16), ((2 * STRIP, 2 * DIM), BF16)]
    outs += [((2 * STRIP, 2 * DIM), BF16)]
    results = call(first_forward, operands, specs, outs, [((WIN_TOK, QLANES), F32)])
    saved, grid, edges, cot_edges = results[:9], results[9], results[10], results[11]

    above, edges = exchange(grid[:144], edges, sizes, 1)
    cot_above, cot_edges = exchange(cot[:144], cot_edges, sizes, 1)

    operands = [last, grid, above, edges, cot, cot_above, cot_edges, *weights, tables, trows, tcols, pick_shift]
    specs = [pl.BlockSpec(memory_space=pltpu.SMEM)]
    specs += [whole(a) for a in (grid, above, edges, cot, cot_above, cot_edges)]
    specs += [picked(a, 1) for a in (*weights, tables)] + [whole(a) for a in (trows, tcols, pick_shift)]
    src = (SOURCE, 2 * DIM)
    outs = [(src, BF16), (src, BF16), ((WBLOCK, 128), BF16), ((2, DIM), F32), ((HEADS * 24, 6 * SPAN), BF16)]
    scratch = [(src, BF16), (tok, F32), (tok, BF16), (tok, BF16), (tok, BF16), ((WINDOWS, WIN_TOK, QLANES), BF16), (tok, BF16)]
    scratch += [((WIN_TOK, QLANES), F32)] + [(tok, BF16)] * 4 + [((TOKENS, UNITS), BF16)] * 2
    y_src, back, wbuf_last, gains_last, table_last = call(second_both, operands, specs, outs, scratch)

    back_above, back_edges = exchange(back[144:288], back[288:], sizes, -1)
    operands = [back, back_above, back_edges, *saved, *weights, trows, tcols, pick_grid, pick_back]
    specs = [whole(a) for a in (back, back_above, back_edges, *saved)] + [picked(a, 0) for a in weights]
    specs += [whole(a) for a in (trows, tcols, pick_grid, pick_back)]
    outs = [((GRID, 2 * DIM), BF16), ((WBLOCK, 128), BF16), ((2, DIM), F32), ((HEADS * 24, 6 * SPAN), BF16)]
    scratch = [(src, BF16)] + [(tok, BF16)] * 4 + [((TOKENS, UNITS), BF16), ((WIN_TOK, QLANES), F32)]
    grad_inputs, wbuf_first, gains_first, table_first = call(first_backward, operands, specs, outs, scratch)

    y_above, y_edges = exchange(y_src[144:288], y_src[288:], sizes, -1)
    rows = jnp.concatenate([y_above, y_src[:144]]).reshape(ROWS, COLS, 2 * DIM)
    corner = y_edges[STRIP : STRIP + 18].reshape(3, 6, 2 * DIM)
    side = y_edges[:18].reshape(3, 6, 2 * DIM)
    output = jnp.concatenate([jnp.concatenate([corner, side]), rows[:, 6:]], axis=1)

    full = total_sum(wbuf_first, wbuf_last, gains_first, gains_last)
    weight_part = full[: 2 * WBLOCK].reshape(2, 18, DIM, 128).transpose(0, 2, 1, 3).reshape(2, DIM, 18 * 128).astype(F32)
    grad_up = weight_part[:, :, :UNITS]
    grad_down = weight_part[:, :, UNITS : 2 * UNITS].transpose(0, 2, 1)
    grad_qkv = weight_part[:, :, 2 * UNITS : 2 * UNITS + 3 * DIM]
    grad_out = weight_part[:, :, 2 * UNITS + 3 * DIM :]
    grad_gains = full[2 * WBLOCK : 2 * WBLOCK + 6].reshape(2, 2, DIM).astype(F32)
    table_terms = jnp.stack([table_first, table_last]).reshape(2, 1, HEADS, 24 * 6 * SPAN)
    grad_table = lax.psum(table_terms, "lon").astype(F32)
    return (output, grad_inputs.reshape(ROWS, COLS, 2 * DIM), grad_gains, grad_qkv, grad_out, grad_up, grad_down, grad_table)


def solution(mesh):
    sizes = (mesh.shape["lat"], mesh.shape["lon"])

    def program(*arguments):
        return on_device(sizes, *arguments)

    fields, tables = P("lat", "lon", None), P(None, "lat", None, None)
    return jax.shard_map(
        program,
        mesh=mesh,
        in_specs=(fields, fields, P(), P(), P(), P(), P(), tables),
        out_specs=(fields, fields, P(), P(), P(), P(), P(), tables),
        check_vma=False,
    )
```

time: 573 us -> 231 us (0.40); the launches traced: 562 us -> 230 us
  local copies, waits for them, and re-layouts: 185 us -> 15 us
  matrix products: 74.7 us -> 0 us
  waiting for transfers between devices: 162 us -> 97.9 us
  other arithmetic: 46.3 us -> 9.81 us
  Pallas kernels: 0 us -> 34.9 us
  blocking collectives: 65.4 us -> 33.1 us
  starting transfers between devices: 13 us -> 25.6 us
    psum x2 -> x1, waiting for transfers between devices: 148 us -> 67.9 us  [on_device(): grad_table = lax.psum(table_terms, 'lon').astype(F32)]
    dot_general x40 -> x0, matrix products: 74.7 us -> none  [the longest x8 17.3 us: matmul(): return jnp.dot(left_side, right_side, preferred_element_type=jnp.float32)]
    psum x1 -> x0, blocking collectives: 65.4 us -> none  [reduce_weights(): lax.psum((weight_grads[0], weight_grads[1], weight_grads[2], weight_grads...]
    reshape x24 -> x4, local copies, waits for them, and re-layouts: 45.2 us -> 0.96 us  [the longest x1 0.92 us: on_device(): tables = bias_table.reshape(2, HEADS * 24, 6 * SPAN)]
    pallas_call x0 -> x3, Pallas kernels: none -> 34.9 us  [call(): pl.pallas_call(kernel, grid=(1,), out_shape=shapes, in_specs=specs, out_s...]
    all_to_all x0 -> x1, blocking collectives: none -> 33.1 us  [total_sum(): lax.all_to_all(flat.reshape(128, 56, 128), ('lat', 'lon'), 0, 0, tiled=Fa...]
    reduce_sum x25 -> x1, other arithmetic: 23.8 us -> 0.31 us  [total_sum(): mine = jnp.sum(parts.astype(F32), axis=0).astype(BF16)]
    transpose x4 -> x1, local copies, waits for them, and re-layouts: 24 us -> 1.62 us  [on_device(): grad_down = weight_part[:, :, UNITS:2 * UNITS].transpose(0, 2, 1)]
  transfers between devices with their start and end apart: 10 -> 14, of which waited for: 6 -> 6; matrix products, arithmetic and copies ran while one was open for 14% -> 4% of each run, Pallas kernels for 0% -> 0%
where the time goes in v1:
time: 231 us; the launch traced here: 230 us
  waiting for transfers between devices  97.9 us (42%)
  Pallas kernels  34.9 us (15%)
  blocking collectives  33.1 us (14%)
  starting transfers between devices  25.6 us (11%)
  local copies, waits for them, and re-layouts  15 us (6%)
  between operations  14.2 us (6%)
  other arithmetic  9.81 us (4%)
    psum x1, waiting for transfers between devices, on_device(): grad_table = lax.psum(table_terms, 'lon').astype(F32)  67.9 us
    pallas_call x3, Pallas kernels, call(): pl.pallas_call(kernel, grid=(1,), out_shape=shapes, in_specs=specs, out_s...  34.9 us
    all_to_all x1, blocking collectives, total_sum(): lax.all_to_all(flat.reshape(128, 56, 128), ('lat', 'lon'), 0, 0, tiled=Fa...  33.1 us
    ppermute x4, waiting for transfers between devices, exchange(): side = lax.ppermute(edges[:STRIP], both, neighbour(both, sizes, (0, step)))  21.7 us
    ppermute x4, starting transfers between devices, exchange(): above = lax.ppermute(rows, both, neighbour(both, sizes, (step, 0)))  9.38 us
    ppermute x4, starting transfers between devices, exchange(): lax.ppermute(edges[STRIP:], both, neighbour(both, sizes, (step, step)))  7.18 us
    ppermute x4, waiting for transfers between devices, exchange(): lax.ppermute(edges[STRIP:], both, neighbour(both, sizes, (step, step)))  7.03 us
    all_to_all x1, starting transfers between devices, total_sum(): full = lax.all_to_all(spread, ('lat', 'lon'), 0, 0, tiled=False)  4.93 us
  transfers between devices with their start and end apart: 14, of which 6 were waited for; matrix products, arithmetic and copies ran while one was open for 4% of the time, Pallas kernels for 0%

profile of v1, /device:TPU:0, one launch (start us, length us, event | category | flops | bytes accessed | tf_op | source)
XLA Modules:
  0.0 230.4 jit_solution(5950716521576625812)
XLA Ops:
  7.2 2.2 copy.27.down_ref
  9.4 1.3 reduce.1
  10.7 0.9 reshape.73.table_ref
  11.6 10.4 %shard_map.197 = (bf16[576,192]{1,0:T(8,128)(2,1)}, bf16[576,192]{1,0:T(8,128)(2,1)}, bf16[576,192]{1,0:T(8,128)(2,1)}, bf16[576,192]{1,0:T(8,128)(2,1)}, bf16[4...) custom-call(bf16[288,384]{1,0:T(8,128)(2,1)} %bitcast.27, ...), custom_call_target="tpu_custom_call" | custom-call | tf_op jit(solution)/shard_map/pallas_call | solution.py:418
  22.1 0.9 slice.75
  23.0 5.9 %collective-permute-start = (bf16[144,384]{1,0:T(8,128)(2,1)S(1)}, bf16[144,384]{1,0:T(8,128)(2,1)S(1)}, u32[]{:S(2)}, u32[]{:S(2)}) collective-permute-start(bf16[144,384]{1,0:T(8,128)(2,1)S(1)} %slice.75), channel_id=1, source_target_pairs={{8,0},{9,1},{10,2},{11,3},{12,4},{13,5},{14,6},{15,7},{16,8},{17,9... | collective-permute-start | bytes 331784 | tf_op jit(solution)/shard_map/ppermute | solution.py:440
  28.9 0.8 fusion.4
  29.6 3.0 %collective-permute-start.2 = (bf16[32,384]{1,0:T(8,128)(2,1)S(1)}, bf16[32,384]{1,0:T(8,128)(2,1)S(1)}, u32[]{:S(2)}, u32[]{:S(2)}) collective-permute-start(bf16[32,384]{1,0:T(8,128)(2,1)S(1)} %get-tuple-element.61), channel_id=1, source_target_pairs={{9,0},{10,1},{11,2},{12,3},{13,4},{14,5},{15,6},{8,7},{17,8},{18,9... | collective-permute-start | bytes 73736 | tf_op jit(solution)/shard_map/ppermute | solution.py:442
  32.7 0.3 collective-permute-start.1
  32.9 1.2 collective-permute-start.3
  34.1 0.8 fusion.3
  34.9 1.2 collective-permute-start.5
  36.1 2.1 collective-permute-start.4
  38.2 0.6 pad_maximum_fusion.4.edges_ref
  38.8 1.1 collective-permute-done.4
  39.9 0.6 pad_maximum_fusion.5.cot_edges_ref
  40.6 0.6 copy-done.3
  41.2 14.0 %shard_map.198 = (bf16[352,384]{1,0:T(8,128)(2,1)}, bf16[352,384]{1,0:T(8,128)(2,1)}, bf16[3456,128]{1,0:T(8,128)(2,1)}, f32[2,192]{1,0:T(2,128)}, bf16[144,138]{1,0:T(8,128)(2,1)}) custom-call(f32[1]{0:T(128)} %bitcast.flag_ref, bf16[288,384]{1,0:T(8,128)(2,1)} %get-tuple-element.29.grid_ref, bf16[144,384]{1,0:T(8,128)(2,1)} %copy-done.3, ...), custom_call_target="tpu_custom_call" | custom-call | tf_op jit(solution)/shard_map/pallas_call | solution.py:418
  55.3 0.8 fusion
  56.0 0.8 collective-permute-start.11
  56.9 0.5 collective-permute-start.10
  57.3 0.9 slice.89
  58.2 2.2 collective-permute-start.9
  60.5 0.7 convert.13
  61.1 3.6 %collective-permute-done.11 = bf16[32,384]{1,0:T(8,128)(2,1)S(1)} collective-permute-done((bf16[32,384]{1,0:T(8,128)(2,1)S(1)}, bf16[32,384]{1,0:T(8,128)(2,1)S(1)}, u32[]{:S(2)}, u32[]{:S(2)}) %collective-permute-start.11) | collective-permute-done | bytes 24608 | tf_op jit(solution)/shard_map/ppermute | solution.py:442
  64.7 0.6 pad_maximum_fusion.6.edges_ref
  65.4 1.2 collective-permute-done.9.above_ref
  66.6 0.6 copy-done.5
  67.2 10.4 %shard_map.199 = (bf16[288,384]{1,0:T(8,128)(2,1)}, bf16[3456,128]{1,0:T(8,128)(2,1)}, f32[2,192]{1,0:T(2,128)}, bf16[144,138]{1,0:T(8,128)(2,1)}) custom-call(bf16[352,384]{1,0:T(8,128)(2,1)} %get-tuple-element.33.back_ref, bf16[144,384]{1,0:T(8,128)(2,1)} %copy-done.5, bf16[64,384]{1,0:T(8,128)(2,1)} %pad_maximum_fusion.6.edges_ref, ...), custom_call_target="tpu_custom_call" | custom-call | tf_op jit(solution)/shard_map/pallas_call | solution.py:418
  77.6 0.7 convert.12
  78.4 1.3 pad_maximum_fusion
  79.7 33.1 %all_to_all.10 = bf16[128,56,128]{2,1,0:T(8,128)(2,1)S(1)} all-to-all(bf16[128,56,128]{2,1,0:T(8,128)(2,1)S(1)} %bitcast.20), channel_id=1, replica_groups=mesh['lat'=16,'lon'=8] {'lat','lon'}, dimensions={0} | all-to-all | bytes 3670016 | tf_op jit(solution)/shard_map/all_to_all | solution.py:449
  112.8 0.3 reduce_sum.12
  113.2 1.5 broadcast_in_dim.2
  114.7 4.9 %all-to-all-start.1 = ((bf16[128,56,128]{2,1,0:T(8,128)(2,1)}), bf16[128,56,128]{2,1,0:T(8,128)(2,1)S(1)}, u32[]{:S(2)}, u32[]{:S(2)}) async-start(bf16[128,56,128]{2,1,0:T(8,128)(2,1)} %broadcast_in_dim.2), calls=%async_computation.1 | async-start | bytes 3670016 | tf_op jit(solution)/shard_map/all_to_all | solution.py:452
  119.8 1.2 collective-permute-start.7
  121.0 2.1 collective-permute-start.6
  123.3 20.6 %collective-permute-done.7 = bf16[32,384]{1,0:T(8,128)(2,1)S(1)} collective-permute-done((bf16[32,384]{1,0:T(8,128)(2,1)S(1)}, bf16[32,384]{1,0:T(8,128)(2,1)S(1)}, u32[]{:S(2)}, u32[]{:S(2)}) %collective-permute-start.7) | collective-permute-done | bytes 24608 | tf_op jit(solution)/shard_map/ppermute | solution.py:441
  143.9 3.4 %collective-permute-done.6 = bf16[32,384]{1,0:T(8,128)(2,1)S(1)} collective-permute-done((bf16[32,384]{1,0:T(8,128)(2,1)S(1)}, bf16[32,384]{1,0:T(8,128)(2,1)S(1)}, u32[]{:S(2)}, u32[]{:S(2)}) %collective-permute-start.6) | collective-permute-done | bytes 24608 | tf_op jit(solution)/shard_map/ppermute | solution.py:442
  147.6 0.9 pad_maximum_fusion.3
  148.6 0.8 pad_maximum_fusion.2
  149.3 67.9 %all-reduce.3.cloned.1.call-done = bf16[2,1,6,3312]{3,1,2,0:T(2,128)(2,1)} async-done(((bf16[2,1,6,3312]{3,1,2,0:T(2,128)(2,1)}), bf16[2,1,6,3312]{3,1,2,0:T(2,128)(2,1)}) %all-reduce.3.cloned.1.call-update) | async-done | bytes 79504 | tf_op jit(solution)/shard_map/psum | solution.py:513
  217.3 1.7 convert_element_type.37
  219.1 0.2 copy_bitcast_fusion
  219.4 1.0 slice.103
  220.4 0.9 slice.104
  221.3 1.6 slice_bitcast_fusion
  222.9 0.7 reshape.83
  (41 shorter events, 0.9 us)
Async XLA Ops:
  11.6 21.3 %copy-start = (bf16[6,48,384]{2,1,0:T(8,128)(2,1)S(1)}, bf16[6,48,384]{2,1,0:T(8,128)(2,1)}, u32[]{:S(2)}) copy-start(bf16[6,48,384]{2,1,0:T(8,128)(2,1)} %param.15) | copy-start | bytes 663556
  23.0 17.6 %collective-permute-start = (bf16[144,384]{1,0:T(8,128)(2,1)S(1)}, bf16[144,384]{1,0:T(8,128)(2,1)S(1)}, u32[]{:S(2)}, u32[]{:S(2)}) collective-permute-start(bf16[144,384]{1,0:T(8,128)(2,1)S(1)} %slice.75), channel_id=1, source_target_pairs={{8,0},{9,1},{10,2},{11,3},{12,4},{13,5},{14,6},{15,7},{16,8},{17,9... | collective-permute-start | bytes 331784 | tf_op jit(solution)/shard_map/ppermute | solution.py:440
  29.6 6.5 %collective-permute-start.2 = (bf16[32,384]{1,0:T(8,128)(2,1)S(1)}, bf16[32,384]{1,0:T(8,128)(2,1)S(1)}, u32[]{:S(2)}, u32[]{:S(2)}) collective-permute-start(bf16[32,384]{1,0:T(8,128)(2,1)S(1)} %get-tuple-element.61), channel_id=1, source_target_pairs={{9,0},{10,1},{11,2},{12,3},{13,4},{14,5},{15,6},{8,7},{17,8},{18,9... | collective-permute-start | bytes 73736 | tf_op jit(solution)/shard_map/ppermute | solution.py:442
  32.7 5.5 %collective-permute-start.1 = (bf16[32,384]{1,0:T(8,128)(2,1)S(1)}, bf16[32,384]{1,0:T(8,128)(2,1)S(1)}, u32[]{:S(2)}, u32[]{:S(2)}) collective-permute-start(bf16[32,384]{1,0:T(8,128)(2,1)S(1)} %get-tuple-element.60), channel_id=1, source_target_pairs={{1,0},{2,1},{3,2},{4,3},{5,4},{6,5},{7,6},{0,7},{9,8},{10,9},{11,1... | collective-permute-start | bytes 73736 | tf_op jit(solution)/shard_map/ppermute | solution.py:441
  32.9 7.6 %collective-permute-start.3 = (bf16[144,384]{1,0:T(8,128)(2,1)S(1)}, bf16[144,384]{1,0:T(8,128)(2,1)S(1)}, u32[]{:S(2)}, u32[]{:S(2)}) collective-permute-start(bf16[144,384]{1,0:T(8,128)(2,1)S(1)} %bitcast.28), channel_id=1, source_target_pairs={{8,0},{9,1},{10,2},{11,3},{12,4},{13,5},{14,6},{15,7},{16,8},{17,9... | collective-permute-start | bytes 331784 | tf_op jit(solution)/shard_map/ppermute | solution.py:440
  34.9 3.9 %collective-permute-start.5 = (bf16[32,384]{1,0:T(8,128)(2,1)S(1)}, bf16[32,384]{1,0:T(8,128)(2,1)S(1)}, u32[]{:S(2)}, u32[]{:S(2)}) collective-permute-start(bf16[32,384]{1,0:T(8,128)(2,1)S(1)} %get-tuple-element.59), channel_id=1, source_target_pairs={{9,0},{10,1},{11,2},{12,3},{13,4},{14,5},{15,6},{8,7},{17,8},{18,9... | collective-permute-start | bytes 73736 | tf_op jit(solution)/shard_map/ppermute | solution.py:442
  36.1 3.8 %collective-permute-start.4 = (bf16[32,384]{1,0:T(8,128)(2,1)S(1)}, bf16[32,384]{1,0:T(8,128)(2,1)S(1)}, u32[]{:S(2)}, u32[]{:S(2)}) collective-permute-start(bf16[32,384]{1,0:T(8,128)(2,1)S(1)} %get-tuple-element.58), channel_id=1, source_target_pairs={{1,0},{2,1},{3,2},{4,3},{5,4},{6,5},{7,6},{0,7},{9,8},{10,9},{11,1... | collective-permute-start | bytes 73736 | tf_op jit(solution)/shard_map/ppermute | solution.py:441
  40.6 0.6 copy-start.3
  40.6 0.7 copy-start.4
  56.0 8.7 %collective-permute-start.11 = (bf16[32,384]{1,0:T(8,128)(2,1)S(1)}, bf16[32,384]{1,0:T(8,128)(2,1)S(1)}, u32[]{:S(2)}, u32[]{:S(2)}) collective-permute-start(bf16[32,384]{1,0:T(8,128)(2,1)S(1)} %get-tuple-element.53), channel_id=1, source_target_pairs={{127,0},{120,1},{121,2},{122,3},{123,4},{124,5},{125,6},{126,7},{7... | collective-permute-start | bytes 73736 | tf_op jit(solution)/shard_map/ppermute | solution.py:442
  56.9 7.8 %collective-permute-start.10 = (bf16[32,384]{1,0:T(8,128)(2,1)S(1)}, bf16[32,384]{1,0:T(8,128)(2,1)S(1)}, u32[]{:S(2)}, u32[]{:S(2)}) collective-permute-start(bf16[32,384]{1,0:T(8,128)(2,1)S(1)} %get-tuple-element.52), channel_id=1, source_target_pairs={{7,0},{0,1},{1,2},{2,3},{3,4},{4,5},{5,6},{6,7},{15,8},{8,9},{9,10... | collective-permute-start | bytes 73736 | tf_op jit(solution)/shard_map/ppermute | solution.py:441
  58.2 8.3 %collective-permute-start.9 = (bf16[144,384]{1,0:T(8,128)(2,1)S(1)}, bf16[144,384]{1,0:T(8,128)(2,1)S(1)}, u32[]{:S(2)}, u32[]{:S(2)}) collective-permute-start(bf16[144,384]{1,0:T(8,128)(2,1)S(1)} %slice.89), channel_id=1, source_target_pairs={{120,0},{121,1},{122,2},{123,3},{124,4},{125,5},{126,6},{127,7},{0... | collective-permute-start | bytes 331784 | tf_op jit(solution)/shard_map/ppermute | solution.py:440
  66.6 0.6 copy-start.5
  67.2 11.2 %copy-start.1 = (bf16[3456,128]{1,0:T(8,128)(2,1)S(1)}, bf16[3456,128]{1,0:T(8,128)(2,1)}, u32[]{:S(2)}) copy-start(bf16[3456,128]{1,0:T(8,128)(2,1)} %get-tuple-element.45) | copy-start | bytes 2654212
  114.7 5.0 %copy-start.2 = (bf16[352,384]{1,0:T(8,128)(2,1)S(1)}, bf16[352,384]{1,0:T(8,128)(2,1)}, u32[]{:S(2)}) copy-start(bf16[352,384]{1,0:T(8,128)(2,1)} %get-tuple-element.32) | copy-start | bytes 811012
  114.7 8.4 %copy-start.6 = (bf16[144,138]{1,0:T(8,128)(2,1)S(1)}, bf16[144,138]{1,0:T(8,128)(2,1)}, u32[]{:S(2)}) copy-start(bf16[144,138]{1,0:T(8,128)(2,1)} %get-tuple-element.49) | copy-start | bytes 119236
  114.7 32.8 %copy-start.7 = (bf16[144,138]{1,0:T(8,128)(2,1)S(1)}, bf16[144,138]{1,0:T(8,128)(2,1)}, u32[]{:S(2)}) copy-start(bf16[144,138]{1,0:T(8,128)(2,1)} %get-tuple-element.48) | copy-start | bytes 119236
  114.7 104.3 %all-to-all-start.1 = ((bf16[128,56,128]{2,1,0:T(8,128)(2,1)}), bf16[128,56,128]{2,1,0:T(8,128)(2,1)S(1)}, u32[]{:S(2)}, u32[]{:S(2)}) async-start(bf16[128,56,128]{2,1,0:T(8,128)(2,1)} %broadcast_in_dim.2), calls=%async_computation.1 | async-start | bytes 3670016 | tf_op jit(solution)/shard_map/all_to_all | solution.py:452
  119.6 97.7 %all-reduce.3.cloned.1.call-start = ((), (), s32[]{:S(2)}) async-start(), calls=%async_computation.2 | async-start | bytes 319488 | tf_op jit(solution)/shard_map/psum | solution.py:513
  119.7 27.7 %collective-permute-start.8 = (bf16[144,384]{1,0:T(8,128)(2,1)S(1)}, bf16[144,384]{1,0:T(8,128)(2,1)S(1)}, u32[]{:S(2)}, u32[]{:S(2)}) collective-permute-start(bf16[144,384]{1,0:T(8,128)(2,1)S(1)} %get-tuple-element.56), channel_id=1, source_target_pairs={{120,0},{121,1},{122,2},{123,3},{124,4},{125,5},{126,6},{127,7},{0... | collective-permute-start | bytes 331784 | tf_op jit(solution)/shard_map/ppermute | solution.py:440
  119.8 24.1 %collective-permute-start.7 = (bf16[32,384]{1,0:T(8,128)(2,1)S(1)}, bf16[32,384]{1,0:T(8,128)(2,1)S(1)}, u32[]{:S(2)}, u32[]{:S(2)}) collective-permute-start(bf16[32,384]{1,0:T(8,128)(2,1)S(1)} %get-tuple-element.55), channel_id=1, source_target_pairs={{7,0},{0,1},{1,2},{2,3},{3,4},{4,5},{5,6},{6,7},{15,8},{8,9},{9,10... | collective-permute-start | bytes 73736 | tf_op jit(solution)/shard_map/ppermute | solution.py:441
  121.0 26.3 %collective-permute-start.6 = (bf16[32,384]{1,0:T(8,128)(2,1)S(1)}, bf16[32,384]{1,0:T(8,128)(2,1)S(1)}, u32[]{:S(2)}, u32[]{:S(2)}) collective-permute-start(bf16[32,384]{1,0:T(8,128)(2,1)S(1)} %get-tuple-element.54), channel_id=1, source_target_pairs={{127,0},{120,1},{121,2},{122,3},{123,4},{124,5},{125,6},{126,7},{7... | collective-permute-start | bytes 73736 | tf_op jit(solution)/shard_map/ppermute | solution.py:442
Sparse Core Ops, SparseCore 0:
  148.7 68.5 all-reduce.2

commit v2 on v1

--- a/solution.py
+++ b/solution.py
@@ -22,6 +22,8 @@
 GROUP = 12
 SPAN = 23
 WIDE = SPAN * GROUP
+CELL = 6 * SPAN
+TABLE = 24 * CELL
 QLANES = HEADS * WIN_TOK
 STRIP = 32
 SOURCE = 288 + 2 * STRIP
@@ -30,6 +32,10 @@
 LOG2E = math.log2(math.e)
 SCALE = 1.0 / math.sqrt(HEAD_DIM)
 WBLOCK = 18 * DIM
+CHUNK = 448
+HALF = 8 * CHUNK
+TCHUNK = 64
+TROWS = 208
 
 F32 = jnp.float32
 BF16 = jnp.bfloat16
@@ -77,12 +83,12 @@
 
 
 def table_rows():
-    picked = np.zeros((2, HEADS * 16, HEADS * 24), np.float32)
+    picked = np.zeros((2, HEADS * 16, 24 * 8), np.float32)
     for h in range(HEADS):
         for lq in range(2):
             for lp in range(2):
                 for rq in range(6):
-                    picked[lp, h * 16 + lq * 6 + rq, ((h * 2 + lq) * 2 + lp) * 6 + rq] = 1
+                    picked[lp, h * 16 + lq * 6 + rq, (lq * 12 + lp * 6 + rq) * 8 + h] = 1
     return picked
 
 
@@ -165,7 +171,8 @@
 
 
 def expand_table(table_ref, trows_ref, tcols_ref, bias_ref):
-    table = table_ref[...] * LOG2E
+    table = jnp.concatenate([table_ref[...] * LOG2E, jnp.zeros((2, TABLE), F32)], axis=0)
+    table = jnp.concatenate([table[:, k * CELL : (k + 1) * CELL] for k in range(24)], axis=0)
     high = table.astype(BF16)
     low = (table - high.astype(F32)).astype(BF16)
     wide = jnp.zeros((HEADS * 16, WIDE), F32)
@@ -203,11 +210,13 @@
             total = piece if total is None else total + piece
         parts.append(jnp.concatenate([total, jnp.zeros((16 - GROUP, WIDE), F32)], axis=0))
     wide = jnp.concatenate(parts, axis=0).astype(BF16)
-    result = jnp.zeros((HEADS * 24, 6 * SPAN), F32)
+    result = jnp.zeros((24 * 8, CELL), F32)
     for lp in range(2):
         narrow = nt(wide, tcols_ref[lp]).astype(BF16)
         result += tn(trows_ref[lp], narrow)
-    return result
+    cells = [result[k * 8 : (k + 1) * 8] for k in range(24)] + [jnp.zeros((8, 26 * 128 - TABLE), F32)]
+    flat = jnp.concatenate(cells, axis=1)
+    return jnp.concatenate([flat[:, j * 128 : (j + 1) * 128] for j in range(26)], axis=0).astype(BF16)
 
 
 def attention(q_ref, k_ref, v_ref, bias_ref, probs_ref, ctx_ref, masks):
@@ -280,12 +289,11 @@
 
 
 def first_forward(
-    x_ref, cot_ref, gains_ref, qkv_ref, out_ref, up_ref, down_ref, table_ref, trows_ref, tcols_ref, pick_ref, strips_ref,
-    xw_ref, q_ref, k_ref, v_ref, probs_ref, ctx_ref, hidden_ref, expanded_ref, slope_ref, grid_ref, edges_ref, cot_edges_ref,
+    x_ref, gains_ref, qkv_ref, out_ref, up_ref, down_ref, table_ref, trows_ref, tcols_ref, pick_ref, strips_ref,
+    xw_ref, q_ref, k_ref, v_ref, probs_ref, ctx_ref, hidden_ref, expanded_ref, slope_ref, top_ref, bottom_ref, side_ref, corner_ref,
     bias_ref,
 ):
     masks = head_rows()
-    cot_edges_ref[...] = nn(strips_ref[...], cot_ref[...]).astype(BF16)
     x = gather_tokens(pick_ref[...], x_ref[...])
     xw_ref[...] = x.astype(BF16)
     hat, _ = normalize(x)
@@ -306,38 +314,53 @@
         expanded = (pre * below).astype(BF16)
         expanded_ref[:, cols] = expanded
         slope_ref[:, cols] = (below + pre * density).astype(BF16)
-        total = total + nn(expanded, down_ref[cols, :])
+        total = total + nt(expanded, down_ref[:, cols])
     grid = scatter_tokens(pick_ref[...], total.astype(BF16)).astype(BF16)
-    grid_ref[...] = grid
-    edges_ref[...] = nn(strips_ref[...], grid).astype(BF16)
+    top_ref[...] = grid[:144]
+    bottom_ref[...] = grid[144:]
+    edges = nn(strips_ref[...], grid).astype(BF16)
+    side_ref[...] = edges[:STRIP]
+    corner_ref[...] = edges[STRIP:]
+
+
+def fill_source(source_ref, own, above_ref, side_ref, corner_ref):
+    source_ref[0:144, :] = own
+    source_ref[144:288, :] = above_ref[...]
+    source_ref[288:SOURCE, :] = jnp.zeros((2 * STRIP, 2 * DIM), BF16)
+    source_ref[288 : 288 + side_ref.shape[0], :] = side_ref[...]
+    source_ref[288 + STRIP : 288 + STRIP + corner_ref.shape[0], :] = corner_ref[...]
+
+
+def put_source(own_ref, row_ref, side_ref, corner_ref, value):
+    own_ref[...] = value[0:144]
+    row_ref[...] = value[144:288]
+    side_ref[...] = value[288 : 288 + STRIP]
+    corner_ref[...] = value[288 + STRIP :]
 
 
 def second_both(
-    flag_ref, grid_ref, above_ref, edges_ref, cot_ref, cot_above_ref, cot_edges_ref,
+    own_ref, above_ref, side_ref, corner_ref, cot_ref, cot_above_ref, cot_side_ref, cot_corner_ref,
     gains_ref, qkv_ref, out_ref, up_ref, down_ref, table_ref, trows_ref, tcols_ref, pick_ref,
-    y_ref, back_ref, wbuf_ref, gain_grad_ref, table_grad_ref,
+    y_own_ref, y_row_ref, y_side_ref, y_corner_ref, back_own_ref, back_row_ref, back_side_ref, back_corner_ref,
+    wbuf_ref, gain_grad_ref, table_grad_ref,
     source_ref, x_ref, q_ref, k_ref, v_ref, probs_ref, ctx_ref, bias_ref, gctx_ref, dq_ref, dk_ref, dv_ref, gpre_ref, expanded_ref,
 ):
     masks = head_rows()
 
-    def assemble(grid, above, edges):
-        source_ref[0:144, :] = grid[144:288, :]
-        source_ref[144:288, :] = above[...]
-        source_ref[288:SOURCE, :] = edges[...]
-        return gather_tokens(pick_ref[...], source_ref[...])
-
-    x_ref[...] = assemble(grid_ref, above_ref, edges_ref)
+    fill_source(source_ref, own_ref[...], above_ref, side_ref, corner_ref)
+    x_ref[...] = gather_tokens(pick_ref[...], source_ref[...])
     hat, _ = normalize(x_ref[...])
     normed = (hat * gains_ref[0:1, :]).astype(BF16)
     project(normed, qkv_ref, q_ref, k_ref, v_ref)
     expand_table(table_ref, trows_ref, tcols_ref, bias_ref)
-    add_mask(bias_ref, flag_ref[0])
+    add_mask(bias_ref, (lax.axis_index("lat") == lax.axis_size("lat") - 1).astype(F32))
     attention(q_ref, k_ref, v_ref, bias_ref, probs_ref, ctx_ref, masks)
     branch = nn(ctx_ref[...], out_ref[...]).astype(BF16)
     hidden = x_ref[...] + branch.astype(F32)
     hat_mlp, inv_mlp = normalize(hidden)
     normed_mlp = (hat_mlp * gains_ref[1:2, :]).astype(BF16)
-    g32 = assemble(cot_ref, cot_above_ref, cot_edges_ref)
+    fill_source(source_ref, cot_ref[144:288, :], cot_above_ref, cot_side_ref, cot_corner_ref)
+    g32 = gather_tokens(pick_ref[...], source_ref[...])
     g = g32.astype(BF16)
     total = hidden
     gnormed = jnp.zeros((TOKENS, DIM), F32)
@@ -347,12 +370,13 @@
         below, density = gelu_parts(pre)
         expanded = (pre * below).astype(BF16)
         expanded_ref[:, cols] = expanded
-        total = total + nn(expanded, down_ref[cols, :])
-        gact = nt(g, down_ref[cols, :]).astype(BF16).astype(F32)
+        total = total + nt(expanded, down_ref[:, cols])
+        gact = nn(g, down_ref[:, cols]).astype(BF16).astype(F32)
         gpre = ((below + pre * density) * gact).astype(BF16)
         gpre_ref[:, cols] = gpre
         gnormed = gnormed + nt(gpre, up_ref[:, cols])
-    y_ref[...] = scatter_tokens(pick_ref[...], total.astype(BF16)).astype(BF16)
+    y = scatter_tokens(pick_ref[...], total.astype(BF16)).astype(BF16)
+    put_source(y_own_ref, y_row_ref, y_side_ref, y_corner_ref, y)
     gnormed = gnormed.astype(BF16).astype(F32)
     gain_grad_ref[1:2, :] = jnp.sum(gnormed * hat_mlp, axis=0, keepdims=True)
     ghid = g32 + norm_backward(gnormed, gains_ref[1:2, :], hat_mlp, inv_mlp)
@@ -361,23 +385,25 @@
         q_ref, k_ref, v_ref, probs_ref, ctx_ref, gctx_ref, dq_ref, dk_ref, dv_ref, bias_ref, masks,
     )
     gain_grad_ref[0:1, :] = gain_grad
-    back_ref[...] = scatter_tokens(pick_ref[...], gblock.astype(BF16)).astype(BF16)
+    back = scatter_tokens(pick_ref[...], gblock.astype(BF16)).astype(BF16)
+    put_source(back_own_ref, back_row_ref, back_side_ref, back_corner_ref, back)
     weight_grads(
         wbuf_ref, normed, dq_ref[...], dk_ref[...], dv_ref[...], ctx_ref[...], gbranch, normed_mlp, gpre_ref, expanded_ref, g
     )
-    table_grad_ref[...] = collapse_table(bias_ref, trows_ref, tcols_ref).astype(BF16)
+    table_grad_ref[...] = collapse_table(bias_ref, trows_ref, tcols_ref)
 
 
 def first_backward(
-    back_ref, above_ref, edges_ref, xw_ref, q_ref, k_ref, v_ref, probs_ref, ctx_ref, hidden_ref, expanded_ref, slope_ref,
+    back_ref, above_ref, side_ref, corner_ref, xw_ref, q_ref, k_ref, v_ref, probs_ref, ctx_ref, hidden_ref, expanded_ref, slope_ref,
     gains_ref, qkv_ref, out_ref, up_ref, down_ref, trows_ref, tcols_ref, pick_ref, returned_ref,
-    gin_ref, wbuf_ref, gain_grad_ref, table_grad_ref,
-    source_ref, gctx_ref, dq_ref, dk_ref, dv_ref, gpre_ref, grad_ref,
+    last_wbuf_ref, last_gain_ref, last_table_ref,
+    gin_ref, mine_ref, theirs_ref, tables_ref,
+    source_ref, gctx_ref, dq_ref, dk_ref, dv_ref, gpre_ref, grad_ref, wbuf_ref, gain_grad_ref, sems,
 ):
     masks = head_rows()
-    source_ref[0:144, :] = back_ref[0:144, :]
-    source_ref[144:288, :] = above_ref[...]
-    source_ref[288:SOURCE, :] = edges_ref[...]
+    fetch = pltpu.make_async_copy(last_wbuf_ref, wbuf_ref.at[pl.ds(WBLOCK, WBLOCK), :], sems.at[0])
+    fetch.start()
+    fill_source(source_ref, back_ref[...], above_ref, side_ref, corner_ref)
     g32 = gather_tokens(returned_ref[...], source_ref[...])
     g = g32.astype(BF16)
     hat_mlp, inv_mlp = normalize(hidden_ref[...])
@@ -385,7 +411,7 @@
     gnormed = jnp.zeros((TOKENS, DIM), F32)
     for j in range(3):
         cols = slice(j * 256, (j + 1) * 256)
-        gact = nt(g, down_ref[cols, :]).astype(BF16).astype(F32)
+        gact = nn(g, down_ref[:, cols]).astype(BF16).astype(F32)
         gpre = (slope_ref[:, cols].astype(F32) * gact).astype(BF16)
         gpre_ref[:, cols] = gpre
         gnormed = gnormed + nt(gpre, up_ref[:, cols])
@@ -401,7 +427,94 @@
     weight_grads(
         wbuf_ref, normed, dq_ref[...], dk_ref[...], dv_ref[...], ctx_ref[...], gbranch, normed_mlp, gpre_ref, expanded_ref, g
     )
-    table_grad_ref[...] = collapse_table(grad_ref, trows_ref, tcols_ref).astype(BF16)
+    tables_ref[0:TROWS, :] = collapse_table(grad_ref, trows_ref, tcols_ref)
+    tables_ref[TROWS : 2 * TROWS, :] = last_table_ref[...]
+    tables_ref[2 * TROWS :, :] = jnp.zeros((8 * TCHUNK - 2 * TROWS, 128), BF16)
+    gains = jnp.concatenate([ref[i : i + 1, :] for ref in (gain_grad_ref, last_gain_ref) for i in range(2)], axis=1)
+    wbuf_ref[2 * WBLOCK :, :] = jnp.zeros((2 * HALF - 2 * WBLOCK, 128), BF16)
+    for j in range(6):
+        tile = jnp.concatenate([gains[:, j * 128 : (j + 1) * 128], jnp.zeros((15, 128), F32)], axis=0)
+        wbuf_ref[2 * WBLOCK + j * 16 : 2 * WBLOCK + (j + 1) * 16, :] = tile.astype(BF16)
+    fetch.wait()
+    core = lax.rem(lax.axis_index("lat"), 2)
+    keep = pltpu.make_async_copy(wbuf_ref.at[pl.ds(core * HALF, HALF), :], mine_ref, sems.at[1])
+    send = pltpu.make_async_copy(wbuf_ref.at[pl.ds((1 - core) * HALF, HALF), :], theirs_ref, sems.at[2])
+    send.start()
+    keep.start()
+    send.wait()
+    keep.wait()
+
+
+def pack_core(mine_ref, other_ref, tables_ref, packed_ref):
+    for j in range(8):
+        rows = slice(j * CHUNK, (j + 1) * CHUNK)
+        total = mine_ref[rows, :].astype(F32) + other_ref[rows, :].astype(F32)
+        packed_ref[j, 0:CHUNK, :] = total.astype(BF16)
+        packed_ref[j, CHUNK:, :] = tables_ref[j * TCHUNK : (j + 1) * TCHUNK, :]
+
+
+def sum_eight(ref, rows):
+    total = ref[0, rows, :].astype(F32)
+    for j in range(1, 8):
+        total += ref[j, rows, :].astype(F32)
+    return total.astype(BF16)
+
+
+def sum_lon(parts_ref, spread_ref, table_ref):
+    total = sum_eight(parts_ref, slice(0, CHUNK))
+    for j in range(8):
+        spread_ref[j] = total
+    table_ref[...] = sum_eight(parts_ref, slice(CHUNK, CHUNK + TCHUNK))
+
+
+def sum_lat(parts_ref, table_ref, spread_ref):
+    total = sum_eight(parts_ref, slice(0, CHUNK))
+    for j in range(8):
+        spread_ref[j, 0:CHUNK, :] = total
+        spread_ref[j, CHUNK:, :] = table_ref[...]
+
+
+def unpack(mine_ref, other_ref, qkv_ref, out_ref, up_ref, down_ref, gains_ref, table_ref):
+    core = lax.rem(lax.axis_index("lat"), 2)
+
+    def load(start, count):
+        pieces = []
+        while count:
+            half, place = divmod(start, HALF)
+            j, place = divmod(place, CHUNK)
+            size = min(count, CHUNK - place)
+            here = mine_ref[j, place : place + size, :].astype(F32)
+            there = other_ref[j, place : place + size, :].astype(F32)
+            pieces.append(jnp.where(core == half, here, there))
+            start, count = start + size, count - size
+        return pieces[0] if len(pieces) == 1 else jnp.concatenate(pieces, axis=0)
+
+    for b in range(2):
+        for j in range(18):
+            tile = load(b * WBLOCK + j * DIM, DIM)
+            if j < 6:
+                up_ref[b, :, j * 128 : (j + 1) * 128] = tile
+            elif j < 12:
+                down_ref[b, :, (j - 6) * 128 : (j - 5) * 128] = tile
+            elif j < 16:
+                qkv_ref[b, :, (j - 12) * 128 : (j - 11) * 128] = tile
+            elif j == 16:
+                qkv_ref[b, :, 512:576] = tile[:, :64]
+                out_ref[b, :, 0:64] = tile[:, 64:]
+            else:
+                out_ref[b, :, 64:192] = tile
+        for j in range(26):
+            k, place = divmod(b * TROWS + j * 8, TCHUNK)
+            base = CHUNK + place // 16 * 16
+            pair = mine_ref[k, base : base + 16, :].astype(F32)
+            piece = pair[place % 16 : place % 16 + HEADS]
+            width = min(128, TABLE - j * 128)
+            table_ref[b, 0, :, j * 128 : j * 128 + width] = piece[:, :width]
+    gains = jnp.concatenate([load(2 * WBLOCK + j * 16, 16)[0:1] for j in range(6)], axis=1)
+    for b in range(2):
+        for i in range(2):
+            k = b * 2 + i
+            gains_ref[b, i : i + 1, :] = gains[:, k * DIM : (k + 1) * DIM]
 
 
 def whole(array):
@@ -413,20 +526,26 @@
     return pl.BlockSpec((None,) + rest, lambda i: (index,) + (0,) * len(rest))
 
 
-def call(kernel, operands, specs, outs, scratch):
+def in_place():
+    return pl.BlockSpec(memory_space=pl.ANY)
+
+
+def call(kernel, operands, specs, outs, scratch=(), flops=0, out_specs=None):
     shapes = [jax.ShapeDtypeStruct(shape, dtype) for shape, dtype in outs]
+    moved = sum(a.size * a.dtype.itemsize for a in (*operands, *shapes))
     return pl.pallas_call(
         kernel,
         grid=(1,),
         out_shape=shapes,
         in_specs=specs,
-        out_specs=[whole(s) for s in shapes],
-        scratch_shapes=[pltpu.VMEM(shape, dtype) for shape, dtype in scratch],
+        out_specs=out_specs or [whole(s) for s in shapes],
+        scratch_shapes=list(scratch),
+        cost_estimate=pl.CostEstimate(flops=flops, bytes_accessed=moved, transcendentals=0),
         compiler_params=pltpu.CompilerParams(vmem_limit_bytes=56 * 1024 * 1024),
     )(*operands)
 
 
-def neighbour(axes, sizes, steps):
+def neighbour(sizes, steps):
     pairs = []
     for a in range(sizes[0]):
         for b in range(sizes[1]):
@@ -435,82 +554,97 @@
     return pairs
 
 
-def exchange(rows, edges, sizes, step):
+def exchange(rows, side, corner, sizes, step):
     both = ("lat", "lon")
-    above = lax.ppermute(rows, both, neighbour(both, sizes, (step, 0)))
-    side = lax.ppermute(edges[:STRIP], both, neighbour(both, sizes, (0, step)))
-    corner = lax.ppermute(edges[STRIP:], both, neighbour(both, sizes, (step, step)))
-    return above, jnp.concatenate([side, corner], axis=0)
-
-
-def total_sum(wbuf_first, wbuf_last, gains_first, gains_last):
-    gains = jnp.concatenate([gains_first, gains_last]).reshape(-1).astype(BF16)
-    flat = jnp.concatenate([wbuf_first, wbuf_last, jnp.pad(gains, (0, 256 * 128 - 768)).reshape(256, 128)])
-    parts = lax.all_to_all(flat.reshape(128, 56, 128), ("lat", "lon"), 0, 0, tiled=False)
-    mine = jnp.sum(parts.astype(F32), axis=0).astype(BF16)
-    spread = jnp.broadcast_to(mine[None], (128, 56, 128))
-    full = lax.all_to_all(spread, ("lat", "lon"), 0, 0, tiled=False)
-    return full.reshape(128 * 56, 128)
+    rows = lax.ppermute(rows, both, neighbour(sizes, (step, 0)))
+    side = lax.ppermute(side, both, neighbour(sizes, (0, step)))
+    corner = lax.ppermute(corner, both, neighbour(sizes, (step, step)))
+    return rows, side, corner
+
+
+def vmem(shape, dtype):
+    return pltpu.VMEM(shape, dtype)
+
+
+def sum_over_devices(mine, theirs, tables, sizes):
+    pairs = [(i ^ 1, i) for i in range(sizes[0])]
+    groups = [[core + 2 * k for k in range(sizes[0] // 2)] for core in range(2)]
+    other = lax.ppermute(theirs, "lat", pairs)
+    packed = (8, CHUNK + TCHUNK, 128)
+    [sent] = call(pack_core, [mine, other, tables], [whole(a) for a in (mine, other, tables)], [(packed, BF16)])
+    parts = lax.all_to_all(sent, "lon", 0, 0)
+    spread, table = call(sum_lon, [parts], [whole(parts)], [((8, CHUNK, 128), BF16), ((TCHUNK, 128), BF16)])
+    parts = lax.all_to_all(spread, "lat", 0, 0, axis_index_groups=groups)
+    [spread] = call(sum_lat, [parts, table], [whole(parts), whole(table)], [(packed, BF16)])
+    half = lax.all_to_all(spread, "lon", 0, 0)
+    other = lax.ppermute(half, "lat", pairs)
+    outs = [((2, DIM, 3 * DIM), F32), ((2, DIM, DIM), F32), ((2, DIM, UNITS), F32), ((2, DIM, UNITS), F32)]
+    outs += [((2, 2, DIM), F32), ((2, 1, HEADS, TABLE), F32)]
+    return call(unpack, [half, other], [whole(half), whole(other)], outs)
 
 
 def on_device(sizes, inputs, cotangent, norm_gains, qkv_weight, out_weight, up_weight, down_weight, bias_table):
     x = inputs.reshape(GRID, 2 * DIM)
     cot = cotangent.reshape(GRID, 2 * DIM)
-    tables = bias_table.reshape(2, HEADS * 24, 6 * SPAN)
     trows, tcols = jnp.asarray(table_rows(), BF16), jnp.asarray(table_cols(), BF16)
     pick_grid, pick_shift, pick_back = (
         jnp.asarray(m, BF16) for m in (grid_picker(), shifted_picker(), returned_picker())
     )
     strips = jnp.asarray(strip_picker(), BF16)
-    last = (lax.axis_index("lat") == sizes[0] - 1).astype(F32).reshape(1)
-    weights = (norm_gains, qkv_weight, out_weight, up_weight, down_weight)
-    tok = (TOKENS, DIM)
-
-    operands = [x, cot, *weights, tables, trows, tcols, pick_grid, strips]
-    specs = [whole(x), whole(cot)] + [picked(a, 0) for a in (*weights, tables)]
-    specs += [whole(a) for a in (trows, tcols, pick_grid, strips)]
-    outs = [(tok, BF16), (tok, BF16), (tok, BF16), (tok, BF16), ((WINDOWS, WIN_TOK, QLANES), BF16), (tok, BF16), (tok, F32)]
-    outs += [((TOKENS, UNITS), BF16), ((TOKENS, UNITS), BF16), ((GRID, 2 * DIM), BF16), ((2 * STRIP, 2 * DIM), BF16)]
-    outs += [((2 * STRIP, 2 * DIM), BF16)]
-    results = call(first_forward, operands, specs, outs, [((WIN_TOK, QLANES), F32)])
-    saved, grid, edges, cot_edges = results[:9], results[9], results[10], results[11]
-
-    above, edges = exchange(grid[:144], edges, sizes, 1)
-    cot_above, cot_edges = exchange(cot[:144], cot_edges, sizes, 1)
-
-    operands = [last, grid, above, edges, cot, cot_above, cot_edges, *weights, tables, trows, tcols, pick_shift]
-    specs = [pl.BlockSpec(memory_space=pltpu.SMEM)]
-    specs += [whole(a) for a in (grid, above, edges, cot, cot_above, cot_edges)]
-    specs += [picked(a, 1) for a in (*weights, tables)] + [whole(a) for a in (trows, tcols, pick_shift)]
-    src = (SOURCE, 2 * DIM)
-    outs = [(src, BF16), (src, BF16), ((WBLOCK, 128), BF16), ((2, DIM), F32), ((HEADS * 24, 6 * SPAN), BF16)]
-    scratch = [(src, BF16), (tok, F32), (tok, BF16), (tok, BF16), (tok, BF16), ((WINDOWS, WIN_TOK, QLANES), BF16), (tok, BF16)]
-    scratch += [((WIN_TOK, QLANES), F32)] + [(tok, BF16)] * 4 + [((TOKENS, UNITS), BF16)] * 2
-    y_src, back, wbuf_last, gains_last, table_last = call(second_both, operands, specs, outs, scratch)
-
-    back_above, back_edges = exchange(back[144:288], back[288:], sizes, -1)
-    operands = [back, back_above, back_edges, *saved, *weights, trows, tcols, pick_grid, pick_back]
-    specs = [whole(a) for a in (back, back_above, back_edges, *saved)] + [picked(a, 0) for a in weights]
-    specs += [whole(a) for a in (trows, tcols, pick_grid, pick_back)]
-    outs = [((GRID, 2 * DIM), BF16), ((WBLOCK, 128), BF16), ((2, DIM), F32), ((HEADS * 24, 6 * SPAN), BF16)]
-    scratch = [(src, BF16)] + [(tok, BF16)] * 4 + [((TOKENS, UNITS), BF16), ((WIN_TOK, QLANES), F32)]
-    grad_inputs, wbuf_first, gains_first, table_first = call(first_backward, operands, specs, outs, scratch)
-
-    y_above, y_edges = exchange(y_src[144:288], y_src[288:], sizes, -1)
-    rows = jnp.concatenate([y_above, y_src[:144]]).reshape(ROWS, COLS, 2 * DIM)
-    corner = y_edges[STRIP : STRIP + 18].reshape(3, 6, 2 * DIM)
-    side = y_edges[:18].reshape(3, 6, 2 * DIM)
-    output = jnp.concatenate([jnp.concatenate([corner, side]), rows[:, 6:]], axis=1)
-
-    full = total_sum(wbuf_first, wbuf_last, gains_first, gains_last)
-    weight_part = full[: 2 * WBLOCK].reshape(2, 18, DIM, 128).transpose(0, 2, 1, 3).reshape(2, DIM, 18 * 128).astype(F32)
-    grad_up = weight_part[:, :, :UNITS]
-    grad_down = weight_part[:, :, UNITS : 2 * UNITS].transpose(0, 2, 1)
-    grad_qkv = weight_part[:, :, 2 * UNITS : 2 * UNITS + 3 * DIM]
-    grad_out = weight_part[:, :, 2 * UNITS + 3 * DIM :]
-    grad_gains = full[2 * WBLOCK : 2 * WBLOCK + 6].reshape(2, 2, DIM).astype(F32)
-    table_terms = jnp.stack([table_first, table_last]).reshape(2, 1, HEADS, 24 * 6 * SPAN)
-    grad_table = lax.psum(table_terms, "lon").astype(F32)
+    weights = (norm_gains, qkv_weight, out_weight, up_weight, jnp.swapaxes(down_weight, 1, 2))
+    tok, src, hid = (TOKENS, DIM), (SOURCE, 2 * DIM), (TOKENS, UNITS)
+    strip_shapes = [(144, 2 * DIM), (144, 2 * DIM), (STRIP, 2 * DIM), (STRIP, 2 * DIM)]
+    probs = (WINDOWS, WIN_TOK, QLANES)
+
+    def table_spec(index):
+        return pl.BlockSpec((None, None, HEADS, TABLE), lambda i: (index, 0, 0, 0))
+
+    cot_side = cotangent[3:, :6].reshape(18, 2 * DIM)
+    cot_corner = cotangent[:3, :6].reshape(18, 2 * DIM)
+    cot_strips = exchange(cot[:144], cot_side, cot_corner, sizes, 1)
+
+    fixed = (trows, tcols, pick_grid, strips)
+    operands = [x, *weights, bias_table, *fixed]
+    specs = [whole(x)] + [picked(a, 0) for a in weights] + [table_spec(0)] + [whole(a) for a in fixed]
+    outs = [(tok, BF16)] * 4 + [(probs, BF16), (tok, BF16), (tok, F32), (hid, BF16), (hid, BF16)]
+    outs += [(shape, BF16) for shape in strip_shapes]
+    results = call(first_forward, operands, specs, outs, [vmem((WIN_TOK, QLANES), F32)], 650_000_000)
+    saved, (top, bottom, side, corner) = results[:9], results[9:]
+
+    own_strips = exchange(top, side, corner, sizes, 1)
+    fixed = (trows, tcols, pick_shift)
+    fields = (bottom, *own_strips, cot, *cot_strips)
+    operands = [*fields, *weights, bias_table, *fixed]
+    specs = [whole(a) for a in fields] + [picked(a, 1) for a in weights] + [table_spec(1)] + [whole(a) for a in fixed]
+    outs = [(shape, BF16) for shape in strip_shapes] * 2
+    outs += [((WBLOCK, 128), BF16), ((2, DIM), F32), ((TROWS, 128), BF16)]
+    scratch = [vmem(src, BF16), vmem(tok, F32)] + [vmem(tok, BF16)] * 3 + [vmem(probs, BF16), vmem(tok, BF16)]
+    scratch += [vmem((WIN_TOK, QLANES), F32)] + [vmem(tok, BF16)] * 4 + [vmem(hid, BF16)] * 2
+    results = call(second_both, operands, specs, outs, scratch, 2_000_000_000)
+    y_strips, back_strips, last_grads = results[:4], results[4:8], results[8:]
+
+    back = exchange(*back_strips[1:], sizes, -1)
+    y_strips, back = lax.optimization_barrier((y_strips, back))
+    fixed = (trows, tcols, pick_grid, pick_back)
+    operands = [back_strips[0], *back, *saved, *weights, *fixed, *last_grads]
+    specs = [whole(a) for a in (back_strips[0], *back, *saved)] + [picked(a, 0) for a in weights]
+    specs += [whole(a) for a in fixed] + [in_place(), whole(last_grads[1]), whole(last_grads[2])]
+    outs = [((GRID, 2 * DIM), BF16), ((HALF, 128), BF16), ((HALF, 128), BF16), ((8 * TCHUNK, 128), BF16)]
+    out_specs = [pl.BlockSpec((GRID, 2 * DIM), lambda i: (0, 0)), in_place(), in_place()]
+    out_specs += [pl.BlockSpec((8 * TCHUNK, 128), lambda i: (0, 0))]
+    scratch = [vmem(src, BF16)] + [vmem(tok, BF16)] * 4 + [vmem(hid, BF16), vmem((WIN_TOK, QLANES), F32)]
+    scratch += [vmem((2 * HALF, 128), BF16), vmem((2, DIM), F32), pltpu.SemaphoreType.DMA((3,))]
+    grad_inputs, mine, theirs, tables = call(
+        first_backward, operands, specs, outs, scratch, 1_300_000_000, out_specs
+    )
+
+    y_rows, y_side, y_corner = exchange(*y_strips[1:], sizes, -1)
+    rows = jnp.concatenate([y_rows, y_strips[0]]).reshape(ROWS, COLS, 2 * DIM)
+    edge = jnp.concatenate([y_corner[:18].reshape(3, 6, 2 * DIM), y_side[:18].reshape(3, 6, 2 * DIM)])
+    output = jnp.concatenate([edge, rows[:, 6:]], axis=1)
+
+    grad_qkv, grad_out, grad_up, grad_down, grad_gains, grad_table = sum_over_devices(mine, theirs, tables, sizes)
+    grad_down = jnp.swapaxes(grad_down, 1, 2)
     return (output, grad_inputs.reshape(ROWS, COLS, 2 * DIM), grad_gains, grad_qkv, grad_out, grad_up, grad_down, grad_table)
 
 

time: 231 us -> 155 us (0.67)
  waiting for transfers between devices: 97.9 us -> 22.1 us
  blocking collectives: 33.1 us -> 57.9 us
  between operations: 14.2 us -> 0.79 us
  Pallas kernels: 34.9 us -> 47 us
  other arithmetic: 9.81 us -> 0.78 us
  local copies, waits for them, and re-layouts: 15 us -> 6.72 us
  starting transfers between devices: 25.6 us -> 18.8 us
    psum x1 -> x0, waiting for transfers between devices: 67.9 us -> none  [on_device(): grad_table = lax.psum(table_terms, 'lon').astype(F32)]
    all_to_all x1 -> x3, blocking collectives: 33.1 us -> 57.9 us  [the longest x1 20.2 us: sum_over_devices(): parts = lax.all_to_all(sent, 'lon', 0, 0)]
    pallas_call x3 -> x7, Pallas kernels: 34.9 us -> 47 us  [call(): pl.pallas_call(kernel, grid=(1,), out_shape=shapes, in_specs=specs, out_s...]
    ppermute x12 -> x14, waiting for transfers between devices: 29.9 us -> 22.1 us  [the longest x4 9.77 us: exchange(): side = lax.ppermute(side, both, neighbour(sizes, (0, step)))]
    slice x14 -> x5, local copies, waits for them, and re-layouts: 6.24 us -> 0.08 us  [the longest x1 0.06 us: on_device(): output = jnp.concatenate([edge, rows[:, 6:]], axis=1)]
    all_to_all x1 -> x0, starting transfers between devices: 4.93 us -> none  [total_sum(): full = lax.all_to_all(spread, ('lat', 'lon'), 0, 0, tiled=False)]
    concatenate x7 -> x2, other arithmetic: 3.94 us -> 0.78 us  [the longest x1 0.75 us: on_device(): output = jnp.concatenate([edge, rows[:, 6:]], axis=1)]
    unnamed x17 -> x36, local copies, waits for them, and re-layouts: 3.56 us -> 6.59 us
  transfers between devices with their start and end apart: 14 -> 14, of which waited for: 6 -> 7; matrix products, arithmetic and copies ran while one was open for 4% -> 1% of each run, Pallas kernels for 0% -> 0%
where the time goes in v2:
time: 155 us; the launch traced here: 154 us
  blocking collectives  57.9 us (37%)
  Pallas kernels  47 us (30%)
  waiting for transfers between devices  22.1 us (14%)
  starting transfers between devices  18.8 us (12%)
  local copies, waits for them, and re-layouts  6.72 us (4%)
    pallas_call x7, Pallas kernels, call(): pl.pallas_call(kernel, grid=(1,), out_shape=shapes, in_specs=specs, out_s...  47 us
    all_to_all x1, blocking collectives, sum_over_devices(): parts = lax.all_to_all(sent, 'lon', 0, 0)  20.2 us
    all_to_all x1, blocking collectives, sum_over_devices(): parts = lax.all_to_all(spread, 'lat', 0, 0, axis_index_groups=groups)  19.6 us
    all_to_all x1, blocking collectives, sum_over_devices(): half = lax.all_to_all(spread, 'lon', 0, 0)  18.1 us
    ppermute x4, waiting for transfers between devices, exchange(): side = lax.ppermute(side, both, neighbour(sizes, (0, step)))  9.77 us
    ppermute x4, waiting for transfers between devices, exchange(): corner = lax.ppermute(corner, both, neighbour(sizes, (step, step)))  9.63 us
    ppermute x4, starting transfers between devices, exchange(): rows = lax.ppermute(rows, both, neighbour(sizes, (step, 0)))  8.5 us
    ppermute x4, starting transfers between devices, exchange(): side = lax.ppermute(side, both, neighbour(sizes, (0, step)))  6.97 us
  transfers between devices with their start and end apart: 14, of which 7 were waited for; matrix products, arithmetic and copies ran while one was open for 1% of the time, Pallas kernels for 0%

profile of v2, /device:TPU:0, one launch (start us, length us, event | category | flops | bytes accessed | tf_op | source)
XLA Modules:
  0.0 154.1 jit_solution(11837205651702650325)
XLA Ops:
  0.6 1.6 %copy.22.table_ref = f32[2,1,6,3312]{3,2,1,0:T(8,128)} copy(f32[2,1,6,3312]{3,1,2,0:T(1,128)} %param.21) | data formatting | bytes 317952 | tf_op args[7]
  2.3 10.2 %shard_map.197 = (bf16[576,192]{1,0:T(8,128)(2,1)}, bf16[576,192]{1,0:T(8,128)(2,1)}, bf16[576,192]{1,0:T(8,128)(2,1)}, bf16[576,192]{1,0:T(8,128)(2,1)}, bf16[4...) custom-call(bf16[288,384]{1,0:T(8,128)(2,1)} %bitcast.11, ...), custom_call_target="tpu_custom_call" | custom-call | flops 650000000 | bytes 7330848 | tf_op jit(solution)/shard_map/pallas_call | solution.py:536
  12.5 5.9 %collective-permute-start = (bf16[144,384]{1,0:T(8,128)(2,1)}, bf16[144,384]{1,0:T(8,128)(2,1)S(1)}, u32[]{:S(2)}, u32[]{:S(2)}) collective-permute-start(bf16[144,384]{1,0:T(8,128)(2,1)} %get-tuple-element.52), channel_id=1, source_target_pairs={{8,0},{9,1},{10,2},{11,3},{12,4},{13,5},{14,6},{15,7},{16,8},{17,9... | collective-permute-start | bytes 331784 | tf_op jit(solution)/shard_map/ppermute | solution.py:559
  18.4 0.7 collective-permute-start.3
  19.2 3.3 %collective-permute-start.4 = (bf16[18,384]{1,0:T(8,128)(2,1)S(1)}, bf16[18,384]{1,0:T(8,128)(2,1)S(1)}, u32[]{:S(2)}, u32[]{:S(2)}) collective-permute-start(bf16[18,384]{1,0:T(8,128)(2,1)S(1)} %reshape.43), channel_id=1, source_target_pairs={{1,0},{2,1},{3,2},{4,3},{5,4},{6,5},{7,6},{0,7},{9,8},{10,9},{11,1... | collective-permute-start | bytes 41480 | tf_op jit(solution)/shard_map/ppermute | solution.py:560
  22.4 1.0 collective-permute-start.1
  23.4 0.0 collective-permute-start.2
  23.5 0.4 collective-permute-done.4.cot_side_ref
  23.9 2.7 %collective-permute-start.5 = (bf16[18,384]{1,0:T(8,128)(2,1)S(1)}, bf16[18,384]{1,0:T(8,128)(2,1)S(1)}, u32[]{:S(2)}, u32[]{:S(2)}) collective-permute-start(bf16[18,384]{1,0:T(8,128)(2,1)S(1)} %reshape.44), channel_id=1, source_target_pairs={{9,0},{10,1},{11,2},{12,3},{13,4},{14,5},{15,6},{8,7},{17,8},{18,9... | collective-permute-start | bytes 41480 | tf_op jit(solution)/shard_map/ppermute | solution.py:561
  26.6 1.5 collective-permute-done.5.cot_corner_ref
  28.1 0.0 collective-permute-done.above_ref
  28.1 0.0 copy-start.9
  28.1 0.0 collective-permute-done.3.cot_above_ref
  28.2 0.0 copy-start.10
  28.2 0.5 copy-done.16
  28.7 0.0 copy-done.13
  28.7 0.0 copy-done.14
  28.7 0.1 copy-done.9
  28.8 0.0 copy-done.10
  28.8 14.3 %shard_map.198 = (bf16[144,384]{1,0:T(8,128)(2,1)}, bf16[144,384]{1,0:T(8,128)(2,1)}, bf16[32,384]{1,0:T(8,128)(2,1)}, bf16[32,384]{1,0:T(8,128)(2,1)}, bf16[144...) custom-call(bf16[144,384]{1,0:T(8,128)(2,1)} %get-tuple-element.51.o, ...), custom_call_target="tpu_custom_call" | custom-call | flops 2000000000 | bytes 4673056 | tf_op jit(solution)/shard_map/pallas_call | solution.py:536
  43.1 1.4 collective-permute-start.6
  44.5 1.5 collective-permute-start.7
  45.9 0.4 collective-permute-start.8
  46.4 4.5 %collective-permute-done.7.side_ref = bf16[32,384]{1,0:T(8,128)(2,1)S(1)} collective-permute-done((bf16[32,384]{1,0:T(8,128)(2,1)}, bf16[32,384]{1,0:T(8,128)(2,1)S(1)}, u32[]{:S(2)}, u32[]{:S(2)}) %collective-permute-start.7) | collective-permute-done | bytes 24608 | tf_op jit(solution)/shard_map/ppermute | solution.py:560
  50.9 4.4 %collective-permute-done.8.corner_ref = bf16[32,384]{1,0:T(8,128)(2,1)S(1)} collective-permute-done((bf16[32,384]{1,0:T(8,128)(2,1)}, bf16[32,384]{1,0:T(8,128)(2,1)S(1)}, u32[]{:S(2)}, u32[]{:S(2)}) %collective-permute-start.8) | collective-permute-done | bytes 24608 | tf_op jit(solution)/shard_map/ppermute | solution.py:561
  55.3 0.6 copy-done.7
  55.9 0.1 copy-done.3
  55.9 11.7 %shard_map.199 = (bf16[288,384]{1,0:T(8,128)(2,1)}, bf16[3584,128]{1,0:T(8,128)(2,1)}, bf16[3584,128]{1,0:T(8,128)(2,1)}, bf16[512,128]{1,0:T(8,128)(2,1)}) custom-call(bf16[144,384]{1,0:T(8,128)(2,1)} %get-tuple-element.66.back_ref, bf16[144,384]{1,0:T(8,128)(2,1)} %copy-done.3, bf16[32,384]{1,0:T(8,128)(2,1)} %copy-done.6, bf16[32,384]{1,0:T(8,128)(2,1)} %copy-done.7, ...), custom_call_target="tpu_custom_call" | custom-call | flops 1300000000 | bytes 10446112 | tf_op jit(solution)/shard_map/pallas_call | solution.py:536
  67.6 0.1 collective-permute-start.12
  67.7 2.7 %collective-permute-done.12.other_ref = bf16[3584,128]{1,0:T(8,128)(2,1)S(1)} collective-permute-done((bf16[3584,128]{1,0:T(8,128)(2,1)}, bf16[3584,128]{1,0:T(8,128)(2,1)S(1)}, u32[]{:S(2)}, u32[]{:S(2)}) %collective-permute-start.12) | collective-permute-done | bytes 917536 | tf_op jit(solution)/shard_map/ppermute | solution.py:572
  70.4 0.9 copy-done.2
  71.3 2.6 %shard_map.200 = bf16[8,512,128]{2,1,0:T(8,128)(2,1)} custom-call(bf16[3584,128]{1,0:T(8,128)(2,1)} %get-tuple-element.83.mine_ref, bf16[3584,128]{1,0:T(8,128)(2,1)} %copy-done.2, bf16[512,128]{1,0:T(8,128)(2,1)} %get-tuple-element.85.tables_ref), custom_call_target="tpu_custom_call" | custom-call | bytes 3014656 | tf_op jit(solution)/shard_map/pallas_call | solution.py:536
  73.9 20.2 %all_to_all.15.parts_ref = bf16[8,512,128]{2,1,0:T(8,128)(2,1)} all-to-all(bf16[8,512,128]{2,1,0:T(8,128)(2,1)} %shard_map.200), channel_id=1, replica_groups=mesh['lat'=16,'lon'=8] {'lon'}, dimensions={0} | all-to-all | bytes 2097152 | tf_op jit(solution)/shard_map/all_to_all | solution.py:575
  94.1 2.3 %shard_map.201 = (bf16[8,448,128]{2,1,0:T(8,128)(2,1)}, bf16[64,128]{1,0:T(8,128)(2,1)}) custom-call(bf16[8,512,128]{2,1,0:T(8,128)(2,1)} %all_to_all.15.parts_ref), custom_call_target="tpu_custom_call" | custom-call | bytes 1982464 | tf_op jit(solution)/shard_map/pallas_call | solution.py:536
  96.4 19.6 %all_to_all.16.parts_ref = bf16[8,448,128]{2,1,0:T(8,128)(2,1)} all-to-all(bf16[8,448,128]{2,1,0:T(8,128)(2,1)} %get-tuple-element.86), channel_id=1, replica_groups={{0,16,32,48,64,80,96,112},{8,24,40,56,72,88,104,120},{1,17,33,49,65,81,..., dimensions={0} | all-to-all | bytes 1835008 | tf_op jit(solution)/shard_map/all_to_all | solution.py:577
  116.0 2.3 %shard_map.202 = bf16[8,512,128]{2,1,0:T(8,128)(2,1)} custom-call(bf16[8,448,128]{2,1,0:T(8,128)(2,1)} %all_to_all.16.parts_ref, bf16[64,128]{1,0:T(8,128)(2,1)} %get-tuple-element.87.table_ref), custom_call_target="tpu_custom_call" | custom-call | bytes 1982464 | tf_op jit(solution)/shard_map/pallas_call | solution.py:536
  118.3 18.1 %all_to_all.17.mine_ref = bf16[8,512,128]{2,1,0:T(8,128)(2,1)S(1)} all-to-all(bf16[8,512,128]{2,1,0:T(8,128)(2,1)} %shard_map.202), channel_id=1, replica_groups=mesh['lat'=16,'lon'=8] {'lon'}, dimensions={0} | all-to-all | bytes 2097152 | tf_op jit(solution)/shard_map/all_to_all | solution.py:579
  136.4 0.0 collective-permute-start.13
  136.4 0.5 collective-permute-start.11
  136.9 1.2 collective-permute-start.10
  138.1 0.0 collective-permute-start.9
  138.1 4.9 %collective-permute-done.10 = bf16[32,384]{1,0:T(8,128)(2,1)S(1)} collective-permute-done((bf16[32,384]{1,0:T(8,128)(2,1)S(1)}, bf16[32,384]{1,0:T(8,128)(2,1)S(1)}, u32[]{:S(2)}, u32[]{:S(2)}) %collective-permute-start.10) | collective-permute-done | bytes 24608 | tf_op jit(solution)/shard_map/ppermute | solution.py:560
  143.0 3.8 %collective-permute-done.9 = bf16[32,384]{1,0:T(8,128)(2,1)S(1)} collective-permute-done((bf16[32,384]{1,0:T(8,128)(2,1)S(1)}, bf16[32,384]{1,0:T(8,128)(2,1)S(1)}, u32[]{:S(2)}, u32[]{:S(2)}) %collective-permute-start.9) | collective-permute-done | bytes 24608 | tf_op jit(solution)/shard_map/ppermute | solution.py:561
  146.9 0.1 slice.30
  147.0 0.8 pad_maximum_fusion.1
  147.7 1.0 copy-done.1
  148.7 3.6 %shard_map.203 = (f32[2,192,576]{2,1,0:T(8,128)}, f32[2,192,192]{2,1,0:T(8,128)}, f32[2,192,768]{2,1,0:T(8,128)}, f32[2,192,768]{2,1,0:T(8,128)}, f32[2,2,192]{2,1,0:T(2,128)}, /*index=5*/f32[2,1,6,3312]{3,2,1,0:T(8,128)}) custom-call(bf16[8,512,128]{2,1,0:T(8,128)(2,1)} %copy-done, bf16[8,512,128]{2,1,0:T(8,128)(2,1)} %copy-done.1), custom_call_target="tpu_custom_call" | custom-call | bytes 5798144 | tf_op jit(solution)/shard_map/pallas_call | solution.py:536
  152.3 1.8 %copy.24 = f32[2,1,6,3312]{3,1,2,0:T(1,128)} copy(f32[2,1,6,3312]{3,2,1,0:T(8,128)} %get-tuple-element.101) | data formatting | bytes 317952
  (37 shorter events, 0.2 us)
Async XLA Ops:
  2.3 16.1 %copy-start.5 = (bf16[6,48,384]{2,1,0:T(8,128)(2,1)S(1)}, bf16[6,48,384]{2,1,0:T(8,128)(2,1)}, u32[]{:S(2)}) copy-start(bf16[6,48,384]{2,1,0:T(8,128)(2,1)} %param.15) | copy-start | bytes 663556
  12.5 15.6 %collective-permute-start = (bf16[144,384]{1,0:T(8,128)(2,1)}, bf16[144,384]{1,0:T(8,128)(2,1)S(1)}, u32[]{:S(2)}, u32[]{:S(2)}) collective-permute-start(bf16[144,384]{1,0:T(8,128)(2,1)} %get-tuple-element.52), channel_id=1, source_target_pairs={{8,0},{9,1},{10,2},{11,3},{12,4},{13,5},{14,6},{15,7},{16,8},{17,9... | collective-permute-start | bytes 331784 | tf_op jit(solution)/shard_map/ppermute | solution.py:559
  18.4 9.8 %collective-permute-start.3 = (bf16[144,384]{1,0:T(8,128)(2,1)S(1)}, bf16[144,384]{1,0:T(8,128)(2,1)S(1)}, u32[]{:S(2)}, u32[]{:S(2)}) collective-permute-start(bf16[144,384]{1,0:T(8,128)(2,1)S(1)} %bitcast.12), channel_id=1, source_target_pairs={{8,0},{9,1},{10,2},{11,3},{12,4},{13,5},{14,6},{15,7},{16,8},{17,9... | collective-permute-start | bytes 331784 | tf_op jit(solution)/shard_map/ppermute | solution.py:559
  19.2 4.8 %collective-permute-start.4 = (bf16[18,384]{1,0:T(8,128)(2,1)S(1)}, bf16[18,384]{1,0:T(8,128)(2,1)S(1)}, u32[]{:S(2)}, u32[]{:S(2)}) collective-permute-start(bf16[18,384]{1,0:T(8,128)(2,1)S(1)} %reshape.43), channel_id=1, source_target_pairs={{1,0},{2,1},{3,2},{4,3},{5,4},{6,5},{7,6},{0,7},{9,8},{10,9},{11,1... | collective-permute-start | bytes 41480 | tf_op jit(solution)/shard_map/ppermute | solution.py:560
  22.4 5.7 %collective-permute-start.1 = (bf16[32,384]{1,0:T(8,128)(2,1)}, bf16[32,384]{1,0:T(8,128)(2,1)S(1)}, u32[]{:S(2)}, u32[]{:S(2)}) collective-permute-start(bf16[32,384]{1,0:T(8,128)(2,1)} %get-tuple-element.53), channel_id=1, source_target_pairs={{1,0},{2,1},{3,2},{4,3},{5,4},{6,5},{7,6},{0,7},{9,8},{10,9},{11,1... | collective-permute-start | bytes 73736 | tf_op jit(solution)/shard_map/ppermute | solution.py:560
  23.4 4.7 %collective-permute-start.2 = (bf16[32,384]{1,0:T(8,128)(2,1)}, bf16[32,384]{1,0:T(8,128)(2,1)S(1)}, u32[]{:S(2)}, u32[]{:S(2)}) collective-permute-start(bf16[32,384]{1,0:T(8,128)(2,1)} %get-tuple-element.54), channel_id=1, source_target_pairs={{9,0},{10,1},{11,2},{12,3},{13,4},{14,5},{15,6},{8,7},{17,8},{18,9... | collective-permute-start | bytes 73736 | tf_op jit(solution)/shard_map/ppermute | solution.py:561
  23.9 4.3 %copy-start.15 = (bf16[18,384]{1,0:T(8,128)(2,1)}, bf16[18,384]{1,0:T(8,128)(2,1)S(1)}, u32[]{:S(2)}) copy-start(bf16[18,384]{1,0:T(8,128)(2,1)S(1)} %collective-permute-done.4.cot_side_ref) | copy-start | bytes 41476
  23.9 4.2 %collective-permute-start.5 = (bf16[18,384]{1,0:T(8,128)(2,1)S(1)}, bf16[18,384]{1,0:T(8,128)(2,1)S(1)}, u32[]{:S(2)}, u32[]{:S(2)}) collective-permute-start(bf16[18,384]{1,0:T(8,128)(2,1)S(1)} %reshape.44), channel_id=1, source_target_pairs={{9,0},{10,1},{11,2},{12,3},{13,4},{14,5},{15,6},{8,7},{17,8},{18,9... | collective-permute-start | bytes 41480 | tf_op jit(solution)/shard_map/ppermute | solution.py:561
  28.1 0.6 copy-start.16
  28.1 0.6 copy-start.13
  28.1 0.6 copy-start.14
  28.1 0.6 copy-start.9
  28.2 0.7 copy-start.10
  43.1 12.1 %collective-permute-start.6 = (bf16[144,384]{1,0:T(8,128)(2,1)}, bf16[144,384]{1,0:T(8,128)(2,1)S(1)}, u32[]{:S(2)}, u32[]{:S(2)}) collective-permute-start(bf16[144,384]{1,0:T(8,128)(2,1)} %get-tuple-element.59), channel_id=1, source_target_pairs={{120,0},{121,1},{122,2},{123,3},{124,4},{125,5},{126,6},{127,7},{0... | collective-permute-start | bytes 331784 | tf_op jit(solution)/shard_map/ppermute | solution.py:559
  44.5 6.4 %collective-permute-start.7 = (bf16[32,384]{1,0:T(8,128)(2,1)}, bf16[32,384]{1,0:T(8,128)(2,1)S(1)}, u32[]{:S(2)}, u32[]{:S(2)}) collective-permute-start(bf16[32,384]{1,0:T(8,128)(2,1)} %get-tuple-element.60), channel_id=1, source_target_pairs={{7,0},{0,1},{1,2},{2,3},{3,4},{4,5},{5,6},{6,7},{15,8},{8,9},{9,10... | collective-permute-start | bytes 73736 | tf_op jit(solution)/shard_map/ppermute | solution.py:560
  45.9 9.3 %collective-permute-start.8 = (bf16[32,384]{1,0:T(8,128)(2,1)}, bf16[32,384]{1,0:T(8,128)(2,1)S(1)}, u32[]{:S(2)}, u32[]{:S(2)}) collective-permute-start(bf16[32,384]{1,0:T(8,128)(2,1)} %get-tuple-element.61), channel_id=1, source_target_pairs={{127,0},{120,1},{121,2},{122,3},{123,4},{124,5},{125,6},{126,7},{7... | collective-permute-start | bytes 73736 | tf_op jit(solution)/shard_map/ppermute | solution.py:561
  50.9 4.4 %copy-start.6 = (bf16[32,384]{1,0:T(8,128)(2,1)}, bf16[32,384]{1,0:T(8,128)(2,1)S(1)}, u32[]{:S(2)}) copy-start(bf16[32,384]{1,0:T(8,128)(2,1)S(1)} %collective-permute-done.7.side_ref) | copy-start | bytes 73732
  55.3 0.6 copy-start.7
  55.3 0.6 copy-start.3
  67.6 2.8 %collective-permute-start.12 = (bf16[3584,128]{1,0:T(8,128)(2,1)}, bf16[3584,128]{1,0:T(8,128)(2,1)S(1)}, u32[]{:S(2)}, u32[]{:S(2)}) collective-permute-start(bf16[3584,128]{1,0:T(8,128)(2,1)} %get-tuple-element.84), channel_id=1, source_target_pairs={{8,0},{0,8},{24,16},{16,24},{40,32},{32,40},{56,48},{48,56},{72,64... | collective-permute-start | bytes 2752520 | tf_op jit(solution)/shard_map/ppermute | solution.py:572
  70.4 0.9 copy-start.2
  118.3 18.1 %copy-start.8 = (bf16[144,384]{1,0:T(8,128)(2,1)S(1)}, bf16[144,384]{1,0:T(8,128)(2,1)}, u32[]{:S(2)}) copy-start(bf16[144,384]{1,0:T(8,128)(2,1)} %get-tuple-element.64) | copy-start | bytes 331780
  118.3 18.6 %copy-start.12 = (bf16[32,384]{1,0:T(8,128)(2,1)S(1)}, bf16[32,384]{1,0:T(8,128)(2,1)}, u32[]{:S(2)}) copy-start(bf16[32,384]{1,0:T(8,128)(2,1)} %get-tuple-element.63) | copy-start | bytes 73732
  118.3 19.9 %copy-start.11 = (bf16[32,384]{1,0:T(8,128)(2,1)S(1)}, bf16[32,384]{1,0:T(8,128)(2,1)}, u32[]{:S(2)}) copy-start(bf16[32,384]{1,0:T(8,128)(2,1)} %get-tuple-element.62) | copy-start | bytes 73732
  118.3 28.6 %copy-start.4 = (bf16[144,384]{1,0:T(8,128)(2,1)S(1)}, bf16[144,384]{1,0:T(8,128)(2,1)}, u32[]{:S(2)}) copy-start(bf16[144,384]{1,0:T(8,128)(2,1)} %get-tuple-element.65) | copy-start | bytes 331780
  136.4 11.3 %copy-start = (bf16[8,512,128]{2,1,0:T(8,128)(2,1)}, bf16[8,512,128]{2,1,0:T(8,128)(2,1)S(1)}, u32[]{:S(2)}) copy-start(bf16[8,512,128]{2,1,0:T(8,128)(2,1)S(1)} %all_to_all.17.mine_ref) | copy-start | bytes 3145732
  136.4 11.3 %collective-permute-start.13 = (bf16[8,512,128]{2,1,0:T(8,128)(2,1)S(1)}, bf16[8,512,128]{2,1,0:T(8,128)(2,1)S(1)}, u32[]{:S(2)}, u32[]{:S(2)}) collective-permute-start(bf16[8,512,128]{2,1,0:T(8,128)(2,1)S(1)} %all_to_all.17.mine_ref), channel_id=1, source_target_pairs={{8,0},{0,8},{24,16},{16,24},{40,32},{32,40},{56,48},{48,56},{72,64... | collective-permute-start | bytes 3145736 | tf_op jit(solution)/shard_map/ppermute | solution.py:580
  136.4 10.4 %collective-permute-start.11 = (bf16[144,384]{1,0:T(8,128)(2,1)S(1)}, bf16[144,384]{1,0:T(8,128)(2,1)S(1)}, u32[]{:S(2)}, u32[]{:S(2)}) collective-permute-start(bf16[144,384]{1,0:T(8,128)(2,1)S(1)} %copy-done.8), channel_id=1, source_target_pairs={{120,0},{121,1},{122,2},{123,3},{124,4},{125,5},{126,6},{127,7},{0... | collective-permute-start | bytes 331784 | tf_op jit(solution)/shard_map/ppermute | solution.py:559
  136.9 6.1 %collective-permute-start.10 = (bf16[32,384]{1,0:T(8,128)(2,1)S(1)}, bf16[32,384]{1,0:T(8,128)(2,1)S(1)}, u32[]{:S(2)}, u32[]{:S(2)}) collective-permute-start(bf16[32,384]{1,0:T(8,128)(2,1)S(1)} %copy-done.12), channel_id=1, source_target_pairs={{7,0},{0,1},{1,2},{2,3},{3,4},{4,5},{5,6},{6,7},{15,8},{8,9},{9,10... | collective-permute-start | bytes 73736 | tf_op jit(solution)/shard_map/ppermute | solution.py:560
  138.1 8.7 %collective-permute-start.9 = (bf16[32,384]{1,0:T(8,128)(2,1)S(1)}, bf16[32,384]{1,0:T(8,128)(2,1)S(1)}, u32[]{:S(2)}, u32[]{:S(2)}) collective-permute-start(bf16[32,384]{1,0:T(8,128)(2,1)S(1)} %copy-done.11), channel_id=1, source_target_pairs={{127,0},{120,1},{121,2},{122,3},{123,4},{124,5},{125,6},{126,7},{7... | collective-permute-start | bytes 73736 | tf_op jit(solution)/shard_map/ppermute | solution.py:561
  147.7 1.0 copy-start.1

commit v3 on v2

--- a/solution.py
+++ b/solution.py
@@ -171,7 +171,7 @@
 
 
 def expand_table(table_ref, trows_ref, tcols_ref, bias_ref):
-    table = jnp.concatenate([table_ref[...] * LOG2E, jnp.zeros((2, TABLE), F32)], axis=0)
+    table = jnp.concatenate([table_ref[h] for h in range(HEADS)] + [jnp.zeros((2, TABLE), F32)], axis=0) * LOG2E
     table = jnp.concatenate([table[:, k * CELL : (k + 1) * CELL] for k in range(24)], axis=0)
     high = table.astype(BF16)
     low = (table - high.astype(F32)).astype(BF16)
@@ -288,22 +288,25 @@
     return gblock, normed, gbranch, gain_grad
 
 
-def first_forward(
-    x_ref, gains_ref, qkv_ref, out_ref, up_ref, down_ref, table_ref, trows_ref, tcols_ref, pick_ref, strips_ref,
-    xw_ref, q_ref, k_ref, v_ref, probs_ref, ctx_ref, hidden_ref, expanded_ref, slope_ref, top_ref, bottom_ref, side_ref, corner_ref,
-    bias_ref,
+def first_attention(
+    x_ref, gains_ref, qkv_ref, out_ref, table_ref, trows_ref, tcols_ref, pick_ref,
+    xw_ref, q_ref, k_ref, v_ref, probs_ref, ctx_ref, hidden_ref, bias_ref,
 ):
-    masks = head_rows()
     x = gather_tokens(pick_ref[...], x_ref[...])
     xw_ref[...] = x.astype(BF16)
     hat, _ = normalize(x)
-    normed = (hat * gains_ref[0:1, :]).astype(BF16)
-    project(normed, qkv_ref, q_ref, k_ref, v_ref)
+    project((hat * gains_ref[0:1, :]).astype(BF16), qkv_ref, q_ref, k_ref, v_ref)
     expand_table(table_ref, trows_ref, tcols_ref, bias_ref)
-    attention(q_ref, k_ref, v_ref, bias_ref, probs_ref, ctx_ref, masks)
+    attention(q_ref, k_ref, v_ref, bias_ref, probs_ref, ctx_ref, head_rows())
     branch = nn(ctx_ref[...], out_ref[...]).astype(BF16)
-    hidden = xw_ref[...].astype(F32) + branch.astype(F32)
-    hidden_ref[...] = hidden
+    hidden_ref[...] = xw_ref[...].astype(F32) + branch.astype(F32)
+
+
+def first_mlp(
+    hidden_ref, gains_ref, up_ref, down_ref, pick_ref, strips_ref,
+    expanded_ref, slope_ref, top_ref, bottom_ref, side_ref, corner_ref,
+):
+    hidden = hidden_ref[...]
     hat, _ = normalize(hidden)
     normed_mlp = (hat * gains_ref[1:2, :]).astype(BF16)
     total = hidden
@@ -338,30 +341,37 @@
     corner_ref[...] = value[288 + STRIP :]
 
 
+def prepare_second(
+    cot_ref, above_ref, side_ref, corner_ref, down_ref, table_ref, trows_ref, tcols_ref, pick_ref,
+    g_ref, gact_ref, bias_ref, source_ref,
+):
+    fill_source(source_ref, cot_ref[144:288, :], above_ref, side_ref, corner_ref)
+    g_ref[...] = gather_tokens(pick_ref[...], source_ref[...]).astype(BF16)
+    for j in range(3):
+        cols = slice(j * 256, (j + 1) * 256)
+        gact_ref[:, cols] = nn(g_ref[...], down_ref[:, cols]).astype(BF16)
+    expand_table(table_ref, trows_ref, tcols_ref, bias_ref)
+    add_mask(bias_ref, (lax.axis_index("lat") == lax.axis_size("lat") - 1).astype(F32))
+
+
 def second_both(
-    own_ref, above_ref, side_ref, corner_ref, cot_ref, cot_above_ref, cot_side_ref, cot_corner_ref,
-    gains_ref, qkv_ref, out_ref, up_ref, down_ref, table_ref, trows_ref, tcols_ref, pick_ref,
+    own_ref, above_ref, side_ref, corner_ref, g_ref, gact_ref, bias_ref,
+    gains_ref, qkv_ref, out_ref, up_ref, down_ref, pick_ref,
     y_own_ref, y_row_ref, y_side_ref, y_corner_ref, back_own_ref, back_row_ref, back_side_ref, back_corner_ref,
-    wbuf_ref, gain_grad_ref, table_grad_ref,
-    source_ref, x_ref, q_ref, k_ref, v_ref, probs_ref, ctx_ref, bias_ref, gctx_ref, dq_ref, dk_ref, dv_ref, gpre_ref, expanded_ref,
+    normed_ref, dq_ref, dk_ref, dv_ref, ctx_ref, gbranch_ref, normed_mlp_ref, gpre_ref, expanded_ref, grad_ref, gain_grad_ref,
+    source_ref, x_ref, q_ref, k_ref, v_ref, probs_ref, gctx_ref,
 ):
     masks = head_rows()
-
     fill_source(source_ref, own_ref[...], above_ref, side_ref, corner_ref)
     x_ref[...] = gather_tokens(pick_ref[...], source_ref[...])
     hat, _ = normalize(x_ref[...])
-    normed = (hat * gains_ref[0:1, :]).astype(BF16)
-    project(normed, qkv_ref, q_ref, k_ref, v_ref)
-    expand_table(table_ref, trows_ref, tcols_ref, bias_ref)
-    add_mask(bias_ref, (lax.axis_index("lat") == lax.axis_size("lat") - 1).astype(F32))
+    project((hat * gains_ref[0:1, :]).astype(BF16), qkv_ref, q_ref, k_ref, v_ref)
     attention(q_ref, k_ref, v_ref, bias_ref, probs_ref, ctx_ref, masks)
     branch = nn(ctx_ref[...], out_ref[...]).astype(BF16)
     hidden = x_ref[...] + branch.astype(F32)
     hat_mlp, inv_mlp = normalize(hidden)
     normed_mlp = (hat_mlp * gains_ref[1:2, :]).astype(BF16)
-    fill_source(source_ref, cot_ref[144:288, :], cot_above_ref, cot_side_ref, cot_corner_ref)
-    g32 = gather_tokens(pick_ref[...], source_ref[...])
-    g = g32.astype(BF16)
+    normed_mlp_ref[...] = normed_mlp
     total = hidden
     gnormed = jnp.zeros((TOKENS, DIM), F32)
     for j in range(3):
@@ -371,43 +381,46 @@
         expanded = (pre * below).astype(BF16)
         expanded_ref[:, cols] = expanded
         total = total + nt(expanded, down_ref[:, cols])
-        gact = nn(g, down_ref[:, cols]).astype(BF16).astype(F32)
-        gpre = ((below + pre * density) * gact).astype(BF16)
+        gpre = ((below + pre * density) * gact_ref[:, cols].astype(F32)).astype(BF16)
         gpre_ref[:, cols] = gpre
         gnormed = gnormed + nt(gpre, up_ref[:, cols])
     y = scatter_tokens(pick_ref[...], total.astype(BF16)).astype(BF16)
     put_source(y_own_ref, y_row_ref, y_side_ref, y_corner_ref, y)
     gnormed = gnormed.astype(BF16).astype(F32)
     gain_grad_ref[1:2, :] = jnp.sum(gnormed * hat_mlp, axis=0, keepdims=True)
-    ghid = g32 + norm_backward(gnormed, gains_ref[1:2, :], hat_mlp, inv_mlp)
+    ghid = g_ref[...].astype(F32) + norm_backward(gnormed, gains_ref[1:2, :], hat_mlp, inv_mlp)
     gblock, normed, gbranch, gain_grad = attention_backward_part(
         x_ref[...], gains_ref[0:1, :], qkv_ref, out_ref, ghid,
-        q_ref, k_ref, v_ref, probs_ref, ctx_ref, gctx_ref, dq_ref, dk_ref, dv_ref, bias_ref, masks,
+        q_ref, k_ref, v_ref, probs_ref, ctx_ref, gctx_ref, dq_ref, dk_ref, dv_ref, grad_ref, masks,
     )
     gain_grad_ref[0:1, :] = gain_grad
     back = scatter_tokens(pick_ref[...], gblock.astype(BF16)).astype(BF16)
     put_source(back_own_ref, back_row_ref, back_side_ref, back_corner_ref, back)
+    normed_ref[...] = normed
+    gbranch_ref[...] = gbranch
+
+
+def second_weights(
+    normed_ref, dq_ref, dk_ref, dv_ref, ctx_ref, gbranch_ref, normed_mlp_ref, gpre_ref, expanded_ref, grad_ref, g_ref,
+    trows_ref, tcols_ref, wbuf_ref, table_grad_ref,
+):
     weight_grads(
-        wbuf_ref, normed, dq_ref[...], dk_ref[...], dv_ref[...], ctx_ref[...], gbranch, normed_mlp, gpre_ref, expanded_ref, g
+        wbuf_ref, normed_ref[...], dq_ref[...], dk_ref[...], dv_ref[...], ctx_ref[...], gbranch_ref[...],
+        normed_mlp_ref[...], gpre_ref, expanded_ref, g_ref[...],
     )
-    table_grad_ref[...] = collapse_table(bias_ref, trows_ref, tcols_ref)
-
-
-def first_backward(
-    back_ref, above_ref, side_ref, corner_ref, xw_ref, q_ref, k_ref, v_ref, probs_ref, ctx_ref, hidden_ref, expanded_ref, slope_ref,
-    gains_ref, qkv_ref, out_ref, up_ref, down_ref, trows_ref, tcols_ref, pick_ref, returned_ref,
-    last_wbuf_ref, last_gain_ref, last_table_ref,
-    gin_ref, mine_ref, theirs_ref, tables_ref,
-    source_ref, gctx_ref, dq_ref, dk_ref, dv_ref, gpre_ref, grad_ref, wbuf_ref, gain_grad_ref, sems,
+    table_grad_ref[...] = collapse_table(grad_ref, trows_ref, tcols_ref)
+
+
+def first_mlp_back(
+    back_ref, above_ref, side_ref, corner_ref, hidden_ref, slope_ref, gains_ref, up_ref, down_ref, returned_ref,
+    g_ref, ghid_ref, normed_mlp_ref, gpre_ref, gain_grad_ref, source_ref,
 ):
-    masks = head_rows()
-    fetch = pltpu.make_async_copy(last_wbuf_ref, wbuf_ref.at[pl.ds(WBLOCK, WBLOCK), :], sems.at[0])
-    fetch.start()
     fill_source(source_ref, back_ref[...], above_ref, side_ref, corner_ref)
     g32 = gather_tokens(returned_ref[...], source_ref[...])
     g = g32.astype(BF16)
+    g_ref[...] = g
     hat_mlp, inv_mlp = normalize(hidden_ref[...])
-    normed_mlp = (hat_mlp * gains_ref[1:2, :]).astype(BF16)
+    normed_mlp_ref[...] = (hat_mlp * gains_ref[1:2, :]).astype(BF16)
     gnormed = jnp.zeros((TOKENS, DIM), F32)
     for j in range(3):
         cols = slice(j * 256, (j + 1) * 256)
@@ -416,21 +429,32 @@
         gpre_ref[:, cols] = gpre
         gnormed = gnormed + nt(gpre, up_ref[:, cols])
     gnormed = gnormed.astype(BF16).astype(F32)
-    gain_grad_ref[1:2, :] = jnp.sum(gnormed * hat_mlp, axis=0, keepdims=True)
-    ghid = g32 + norm_backward(gnormed, gains_ref[1:2, :], hat_mlp, inv_mlp)
+    gain_grad_ref[...] = jnp.sum(gnormed * hat_mlp, axis=0, keepdims=True)
+    ghid_ref[...] = g32 + norm_backward(gnormed, gains_ref[1:2, :], hat_mlp, inv_mlp)
+
+
+def first_attention_back(
+    ghid_ref, g_ref, normed_mlp_ref, gpre_ref, mlp_gain_ref, xw_ref, q_ref, k_ref, v_ref, probs_ref, ctx_ref, expanded_ref,
+    gains_ref, qkv_ref, out_ref, trows_ref, tcols_ref, pick_ref, last_wbuf_ref, last_gain_ref, last_table_ref,
+    gin_ref, mine_ref, theirs_ref, tables_ref,
+    gctx_ref, dq_ref, dk_ref, dv_ref, grad_ref, wbuf_ref, sems,
+):
+    masks = head_rows()
+    fetch = pltpu.make_async_copy(last_wbuf_ref, wbuf_ref.at[pl.ds(WBLOCK, WBLOCK), :], sems.at[0])
+    fetch.start()
     gblock, normed, gbranch, gain_grad = attention_backward_part(
-        xw_ref[...].astype(F32), gains_ref[0:1, :], qkv_ref, out_ref, ghid,
+        xw_ref[...].astype(F32), gains_ref[0:1, :], qkv_ref, out_ref, ghid_ref[...],
         q_ref, k_ref, v_ref, probs_ref, ctx_ref, gctx_ref, dq_ref, dk_ref, dv_ref, grad_ref, masks,
     )
-    gain_grad_ref[0:1, :] = gain_grad
     gin_ref[...] = scatter_tokens(pick_ref[...], gblock.astype(BF16)).astype(BF16)
     weight_grads(
-        wbuf_ref, normed, dq_ref[...], dk_ref[...], dv_ref[...], ctx_ref[...], gbranch, normed_mlp, gpre_ref, expanded_ref, g
+        wbuf_ref, normed, dq_ref[...], dk_ref[...], dv_ref[...], ctx_ref[...], gbranch,
+        normed_mlp_ref[...], gpre_ref, expanded_ref, g_ref[...],
     )
     tables_ref[0:TROWS, :] = collapse_table(grad_ref, trows_ref, tcols_ref)
     tables_ref[TROWS : 2 * TROWS, :] = last_table_ref[...]
     tables_ref[2 * TROWS :, :] = jnp.zeros((8 * TCHUNK - 2 * TROWS, 128), BF16)
-    gains = jnp.concatenate([ref[i : i + 1, :] for ref in (gain_grad_ref, last_gain_ref) for i in range(2)], axis=1)
+    gains = jnp.concatenate([gain_grad, mlp_gain_ref[...], last_gain_ref[0:1, :], last_gain_ref[1:2, :]], axis=1)
     wbuf_ref[2 * WBLOCK :, :] = jnp.zeros((2 * HALF - 2 * WBLOCK, 128), BF16)
     for j in range(6):
         tile = jnp.concatenate([gains[:, j * 128 : (j + 1) * 128], jnp.zeros((15, 128), F32)], axis=0)
@@ -509,7 +533,8 @@
             pair = mine_ref[k, base : base + 16, :].astype(F32)
             piece = pair[place % 16 : place % 16 + HEADS]
             width = min(128, TABLE - j * 128)
-            table_ref[b, 0, :, j * 128 : j * 128 + width] = piece[:, :width]
+            for h in range(HEADS):
+                table_ref[b * HEADS + h, :, j * 128 : j * 128 + width] = piece[h : h + 1, :width]
     gains = jnp.concatenate([load(2 * WBLOCK + j * 16, 16)[0:1] for j in range(6)], axis=1)
     for b in range(2):
         for i in range(2):
@@ -530,7 +555,7 @@
     return pl.BlockSpec(memory_space=pl.ANY)
 
 
-def call(kernel, operands, specs, outs, scratch=(), flops=0, out_specs=None):
+def call(kernel, operands, specs, outs, scratch=(), micros=2, out_specs=None, mebibytes=10):
     shapes = [jax.ShapeDtypeStruct(shape, dtype) for shape, dtype in outs]
     moved = sum(a.size * a.dtype.itemsize for a in (*operands, *shapes))
     return pl.pallas_call(
@@ -540,8 +565,8 @@
         in_specs=specs,
         out_specs=out_specs or [whole(s) for s in shapes],
         scratch_shapes=list(scratch),
-        cost_estimate=pl.CostEstimate(flops=flops, bytes_accessed=moved, transcendentals=0),
-        compiler_params=pltpu.CompilerParams(vmem_limit_bytes=56 * 1024 * 1024),
+        cost_estimate=pl.CostEstimate(flops=micros * 1_100_000_000, bytes_accessed=moved, transcendentals=0),
+        compiler_params=pltpu.CompilerParams(vmem_limit_bytes=mebibytes * 1024 * 1024),
     )(*operands)
 
 
@@ -579,7 +604,7 @@
     half = lax.all_to_all(spread, "lon", 0, 0)
     other = lax.ppermute(half, "lat", pairs)
     outs = [((2, DIM, 3 * DIM), F32), ((2, DIM, DIM), F32), ((2, DIM, UNITS), F32), ((2, DIM, UNITS), F32)]
-    outs += [((2, 2, DIM), F32), ((2, 1, HEADS, TABLE), F32)]
+    outs += [((2, 2, DIM), F32), ((2 * HEADS, 1, TABLE), F32)]
     return call(unpack, [half, other], [whole(half), whole(other)], outs)
 
 
@@ -597,54 +622,86 @@
     probs = (WINDOWS, WIN_TOK, QLANES)
 
     def table_spec(index):
-        return pl.BlockSpec((None, None, HEADS, TABLE), lambda i: (index, 0, 0, 0))
-
+        return pl.BlockSpec((HEADS, 1, TABLE), lambda i: (index, 0, 0))
+
+    bias_table = bias_table.reshape(2 * HEADS, 1, TABLE)
     cot_side = cotangent[3:, :6].reshape(18, 2 * DIM)
     cot_corner = cotangent[:3, :6].reshape(18, 2 * DIM)
     cot_strips = exchange(cot[:144], cot_side, cot_corner, sizes, 1)
 
-    fixed = (trows, tcols, pick_grid, strips)
-    operands = [x, *weights, bias_table, *fixed]
-    specs = [whole(x)] + [picked(a, 0) for a in weights] + [table_spec(0)] + [whole(a) for a in fixed]
-    outs = [(tok, BF16)] * 4 + [(probs, BF16), (tok, BF16), (tok, F32), (hid, BF16), (hid, BF16)]
-    outs += [(shape, BF16) for shape in strip_shapes]
-    results = call(first_forward, operands, specs, outs, [vmem((WIN_TOK, QLANES), F32)], 650_000_000)
-    saved, (top, bottom, side, corner) = results[:9], results[9:]
+    gains, qkv, out, up, down = weights
+    wide_tok, wide_hid = (tok, BF16), (hid, BF16)
+    bias = (WIN_TOK, QLANES)
+
+    def specs_for(arrays, index):
+        specs = []
+        for a in arrays:
+            if any(a is w for w in weights):
+                specs.append(picked(a, index))
+            elif a is bias_table:
+                specs.append(table_spec(index))
+            else:
+                specs.append(whole(a))
+        return specs
+
+    operands = [x, gains, qkv, out, bias_table, trows, tcols, pick_grid]
+    outs = [wide_tok] * 4 + [(probs, BF16), wide_tok, (tok, F32)]
+    results = call(first_attention, operands, specs_for(operands, 0), outs, [vmem(bias, F32)], 7, mebibytes=14)
+    xw, q, k, v, probs_first, ctx, hidden = results
+    hidden, cot_strips = lax.optimization_barrier((hidden, cot_strips))
+
+    operands = [hidden, gains, up, down, pick_grid, strips]
+    outs = [wide_hid, wide_hid] + [(shape, BF16) for shape in strip_shapes]
+    results = call(first_mlp, operands, specs_for(operands, 0), outs, (), 4, mebibytes=14)
+    expanded, slope, top, bottom, side, corner = results
+    (top, side, corner), cot_strips = lax.optimization_barrier(((top, side, corner), cot_strips))
 
     own_strips = exchange(top, side, corner, sizes, 1)
-    fixed = (trows, tcols, pick_shift)
-    fields = (bottom, *own_strips, cot, *cot_strips)
-    operands = [*fields, *weights, bias_table, *fixed]
-    specs = [whole(a) for a in fields] + [picked(a, 1) for a in weights] + [table_spec(1)] + [whole(a) for a in fixed]
-    outs = [(shape, BF16) for shape in strip_shapes] * 2
-    outs += [((WBLOCK, 128), BF16), ((2, DIM), F32), ((TROWS, 128), BF16)]
+    operands = [cot, *cot_strips, down, bias_table, trows, tcols, pick_shift]
+    outs = [wide_tok, wide_hid, (bias, F32)]
+    g, gact, bias_last = call(
+        prepare_second, operands, specs_for(operands, 1), outs, [vmem(src, BF16)], 3, mebibytes=14
+    )
+
+    operands = [bottom, *own_strips, g, gact, bias_last, *weights, pick_shift]
+    outs = [(shape, BF16) for shape in strip_shapes] * 2 + [wide_tok] * 7 + [wide_hid] * 2 + [(bias, F32), ((2, DIM), F32)]
     scratch = [vmem(src, BF16), vmem(tok, F32)] + [vmem(tok, BF16)] * 3 + [vmem(probs, BF16), vmem(tok, BF16)]
-    scratch += [vmem((WIN_TOK, QLANES), F32)] + [vmem(tok, BF16)] * 4 + [vmem(hid, BF16)] * 2
-    results = call(second_both, operands, specs, outs, scratch, 2_000_000_000)
-    y_strips, back_strips, last_grads = results[:4], results[4:8], results[8:]
+    results = call(second_both, operands, specs_for(operands, 1), outs, scratch, 12, mebibytes=14)
+    y_strips, back_strips, terms, last_gain = results[:4], results[4:8], results[8:18], results[18]
 
     back = exchange(*back_strips[1:], sizes, -1)
+    operands = [*terms, g, trows, tcols]
+    outs = [((WBLOCK, 128), BF16), ((TROWS, 128), BF16)]
+    last_wbuf, last_table = call(second_weights, operands, specs_for(operands, 1), outs, (), 4, mebibytes=14)
     y_strips, back = lax.optimization_barrier((y_strips, back))
-    fixed = (trows, tcols, pick_grid, pick_back)
-    operands = [back_strips[0], *back, *saved, *weights, *fixed, *last_grads]
-    specs = [whole(a) for a in (back_strips[0], *back, *saved)] + [picked(a, 0) for a in weights]
-    specs += [whole(a) for a in fixed] + [in_place(), whole(last_grads[1]), whole(last_grads[2])]
+    y_moved = exchange(*y_strips[1:], sizes, -1)
+
+    operands = [back_strips[0], *back, hidden, slope, gains, up, down, pick_back]
+    outs = [wide_tok, (tok, F32), wide_tok, wide_hid, ((1, DIM), F32)]
+    results = call(first_mlp_back, operands, specs_for(operands, 0), outs, [vmem(src, BF16)], 3, mebibytes=14)
+    g, ghid, normed_mlp, gpre, mlp_gain = results
+    ghid, y_moved = lax.optimization_barrier((ghid, y_moved))
+
+    operands = [ghid, g, normed_mlp, gpre, mlp_gain, xw, q, k, v, probs_first, ctx, expanded, gains, qkv, out]
+    operands += [trows, tcols, pick_grid, last_wbuf, last_gain, last_table]
+    specs = specs_for(operands, 0)
+    specs[-3] = in_place()
     outs = [((GRID, 2 * DIM), BF16), ((HALF, 128), BF16), ((HALF, 128), BF16), ((8 * TCHUNK, 128), BF16)]
     out_specs = [pl.BlockSpec((GRID, 2 * DIM), lambda i: (0, 0)), in_place(), in_place()]
     out_specs += [pl.BlockSpec((8 * TCHUNK, 128), lambda i: (0, 0))]
-    scratch = [vmem(src, BF16)] + [vmem(tok, BF16)] * 4 + [vmem(hid, BF16), vmem((WIN_TOK, QLANES), F32)]
-    scratch += [vmem((2 * HALF, 128), BF16), vmem((2, DIM), F32), pltpu.SemaphoreType.DMA((3,))]
+    scratch = [vmem(tok, BF16)] * 4 + [vmem(bias, F32), vmem((2 * HALF, 128), BF16), pltpu.SemaphoreType.DMA((3,))]
     grad_inputs, mine, theirs, tables = call(
-        first_backward, operands, specs, outs, scratch, 1_300_000_000, out_specs
+        first_attention_back, operands, specs, outs, scratch, 8, out_specs, 14
     )
 
-    y_rows, y_side, y_corner = exchange(*y_strips[1:], sizes, -1)
+    y_rows, y_side, y_corner = y_moved
     rows = jnp.concatenate([y_rows, y_strips[0]]).reshape(ROWS, COLS, 2 * DIM)
     edge = jnp.concatenate([y_corner[:18].reshape(3, 6, 2 * DIM), y_side[:18].reshape(3, 6, 2 * DIM)])
     output = jnp.concatenate([edge, rows[:, 6:]], axis=1)
 
     grad_qkv, grad_out, grad_up, grad_down, grad_gains, grad_table = sum_over_devices(mine, theirs, tables, sizes)
     grad_down = jnp.swapaxes(grad_down, 1, 2)
+    grad_table = grad_table.reshape(2, 1, HEADS, TABLE)
     return (output, grad_inputs.reshape(ROWS, COLS, 2 * DIM), grad_gains, grad_qkv, grad_out, grad_up, grad_down, grad_table)
 
 

time: 155 us -> 132 us (0.85)
  Pallas kernels: 47 us -> 30.4 us
  blocking collectives: 57.9 us -> 53.9 us
  starting transfers between devices: 18.8 us -> 15.4 us
  local copies, waits for them, and re-layouts: 6.72 us -> 9.17 us
  waiting for transfers between devices: 22.1 us -> 19.7 us
    pallas_call x7 -> x11, Pallas kernels: 47 us -> 30.4 us  [call(): pl.pallas_call(kernel, grid=(1,), out_shape=shapes, in_specs=specs, out_s...]
    ppermute x4, starting transfers between devices: 8.5 us -> 3.31 us  [exchange(): rows = lax.ppermute(rows, both, neighbour(sizes, (step, 0)))]
    ppermute x4, waiting for transfers between devices: 9.77 us -> 6.8 us  [exchange(): side = lax.ppermute(side, both, neighbour(sizes, (0, step)))]
    all_to_all x1, blocking collectives: 19.6 us -> 17.8 us  [sum_over_devices(): parts = lax.all_to_all(spread, 'lat', 0, 0, axis_index_groups=groups)]
    all_to_all x1, blocking collectives: 20.2 us -> 18.4 us  [sum_over_devices(): parts = lax.all_to_all(sent, 'lon', 0, 0)]
    ppermute x1, waiting for transfers between devices: 0.01 us -> 1.75 us  [sum_over_devices(): other = lax.ppermute(half, 'lat', pairs)]
    unnamed x36 -> x42, local copies, waits for them, and re-layouts: 6.59 us -> 7.4 us
  transfers between devices with their start and end apart: 14 -> 14, of which waited for: 7 -> 8; matrix products, arithmetic and copies ran while one was open for 1% -> 1% of each run, Pallas kernels for 0% -> 8%
where the time goes in v3:
time: 132 us; the launch traced here: 130 us
  blocking collectives  53.9 us (41%)
  Pallas kernels  30.4 us (23%)
  waiting for transfers between devices  19.7 us (15%)
  starting transfers between devices  15.4 us (12%)
  local copies, waits for them, and re-layouts  9.17 us (7%)
    pallas_call x11, Pallas kernels, call(): pl.pallas_call(kernel, grid=(1,), out_shape=shapes, in_specs=specs, out_s...  30.4 us
    all_to_all x1, blocking collectives, sum_over_devices(): parts = lax.all_to_all(sent, 'lon', 0, 0)  18.4 us
    all_to_all x1, blocking collectives, sum_over_devices(): parts = lax.all_to_all(spread, 'lat', 0, 0, axis_index_groups=groups)  17.8 us
    all_to_all x1, blocking collectives, sum_over_devices(): half = lax.all_to_all(spread, 'lon', 0, 0)  17.8 us
    ppermute x4, waiting for transfers between devices, exchange(): corner = lax.ppermute(corner, both, neighbour(sizes, (step, step)))  8.68 us
    unnamed x42, local copies, waits for them, and re-layouts  7.4 us
    ppermute x4, starting transfers between devices, exchange(): side = lax.ppermute(side, both, neighbour(sizes, (0, step)))  7.25 us
    ppermute x4, waiting for transfers between devices, exchange(): side = lax.ppermute(side, both, neighbour(sizes, (0, step)))  6.8 us
  transfers between devices with their start and end apart: 14, of which 8 were waited for; matrix products, arithmetic and copies ran while one was open for 1% of the time, Pallas kernels for 8%

profile of v3, /device:TPU:0, one launch (start us, length us, event | category | flops | bytes accessed | tf_op | source)
XLA Modules:
  0.0 130.3 jit_solution(2287752493473015698)
XLA Ops:
  0.6 0.7 fusion
  1.4 4.3 %collective-permute-start.1 = (bf16[18,384]{1,0:T(8,128)(2,1)S(1)}, bf16[18,384]{1,0:T(8,128)(2,1)S(1)}, u32[]{:S(2)}, u32[]{:S(2)}) collective-permute-start(bf16[18,384]{1,0:T(8,128)(2,1)S(1)} %reshape.49), channel_id=1, source_target_pairs={{1,0},{2,1},{3,2},{4,3},{5,4},{6,5},{7,6},{0,7},{9,8},{10,9},{11,1... | collective-permute-start | bytes 41480 | tf_op jit(solution)/shard_map/ppermute | solution.py:585
  5.7 4.2 %collective-permute-start.2 = (bf16[18,384]{1,0:T(8,128)(2,1)S(1)}, bf16[18,384]{1,0:T(8,128)(2,1)S(1)}, u32[]{:S(2)}, u32[]{:S(2)}) collective-permute-start(bf16[18,384]{1,0:T(8,128)(2,1)S(1)} %reshape.50), channel_id=1, source_target_pairs={{9,0},{10,1},{11,2},{12,3},{13,4},{14,5},{15,6},{8,7},{17,8},{18,9... | collective-permute-start | bytes 41480 | tf_op jit(solution)/shard_map/ppermute | solution.py:586
  9.9 0.9 slice.21
  10.8 2.1 %collective-permute-start = (bf16[144,384]{1,0:T(8,128)(2,1)S(1)}, bf16[144,384]{1,0:T(8,128)(2,1)S(1)}, u32[]{:S(2)}, u32[]{:S(2)}) collective-permute-start(bf16[144,384]{1,0:T(8,128)(2,1)S(1)} %bitcast.18), channel_id=1, source_target_pairs={{8,0},{9,1},{10,2},{11,3},{12,4},{13,5},{14,6},{15,7},{16,8},{17,9... | collective-permute-start | bytes 331784 | tf_op jit(solution)/shard_map/ppermute | solution.py:584
  12.9 1.0 copy-done.3
  13.9 0.9 copy-done.5
  14.8 0.9 copy-done.6
  15.8 0.9 copy-done.8
  16.7 0.7 copy-done.10
  17.4 1.0 copy-done.12
  18.4 0.9 copy-done.16
  19.3 0.9 copy-done.18
  20.2 5.0 %shard_map.197 = (bf16[576,192]{1,0:T(8,128)(2,1)S(1)}, bf16[576,192]{1,0:T(8,128)(2,1)S(1)}, bf16[576,192]{1,0:T(8,128)(2,1)S(1)}, bf16[576,192]{1,0:T(8,128)(2...) custom-call(bf16[288,384]{1,0:T(8,128)(2,1)S(1)} %bitcast.14, ...), custom_call_target="tpu_custom_call" | custom-call | flops 7699999744 | bytes 4074528 | tf_op jit(solution)/shard_map/pallas_call | solution.py:561
  25.3 0.0 copy-start.15
  25.3 2.5 %shard_map.198 = (bf16[576,768]{1,0:T(8,128)(2,1)S(1)}, bf16[576,768]{1,0:T(8,128)(2,1)S(1)}, bf16[144,384]{1,0:T(8,128)(2,1)S(1)}, bf16[144,384]{1,0:T(8,128)(2...) custom-call(f32[576,192]{1,0:T(8,128)S(1)} %get-tuple-element.84.hidden_ref, ...), custom_call_target="tpu_custom_call" | custom-call | flops 4400000000 | bytes 4033536 | tf_op jit(solution)/shard_map/pallas_call | solution.py:561
  27.9 0.1 collective-permute-start.3
  27.9 1.3 %collective-permute-start.4 = (bf16[32,384]{1,0:T(8,128)(2,1)S(1)}, bf16[32,384]{1,0:T(8,128)(2,1)S(1)}, u32[]{:S(2)}, u32[]{:S(2)}) collective-permute-start(bf16[32,384]{1,0:T(8,128)(2,1)S(1)} %get-tuple-element.93), channel_id=1, source_target_pairs={{1,0},{2,1},{3,2},{4,3},{5,4},{6,5},{7,6},{0,7},{9,8},{10,9},{11,1... | collective-permute-start | bytes 73736 | tf_op jit(solution)/shard_map/ppermute | solution.py:585
  29.3 0.1 collective-permute-start.5
  29.4 1.7 %shard_map.199 = (bf16[576,192]{1,0:T(8,128)(2,1)S(1)}, bf16[576,768]{1,0:T(8,128)(2,1)S(1)}, f32[144,864]{1,0:T(8,128)S(1)}) custom-call(bf16[288,384]{1,0:T(8,128)(2,1)S(1)} %bitcast.9, bf16[144,384]{1,0:T(8,128)(2,1)S(1)} %collective-permute-done.above_ref, bf16[18,384]{1,0:T(8,128)(2,1)S(1)} %collective-permute-done.1.side_ref, ...), custom_call_target="tpu_custom_call" | custom-call | flops 3300000000 | bytes 3343392 | tf_op jit(solution)/shard_map/pallas_call | solution.py:561
  31.1 0.8 collective-permute-done.4.side_ref
  31.8 0.7 collective-permute-done.5.corner_ref
  32.6 0.0 copy-start.19
  32.6 8.9 %shard_map.200 = (bf16[144,384]{1,0:T(8,128)(2,1)S(1)}, bf16[144,384]{1,0:T(8,128)(2,1)S(1)}, bf16[32,384]{1,0:T(8,128)(2,1)S(1)}, bf16[32,384]{1,0:T(8,128)(2,1...) custom-call(bf16[144,384]{1,0:T(8,128)(2,1)S(1)} %get-tuple-element., ...), custom_call_target="tpu_custom_call" | custom-call | flops 13200000000 | bytes 8409600 | tf_op jit(solution)/shard_map/pallas_call | solution.py:561
  41.5 1.1 collective-permute-start.6
  42.6 1.6 %collective-permute-start.7 = (bf16[32,384]{1,0:T(8,128)(2,1)S(1)}, bf16[32,384]{1,0:T(8,128)(2,1)S(1)}, u32[]{:S(2)}, u32[]{:S(2)}) collective-permute-start(bf16[32,384]{1,0:T(8,128)(2,1)S(1)} %get-tuple-element.107), channel_id=1, source_target_pairs={{7,0},{0,1},{1,2},{2,3},{3,4},{4,5},{5,6},{6,7},{15,8},{8,9},{9,10... | collective-permute-start | bytes 73736 | tf_op jit(solution)/shard_map/ppermute | solution.py:585
  44.3 0.4 collective-permute-start.8
  44.7 1.4 %shard_map.202 = (bf16[3456,128]{1,0:T(8,128)(2,1)S(1)}, bf16[208,128]{1,0:T(8,128)(2,1)S(1)}) custom-call(bf16[576,192]{1,0:T(8,128)(2,1)S(1)} %get-tuple-element.133.normed_ref, bf16[576,192]{1,0:T(8,128)(2,1)S(1)} %get-tuple-element.134.dq_ref, bf16[576,192]{1,0:T(8,128)(2,1)S(1)} %get-tuple-element.135.dk_ref, ...), custom_call_target="tpu_custom_call" | custom-call | flops 4400000000 | bytes 5200672 | tf_op jit(solution)/shard_map/pallas_call | solution.py:561
  46.1 2.4 %collective-permute-done.7.side_ref = bf16[32,384]{1,0:T(8,128)(2,1)S(1)} collective-permute-done((bf16[32,384]{1,0:T(8,128)(2,1)S(1)}, bf16[32,384]{1,0:T(8,128)(2,1)S(1)}, u32[]{:S(2)}, u32[]{:S(2)}) %collective-permute-start.7) | collective-permute-done | bytes 24608 | tf_op jit(solution)/shard_map/ppermute | solution.py:585
  48.5 4.4 %collective-permute-done.8.corner_ref = bf16[32,384]{1,0:T(8,128)(2,1)S(1)} collective-permute-done((bf16[32,384]{1,0:T(8,128)(2,1)S(1)}, bf16[32,384]{1,0:T(8,128)(2,1)S(1)}, u32[]{:S(2)}, u32[]{:S(2)}) %collective-permute-start.8) | collective-permute-done | bytes 24608 | tf_op jit(solution)/shard_map/ppermute | solution.py:586
  53.0 0.1 collective-permute-start.11
  53.0 0.0 copy-start.13
  53.1 2.2 %shard_map.201 = (bf16[576,192]{1,0:T(8,128)(2,1)S(1)}, f32[576,192]{1,0:T(8,128)S(1)}, bf16[576,192]{1,0:T(8,128)(2,1)S(1)}, bf16[576,768]{1,0:T(8,128)(2,1)S(1)}, f32[1,192]{1,0:T(1,128)S(1)}) custom-call(bf16[144,384]{1,0:T(8,128)(2,1)S(1)} %get-tuple-element.101.back_ref, bf16[144,384]{1,0:T(8,128)(2,1)S(1)} %collective-permute-done.6.above_ref, ...), custom_call_target="tpu_custom_call" | custom-call | flops 3300000000 | bytes 4955904 | tf_op jit(solution)/shard_map/pallas_call | solution.py:561
  55.3 3.6 %collective-permute-done.10 = bf16[32,384]{1,0:T(8,128)(2,1)S(1)} collective-permute-done((bf16[32,384]{1,0:T(8,128)(2,1)S(1)}, bf16[32,384]{1,0:T(8,128)(2,1)S(1)}, u32[]{:S(2)}, u32[]{:S(2)}) %collective-permute-start.10) | collective-permute-done | bytes 24608 | tf_op jit(solution)/shard_map/ppermute | solution.py:585
  58.9 3.6 %collective-permute-done.11 = bf16[32,384]{1,0:T(8,128)(2,1)S(1)} collective-permute-done((bf16[32,384]{1,0:T(8,128)(2,1)S(1)}, bf16[32,384]{1,0:T(8,128)(2,1)S(1)}, u32[]{:S(2)}, u32[]{:S(2)}) %collective-permute-start.11) | collective-permute-done | bytes 24608 | tf_op jit(solution)/shard_map/ppermute | solution.py:586
  62.5 6.1 %shard_map.203 = (bf16[288,384]{1,0:T(8,128)(2,1)}, bf16[3584,128]{1,0:T(8,128)(2,1)S(1)}, bf16[3584,128]{1,0:T(8,128)(2,1)S(1)}, bf16[512,128]{1,0:T(8,128)(2,1)S(1)}) custom-call(f32[576,192]{1,0:T(8,128)S(1)} %get-tuple-element.121.ghid_ref, bf16[576,192]{1,0:T(8,128)(2,1)S(1)} %get-tuple-element.122.g_ref, ...), custom_call_target="tpu_custom_call" | custom-call | flops 8800000000 | bytes 9033760 | tf_op jit(solution)/shard_map/pallas_call | solution.py:561
  68.6 0.1 collective-permute-start.12
  68.7 2.5 %collective-permute-done.12.other_ref = bf16[3584,128]{1,0:T(8,128)(2,1)S(1)} collective-permute-done((bf16[3584,128]{1,0:T(8,128)(2,1)S(1)}, bf16[3584,128]{1,0:T(8,128)(2,1)S(1)}, u32[]{:S(2)}, u32[]{:S(2)}) %collective-permute-start.12) | collective-permute-done | bytes 917536 | tf_op jit(solution)/shard_map/ppermute | solution.py:597
  71.1 0.2 shard_map.204
  71.4 18.4 %all_to_all.15.parts_ref = bf16[8,512,128]{2,1,0:T(8,128)(2,1)S(1)} all-to-all(bf16[8,512,128]{2,1,0:T(8,128)(2,1)S(1)} %shard_map.204), channel_id=1, replica_groups=mesh['lat'=16,'lon'=8] {'lon'}, dimensions={0} | all-to-all | bytes 2097152 | tf_op jit(solution)/shard_map/all_to_all | solution.py:600
  89.7 0.1 shard_map.205
  89.8 17.8 %all_to_all.16.parts_ref = bf16[8,448,128]{2,1,0:T(8,128)(2,1)S(1)} all-to-all(bf16[8,448,128]{2,1,0:T(8,128)(2,1)S(1)} %get-tuple-element.150), channel_id=1, replica_groups={{0,16,32,48,64,80,96,112},{8,24,40,56,72,88,104,120},{1,17,33,49,65,81,..., dimensions={0} | all-to-all | bytes 1835008 | tf_op jit(solution)/shard_map/all_to_all | solution.py:602
  107.7 0.1 shard_map.206
  107.8 17.8 %all_to_all.17.mine_ref = bf16[8,512,128]{2,1,0:T(8,128)(2,1)S(1)} all-to-all(bf16[8,512,128]{2,1,0:T(8,128)(2,1)S(1)} %shard_map.206), channel_id=1, replica_groups=mesh['lat'=16,'lon'=8] {'lon'}, dimensions={0} | all-to-all | bytes 2097152 | tf_op jit(solution)/shard_map/all_to_all | solution.py:604
  125.6 0.1 slice.28
  125.7 0.8 pad_maximum_fusion.1
  126.5 1.8 %collective-permute-done.13.other_ref = bf16[8,512,128]{2,1,0:T(8,128)(2,1)S(1)} collective-permute-done((bf16[8,512,128]{2,1,0:T(8,128)(2,1)S(1)}, bf16[8,512,128]{2,1,0:T(8,128)(2,1)S(1)}, u32[]{:S(2)}, u32[]{:S(2)}) %collective-permute-start.13) | collective-permute-done | bytes 1048608 | tf_op jit(solution)/shard_map/ppermute | solution.py:605
  128.2 2.1 %shard_map.207 = (f32[2,192,576]{2,1,0:T(8,128)}, f32[2,192,192]{2,1,0:T(8,128)}, f32[2,192,768]{2,1,0:T(8,128)}, f32[2,192,768]{2,1,0:T(8,128)}, f32[2,2,192]{2,1,0:T(2,128)}, /*index=5*/f32[12,1,3312]{2,1,0:T(1,128)}) custom-call(bf16[8,512,128]{2,1,0:T(8,128)(2,1)S(1)} %all_to_all.17.mine_ref, bf16[8,512,128]{2,1,0:T(8,128)(2,1)S(1)} %collective-permute-done.13.other_ref), custom_call_target="tpu_custom_call" | custom-call | flops 2200000000 | bytes 5798144 | tf_op jit(solution)/shard_map/pallas_call | solution.py:561
  (47 shorter events, 0.2 us)
Async XLA Ops:
  1.4 23.8 %collective-permute-start.1 = (bf16[18,384]{1,0:T(8,128)(2,1)S(1)}, bf16[18,384]{1,0:T(8,128)(2,1)S(1)}, u32[]{:S(2)}, u32[]{:S(2)}) collective-permute-start(bf16[18,384]{1,0:T(8,128)(2,1)S(1)} %reshape.49), channel_id=1, source_target_pairs={{1,0},{2,1},{3,2},{4,3},{5,4},{6,5},{7,6},{0,7},{9,8},{10,9},{11,1... | collective-permute-start | bytes 41480 | tf_op jit(solution)/shard_map/ppermute | solution.py:585
  5.7 19.6 %collective-permute-start.2 = (bf16[18,384]{1,0:T(8,128)(2,1)S(1)}, bf16[18,384]{1,0:T(8,128)(2,1)S(1)}, u32[]{:S(2)}, u32[]{:S(2)}) collective-permute-start(bf16[18,384]{1,0:T(8,128)(2,1)S(1)} %reshape.50), channel_id=1, source_target_pairs={{9,0},{10,1},{11,2},{12,3},{13,4},{14,5},{15,6},{8,7},{17,8},{18,9... | collective-permute-start | bytes 41480 | tf_op jit(solution)/shard_map/ppermute | solution.py:586
  10.8 14.4 %collective-permute-start = (bf16[144,384]{1,0:T(8,128)(2,1)S(1)}, bf16[144,384]{1,0:T(8,128)(2,1)S(1)}, u32[]{:S(2)}, u32[]{:S(2)}) collective-permute-start(bf16[144,384]{1,0:T(8,128)(2,1)S(1)} %bitcast.18), channel_id=1, source_target_pairs={{8,0},{9,1},{10,2},{11,3},{12,4},{13,5},{14,6},{15,7},{16,8},{17,9... | collective-permute-start | bytes 331784 | tf_op jit(solution)/shard_map/ppermute | solution.py:584
  12.9 1.0 copy-start.3
  13.9 0.9 copy-start.5
  14.8 0.9 copy-start.6
  15.8 0.9 copy-start.8
  16.7 0.7 copy-start.10
  17.4 1.0 copy-start.12
  18.4 0.9 copy-start.16
  19.3 0.9 copy-start.18
  20.2 5.0 %copy-start.1 = (bf16[2,192,768]{2,1,0:T(8,128)(2,1)S(1)}, bf16[2,192,768]{2,1,0:T(8,128)(2,1)}, u32[]{:S(2)}) copy-start(bf16[2,192,768]{2,1,0:T(8,128)(2,1)} %up_ref.5) | copy-start | bytes 1769476
  20.2 5.0 %copy-start.2 = (bf16[2,768,192]{1,2,0:T(8,128)(2,1)S(1)}, bf16[2,768,192]{1,2,0:T(8,128)(2,1)}, u32[]{:S(2)}) copy-start(bf16[2,768,192]{1,2,0:T(8,128)(2,1)} %param.20) | copy-start | bytes 1769476
  20.2 5.0 %copy-start.11 = (f32[2,2,192]{2,1,0:T(2,128)S(1)}, f32[2,2,192]{2,1,0:T(2,128)}, u32[]{:S(2)}) copy-start(f32[2,2,192]{2,1,0:T(2,128)} %gains_ref.9) | copy-start | bytes 9220
  20.2 5.1 %copy-start.20 = (bf16[64,288]{1,0:T(8,128)(2,1)S(1)}, bf16[64,288]{1,0:T(8,128)(2,1)}, u32[]{:S(2)}) copy-start(bf16[64,288]{1,0:T(8,128)(2,1)} %constant.17.clone.strips_ref) | copy-start | bytes 110596
  25.3 4.1 %copy-start = (bf16[6,48,384]{2,1,0:T(8,128)(2,1)S(1)}, bf16[6,48,384]{2,1,0:T(8,128)(2,1)}, u32[]{:S(2)}) copy-start(bf16[6,48,384]{2,1,0:T(8,128)(2,1)} %param.15) | copy-start | bytes 663556
  25.3 4.1 %copy-start.9 = (f32[2,1,6,3312]{3,1,2,0:T(1,128)S(1)}, f32[2,1,6,3312]{3,1,2,0:T(1,128)}, u32[]{:S(2)}) copy-start(f32[2,1,6,3312]{3,1,2,0:T(1,128)} %param.21) | copy-start | bytes 476932
  25.3 4.1 %copy-start.15 = (bf16[576,352]{1,0:T(8,128)(2,1)S(1)}, bf16[576,352]{1,0:T(8,128)(2,1)}, u32[]{:S(2)}) copy-start(bf16[576,352]{1,0:T(8,128)(2,1)} %constant.15.clone.pick_ref) | copy-start | bytes 1216516
  27.9 4.7 %collective-permute-start.3 = (bf16[144,384]{1,0:T(8,128)(2,1)S(1)}, bf16[144,384]{1,0:T(8,128)(2,1)S(1)}, u32[]{:S(2)}, u32[]{:S(2)}) collective-permute-start(bf16[144,384]{1,0:T(8,128)(2,1)S(1)} %get-tuple-element.92), channel_id=1, source_target_pairs={{8,0},{9,1},{10,2},{11,3},{12,4},{13,5},{14,6},{15,7},{16,8},{17,9... | collective-permute-start | bytes 331784 | tf_op jit(solution)/shard_map/ppermute | solution.py:584
  27.9 3.9 %collective-permute-start.4 = (bf16[32,384]{1,0:T(8,128)(2,1)S(1)}, bf16[32,384]{1,0:T(8,128)(2,1)S(1)}, u32[]{:S(2)}, u32[]{:S(2)}) collective-permute-start(bf16[32,384]{1,0:T(8,128)(2,1)S(1)} %get-tuple-element.93), channel_id=1, source_target_pairs={{1,0},{2,1},{3,2},{4,3},{5,4},{6,5},{7,6},{0,7},{9,8},{10,9},{11,1... | collective-permute-start | bytes 73736 | tf_op jit(solution)/shard_map/ppermute | solution.py:585
  29.3 3.3 %collective-permute-start.5 = (bf16[32,384]{1,0:T(8,128)(2,1)S(1)}, bf16[32,384]{1,0:T(8,128)(2,1)S(1)}, u32[]{:S(2)}, u32[]{:S(2)}) collective-permute-start(bf16[32,384]{1,0:T(8,128)(2,1)S(1)} %get-tuple-element.94), channel_id=1, source_target_pairs={{9,0},{10,1},{11,2},{12,3},{13,4},{14,5},{15,6},{8,7},{17,8},{18,9... | collective-permute-start | bytes 73736 | tf_op jit(solution)/shard_map/ppermute | solution.py:586
  29.4 3.2 %copy-start.4 = (bf16[2,192,576]{2,1,0:T(8,128)(2,1)S(1)}, bf16[2,192,576]{2,1,0:T(8,128)(2,1)}, u32[]{:S(2)}) copy-start(bf16[2,192,576]{2,1,0:T(8,128)(2,1)} %qkv_ref.5) | copy-start | bytes 1327108
  29.4 3.2 %copy-start.7 = (bf16[2,192,192]{2,1,0:T(8,128)(2,1)S(1)}, bf16[2,192,192]{2,1,0:T(8,128)(2,1)}, u32[]{:S(2)}) copy-start(bf16[2,192,192]{2,1,0:T(8,128)(2,1)} %out_ref.5) | copy-start | bytes 442372
  32.6 12.1 %copy-start.17 = (bf16[2,138,276]{2,1,0:T(8,128)(2,1)S(1)}, bf16[2,138,276]{2,1,0:T(8,128)(2,1)}, u32[]{:S(2)}) copy-start(bf16[2,138,276]{2,1,0:T(8,128)(2,1)} %constant.13.clone.tcols_ref) | copy-start | bytes 457060
  32.6 12.1 %copy-start.19 = (bf16[2,96,192]{2,1,0:T(8,128)(2,1)S(1)}, bf16[2,96,192]{2,1,0:T(8,128)(2,1)}, u32[]{:S(2)}) copy-start(bf16[2,96,192]{2,1,0:T(8,128)(2,1)} %constant.12.clone.trows_ref) | copy-start | bytes 221188
  41.5 11.5 %collective-permute-start.6 = (bf16[144,384]{1,0:T(8,128)(2,1)S(1)}, bf16[144,384]{1,0:T(8,128)(2,1)S(1)}, u32[]{:S(2)}, u32[]{:S(2)}) collective-permute-start(bf16[144,384]{1,0:T(8,128)(2,1)S(1)} %get-tuple-element.106), channel_id=1, source_target_pairs={{120,0},{121,1},{122,2},{123,3},{124,4},{125,5},{126,6},{127,7},{0... | collective-permute-start | bytes 331784 | tf_op jit(solution)/shard_map/ppermute | solution.py:584
  42.6 5.9 %collective-permute-start.7 = (bf16[32,384]{1,0:T(8,128)(2,1)S(1)}, bf16[32,384]{1,0:T(8,128)(2,1)S(1)}, u32[]{:S(2)}, u32[]{:S(2)}) collective-permute-start(bf16[32,384]{1,0:T(8,128)(2,1)S(1)} %get-tuple-element.107), channel_id=1, source_target_pairs={{7,0},{0,1},{1,2},{2,3},{3,4},{4,5},{5,6},{6,7},{15,8},{8,9},{9,10... | collective-permute-start | bytes 73736 | tf_op jit(solution)/shard_map/ppermute | solution.py:585
  44.3 8.7 %collective-permute-start.8 = (bf16[32,384]{1,0:T(8,128)(2,1)S(1)}, bf16[32,384]{1,0:T(8,128)(2,1)S(1)}, u32[]{:S(2)}, u32[]{:S(2)}) collective-permute-start(bf16[32,384]{1,0:T(8,128)(2,1)S(1)} %get-tuple-element.108), channel_id=1, source_target_pairs={{127,0},{120,1},{121,2},{122,3},{123,4},{124,5},{125,6},{126,7},{7... | collective-permute-start | bytes 73736 | tf_op jit(solution)/shard_map/ppermute | solution.py:586
  44.7 8.4 %copy-start.14 = (bf16[576,352]{1,0:T(8,128)(2,1)S(1)}, bf16[576,352]{1,0:T(8,128)(2,1)}, u32[]{:S(2)}) copy-start(bf16[576,352]{1,0:T(8,128)(2,1)} %constant.16.clone.returned_ref) | copy-start | bytes 1216516
  52.9 9.5 %collective-permute-start.9 = (bf16[144,384]{1,0:T(8,128)(2,1)S(1)}, bf16[144,384]{1,0:T(8,128)(2,1)S(1)}, u32[]{:S(2)}, u32[]{:S(2)}) collective-permute-start(bf16[144,384]{1,0:T(8,128)(2,1)S(1)} %get-tuple-element.114), channel_id=1, source_target_pairs={{120,0},{121,1},{122,2},{123,3},{124,4},{125,5},{126,6},{127,7},{0... | collective-permute-start | bytes 331784 | tf_op jit(solution)/shard_map/ppermute | solution.py:584
  52.9 5.9 %collective-permute-start.10 = (bf16[32,384]{1,0:T(8,128)(2,1)S(1)}, bf16[32,384]{1,0:T(8,128)(2,1)S(1)}, u32[]{:S(2)}, u32[]{:S(2)}) collective-permute-start(bf16[32,384]{1,0:T(8,128)(2,1)S(1)} %get-tuple-element.115), channel_id=1, source_target_pairs={{7,0},{0,1},{1,2},{2,3},{3,4},{4,5},{5,6},{6,7},{15,8},{8,9},{9,10... | collective-permute-start | bytes 73736 | tf_op jit(solution)/shard_map/ppermute | solution.py:585
  53.0 9.5 %collective-permute-start.11 = (bf16[32,384]{1,0:T(8,128)(2,1)S(1)}, bf16[32,384]{1,0:T(8,128)(2,1)S(1)}, u32[]{:S(2)}, u32[]{:S(2)}) collective-permute-start(bf16[32,384]{1,0:T(8,128)(2,1)S(1)} %get-tuple-element.116), channel_id=1, source_target_pairs={{127,0},{120,1},{121,2},{122,3},{123,4},{124,5},{125,6},{126,7},{7... | collective-permute-start | bytes 73736 | tf_op jit(solution)/shard_map/ppermute | solution.py:586
  53.0 9.4 %copy-start.13 = (bf16[576,288]{1,0:T(8,128)(2,1)S(1)}, bf16[576,288]{1,0:T(8,128)(2,1)}, u32[]{:S(2)}) copy-start(bf16[576,288]{1,0:T(8,128)(2,1)} %constant.14.clone.pick_ref) | copy-start | bytes 995332
  68.6 2.6 %collective-permute-start.12 = (bf16[3584,128]{1,0:T(8,128)(2,1)S(1)}, bf16[3584,128]{1,0:T(8,128)(2,1)S(1)}, u32[]{:S(2)}, u32[]{:S(2)}) collective-permute-start(bf16[3584,128]{1,0:T(8,128)(2,1)S(1)} %get-tuple-element.148), channel_id=1, source_target_pairs={{8,0},{0,8},{24,16},{16,24},{40,32},{32,40},{56,48},{48,56},{72,64... | collective-permute-start | bytes 2752520 | tf_op jit(solution)/shard_map/ppermute | solution.py:597
  125.6 2.7 %collective-permute-start.13 = (bf16[8,512,128]{2,1,0:T(8,128)(2,1)S(1)}, bf16[8,512,128]{2,1,0:T(8,128)(2,1)S(1)}, u32[]{:S(2)}, u32[]{:S(2)}) collective-permute-start(bf16[8,512,128]{2,1,0:T(8,128)(2,1)S(1)} %all_to_all.17.mine_ref), channel_id=1, source_target_pairs={{8,0},{0,8},{24,16},{16,24},{40,32},{32,40},{56,48},{48,56},{72,64... | collective-permute-start | bytes 3145736 | tf_op jit(solution)/shard_map/ppermute | solution.py:605

commit v4 on v3

--- a/solution.py
+++ b/solution.py
@@ -289,13 +289,25 @@
 
 
 def first_attention(
-    x_ref, gains_ref, qkv_ref, out_ref, table_ref, trows_ref, tcols_ref, pick_ref,
-    xw_ref, q_ref, k_ref, v_ref, probs_ref, ctx_ref, hidden_ref, bias_ref,
+    far_x, far_pick, far_gains, far_qkv, far_table, far_trows, far_tcols, far_out,
+    xw_ref, q_ref, k_ref, v_ref, probs_ref, ctx_ref, hidden_ref,
+    bias_ref, x_ref, pick_ref, gains_ref, qkv_ref, table_ref, trows_ref, tcols_ref, out_ref, sems,
 ):
+    pairs = [
+        (far_x, x_ref), (far_pick, pick_ref), (far_gains.at[0], gains_ref), (far_qkv.at[0], qkv_ref),
+        (far_table.at[pl.ds(0, HEADS)], table_ref), (far_trows, trows_ref), (far_tcols, tcols_ref), (far_out.at[0], out_ref),
+    ]
+    fetches = [pltpu.make_async_copy(far, near, sems.at[i]) for i, (far, near) in enumerate(pairs)]
+    for fetch in fetches:
+        fetch.start()
+    for fetch in fetches[:4]:
+        fetch.wait()
     x = gather_tokens(pick_ref[...], x_ref[...])
     xw_ref[...] = x.astype(BF16)
     hat, _ = normalize(x)
     project((hat * gains_ref[0:1, :]).astype(BF16), qkv_ref, q_ref, k_ref, v_ref)
+    for fetch in fetches[4:]:
+        fetch.wait()
     expand_table(table_ref, trows_ref, tcols_ref, bias_ref)
     attention(q_ref, k_ref, v_ref, bias_ref, probs_ref, ctx_ref, head_rows())
     branch = nn(ctx_ref[...], out_ref[...]).astype(BF16)
@@ -303,9 +315,13 @@
 
 
 def first_mlp(
-    hidden_ref, gains_ref, up_ref, down_ref, pick_ref, strips_ref,
-    expanded_ref, slope_ref, top_ref, bottom_ref, side_ref, corner_ref,
+    hidden_ref, cot_ref, gains_ref, up_ref, down_ref, pick_ref, strips_ref,
+    expanded_ref, slope_ref, bottom_ref, row_ref, side_ref, corner_ref,
 ):
+    row_ref[144:, :] = cot_ref[:144, :]
+    edges = nn(strips_ref[...], cot_ref[...]).astype(BF16)
+    side_ref[STRIP:, :] = edges[:STRIP]
+    corner_ref[STRIP:, :] = edges[STRIP:]
     hidden = hidden_ref[...]
     hat, _ = normalize(hidden)
     normed_mlp = (hat * gains_ref[1:2, :]).astype(BF16)
@@ -319,51 +335,44 @@
         slope_ref[:, cols] = (below + pre * density).astype(BF16)
         total = total + nt(expanded, down_ref[:, cols])
     grid = scatter_tokens(pick_ref[...], total.astype(BF16)).astype(BF16)
-    top_ref[...] = grid[:144]
+    row_ref[:144, :] = grid[:144]
     bottom_ref[...] = grid[144:]
     edges = nn(strips_ref[...], grid).astype(BF16)
-    side_ref[...] = edges[:STRIP]
-    corner_ref[...] = edges[STRIP:]
-
-
-def fill_source(source_ref, own, above_ref, side_ref, corner_ref):
+    side_ref[:STRIP, :] = edges[:STRIP]
+    corner_ref[:STRIP, :] = edges[STRIP:]
+
+
+def fill_source(source_ref, own, row_ref, side_ref, corner_ref, part):
     source_ref[0:144, :] = own
-    source_ref[144:288, :] = above_ref[...]
-    source_ref[288:SOURCE, :] = jnp.zeros((2 * STRIP, 2 * DIM), BF16)
-    source_ref[288 : 288 + side_ref.shape[0], :] = side_ref[...]
-    source_ref[288 + STRIP : 288 + STRIP + corner_ref.shape[0], :] = corner_ref[...]
-
-
-def put_source(own_ref, row_ref, side_ref, corner_ref, value):
+    source_ref[144:288, :] = row_ref[part * 144 : (part + 1) * 144, :]
+    source_ref[288 : 288 + STRIP, :] = side_ref[part * STRIP : (part + 1) * STRIP, :]
+    source_ref[288 + STRIP :, :] = corner_ref[part * STRIP : (part + 1) * STRIP, :]
+
+
+def put_source(own_ref, row_ref, side_ref, corner_ref, part, value):
     own_ref[...] = value[0:144]
-    row_ref[...] = value[144:288]
-    side_ref[...] = value[288 : 288 + STRIP]
-    corner_ref[...] = value[288 + STRIP :]
-
-
-def prepare_second(
-    cot_ref, above_ref, side_ref, corner_ref, down_ref, table_ref, trows_ref, tcols_ref, pick_ref,
-    g_ref, gact_ref, bias_ref, source_ref,
-):
-    fill_source(source_ref, cot_ref[144:288, :], above_ref, side_ref, corner_ref)
-    g_ref[...] = gather_tokens(pick_ref[...], source_ref[...]).astype(BF16)
-    for j in range(3):
-        cols = slice(j * 256, (j + 1) * 256)
-        gact_ref[:, cols] = nn(g_ref[...], down_ref[:, cols]).astype(BF16)
+    row_ref[part * 144 : (part + 1) * 144, :] = value[144:288]
+    side_ref[part * STRIP : (part + 1) * STRIP, :] = value[288 : 288 + STRIP]
+    corner_ref[part * STRIP : (part + 1) * STRIP, :] = value[288 + STRIP :]
+
+
+def second_bias(table_ref, trows_ref, tcols_ref, bias_ref):
     expand_table(table_ref, trows_ref, tcols_ref, bias_ref)
     add_mask(bias_ref, (lax.axis_index("lat") == lax.axis_size("lat") - 1).astype(F32))
 
 
 def second_both(
-    own_ref, above_ref, side_ref, corner_ref, g_ref, gact_ref, bias_ref,
+    own_ref, row_ref, side_ref, corner_ref, cot_ref, bias_ref,
     gains_ref, qkv_ref, out_ref, up_ref, down_ref, pick_ref,
-    y_own_ref, y_row_ref, y_side_ref, y_corner_ref, back_own_ref, back_row_ref, back_side_ref, back_corner_ref,
-    normed_ref, dq_ref, dk_ref, dv_ref, ctx_ref, gbranch_ref, normed_mlp_ref, gpre_ref, expanded_ref, grad_ref, gain_grad_ref,
+    back_own_ref, y_own_ref, sent_row_ref, sent_side_ref, sent_corner_ref,
+    g_ref, normed_ref, dq_ref, dk_ref, dv_ref, ctx_ref, gbranch_ref, normed_mlp_ref, gpre_ref, expanded_ref, grad_ref, gain_grad_ref,
     source_ref, x_ref, q_ref, k_ref, v_ref, probs_ref, gctx_ref,
 ):
     masks = head_rows()
-    fill_source(source_ref, own_ref[...], above_ref, side_ref, corner_ref)
+    fill_source(source_ref, own_ref[...], row_ref, side_ref, corner_ref, 0)
     x_ref[...] = gather_tokens(pick_ref[...], source_ref[...])
+    fill_source(source_ref, cot_ref[144:288, :], row_ref, side_ref, corner_ref, 1)
+    g_ref[...] = gather_tokens(pick_ref[...], source_ref[...]).astype(BF16)
     hat, _ = normalize(x_ref[...])
     project((hat * gains_ref[0:1, :]).astype(BF16), qkv_ref, q_ref, k_ref, v_ref)
     attention(q_ref, k_ref, v_ref, bias_ref, probs_ref, ctx_ref, masks)
@@ -381,11 +390,12 @@
         expanded = (pre * below).astype(BF16)
         expanded_ref[:, cols] = expanded
         total = total + nt(expanded, down_ref[:, cols])
-        gpre = ((below + pre * density) * gact_ref[:, cols].astype(F32)).astype(BF16)
+        gact = nn(g_ref[...], down_ref[:, cols]).astype(BF16).astype(F32)
+        gpre = ((below + pre * density) * gact).astype(BF16)
         gpre_ref[:, cols] = gpre
         gnormed = gnormed + nt(gpre, up_ref[:, cols])
     y = scatter_tokens(pick_ref[...], total.astype(BF16)).astype(BF16)
-    put_source(y_own_ref, y_row_ref, y_side_ref, y_corner_ref, y)
+    put_source(y_own_ref, sent_row_ref, sent_side_ref, sent_corner_ref, 1, y)
     gnormed = gnormed.astype(BF16).astype(F32)
     gain_grad_ref[1:2, :] = jnp.sum(gnormed * hat_mlp, axis=0, keepdims=True)
     ghid = g_ref[...].astype(F32) + norm_backward(gnormed, gains_ref[1:2, :], hat_mlp, inv_mlp)
@@ -395,7 +405,7 @@
     )
     gain_grad_ref[0:1, :] = gain_grad
     back = scatter_tokens(pick_ref[...], gblock.astype(BF16)).astype(BF16)
-    put_source(back_own_ref, back_row_ref, back_side_ref, back_corner_ref, back)
+    put_source(back_own_ref, sent_row_ref, sent_side_ref, sent_corner_ref, 0, back)
     normed_ref[...] = normed
     gbranch_ref[...] = gbranch
 
@@ -412,10 +422,10 @@
 
 
 def first_mlp_back(
-    back_ref, above_ref, side_ref, corner_ref, hidden_ref, slope_ref, gains_ref, up_ref, down_ref, returned_ref,
+    back_ref, row_ref, side_ref, corner_ref, hidden_ref, slope_ref, gains_ref, up_ref, down_ref, returned_ref,
     g_ref, ghid_ref, normed_mlp_ref, gpre_ref, gain_grad_ref, source_ref,
 ):
-    fill_source(source_ref, back_ref[...], above_ref, side_ref, corner_ref)
+    fill_source(source_ref, back_ref[...], row_ref, side_ref, corner_ref, 0)
     g32 = gather_tokens(returned_ref[...], source_ref[...])
     g = g32.astype(BF16)
     g_ref[...] = g
@@ -618,17 +628,12 @@
     strips = jnp.asarray(strip_picker(), BF16)
     weights = (norm_gains, qkv_weight, out_weight, up_weight, jnp.swapaxes(down_weight, 1, 2))
     tok, src, hid = (TOKENS, DIM), (SOURCE, 2 * DIM), (TOKENS, UNITS)
-    strip_shapes = [(144, 2 * DIM), (144, 2 * DIM), (STRIP, 2 * DIM), (STRIP, 2 * DIM)]
     probs = (WINDOWS, WIN_TOK, QLANES)
 
     def table_spec(index):
         return pl.BlockSpec((HEADS, 1, TABLE), lambda i: (index, 0, 0))
 
     bias_table = bias_table.reshape(2 * HEADS, 1, TABLE)
-    cot_side = cotangent[3:, :6].reshape(18, 2 * DIM)
-    cot_corner = cotangent[:3, :6].reshape(18, 2 * DIM)
-    cot_strips = exchange(cot[:144], cot_side, cot_corner, sizes, 1)
-
     gains, qkv, out, up, down = weights
     wide_tok, wide_hid = (tok, BF16), (hid, BF16)
     bias = (WIN_TOK, QLANES)
@@ -644,43 +649,43 @@
                 specs.append(whole(a))
         return specs
 
-    operands = [x, gains, qkv, out, bias_table, trows, tcols, pick_grid]
+    operands = [x, pick_grid, gains, qkv, bias_table, trows, tcols, out]
     outs = [wide_tok] * 4 + [(probs, BF16), wide_tok, (tok, F32)]
-    results = call(first_attention, operands, specs_for(operands, 0), outs, [vmem(bias, F32)], 7, mebibytes=14)
+    scratch = [vmem(bias, F32), vmem(x.shape, BF16), vmem(pick_grid.shape, BF16), vmem((2, DIM), F32), vmem((DIM, 3 * DIM), BF16)]
+    scratch += [vmem((HEADS, 1, TABLE), F32), vmem(trows.shape, BF16), vmem(tcols.shape, BF16), vmem((DIM, DIM), BF16)]
+    scratch += [pltpu.SemaphoreType.DMA((8,))]
+    operands = [pltpu.with_memory_space_constraint(a, pltpu.HBM) for a in operands]
+    specs = [in_place()] * 8
+    results = call(first_attention, operands, specs, outs, scratch, 7, mebibytes=14)
     xw, q, k, v, probs_first, ctx, hidden = results
-    hidden, cot_strips = lax.optimization_barrier((hidden, cot_strips))
-
-    operands = [hidden, gains, up, down, pick_grid, strips]
-    outs = [wide_hid, wide_hid] + [(shape, BF16) for shape in strip_shapes]
+
+    operands = [hidden, cot, gains, up, down, pick_grid, strips]
+    strip_outs = [((288, 2 * DIM), BF16), ((2 * STRIP, 2 * DIM), BF16), ((2 * STRIP, 2 * DIM), BF16)]
+    outs = [wide_hid, wide_hid, ((144, 2 * DIM), BF16)] + strip_outs
     results = call(first_mlp, operands, specs_for(operands, 0), outs, (), 4, mebibytes=14)
-    expanded, slope, top, bottom, side, corner = results
-    (top, side, corner), cot_strips = lax.optimization_barrier(((top, side, corner), cot_strips))
-
-    own_strips = exchange(top, side, corner, sizes, 1)
-    operands = [cot, *cot_strips, down, bias_table, trows, tcols, pick_shift]
-    outs = [wide_tok, wide_hid, (bias, F32)]
-    g, gact, bias_last = call(
-        prepare_second, operands, specs_for(operands, 1), outs, [vmem(src, BF16)], 3, mebibytes=14
-    )
-
-    operands = [bottom, *own_strips, g, gact, bias_last, *weights, pick_shift]
-    outs = [(shape, BF16) for shape in strip_shapes] * 2 + [wide_tok] * 7 + [wide_hid] * 2 + [(bias, F32), ((2, DIM), F32)]
+    expanded, slope, bottom, *sent = results
+    sent, bias_table = lax.optimization_barrier((sent, bias_table))
+
+    arrived = exchange(*sent, sizes, 1)
+    operands = [bias_table, trows, tcols]
+    [bias_last] = call(second_bias, operands, specs_for(operands, 1), [(bias, F32)], (), 2, mebibytes=14)
+
+    operands = [bottom, *arrived, cot, bias_last, *weights, pick_shift]
+    outs = [((144, 2 * DIM), BF16)] * 2 + strip_outs + [wide_tok] * 8 + [wide_hid] * 2 + [(bias, F32), ((2, DIM), F32)]
     scratch = [vmem(src, BF16), vmem(tok, F32)] + [vmem(tok, BF16)] * 3 + [vmem(probs, BF16), vmem(tok, BF16)]
     results = call(second_both, operands, specs_for(operands, 1), outs, scratch, 12, mebibytes=14)
-    y_strips, back_strips, terms, last_gain = results[:4], results[4:8], results[8:18], results[18]
-
-    back = exchange(*back_strips[1:], sizes, -1)
+    back_own, y_own, sent, terms, last_gain = results[0], results[1], results[2:5], results[5:16], results[16]
+
+    arrived = exchange(*sent, sizes, -1)
+    g, *terms = terms
     operands = [*terms, g, trows, tcols]
     outs = [((WBLOCK, 128), BF16), ((TROWS, 128), BF16)]
     last_wbuf, last_table = call(second_weights, operands, specs_for(operands, 1), outs, (), 4, mebibytes=14)
-    y_strips, back = lax.optimization_barrier((y_strips, back))
-    y_moved = exchange(*y_strips[1:], sizes, -1)
-
-    operands = [back_strips[0], *back, hidden, slope, gains, up, down, pick_back]
+
+    operands = [back_own, *arrived, hidden, slope, gains, up, down, pick_back]
     outs = [wide_tok, (tok, F32), wide_tok, wide_hid, ((1, DIM), F32)]
     results = call(first_mlp_back, operands, specs_for(operands, 0), outs, [vmem(src, BF16)], 3, mebibytes=14)
     g, ghid, normed_mlp, gpre, mlp_gain = results
-    ghid, y_moved = lax.optimization_barrier((ghid, y_moved))
 
     operands = [ghid, g, normed_mlp, gpre, mlp_gain, xw, q, k, v, probs_first, ctx, expanded, gains, qkv, out]
     operands += [trows, tcols, pick_grid, last_wbuf, last_gain, last_table]
@@ -694,9 +699,9 @@
         first_attention_back, operands, specs, outs, scratch, 8, out_specs, 14
     )
 
-    y_rows, y_side, y_corner = y_moved
-    rows = jnp.concatenate([y_rows, y_strips[0]]).reshape(ROWS, COLS, 2 * DIM)
-    edge = jnp.concatenate([y_corner[:18].reshape(3, 6, 2 * DIM), y_side[:18].reshape(3, 6, 2 * DIM)])
+    y_rows, y_side, y_corner = arrived
+    rows = jnp.concatenate([y_rows[144:], y_own]).reshape(ROWS, COLS, 2 * DIM)
+    edge = jnp.concatenate([a[STRIP : STRIP + 18].reshape(3, 6, 2 * DIM) for a in (y_corner, y_side)])
     output = jnp.concatenate([edge, rows[:, 6:]], axis=1)
 
     grad_qkv, grad_out, grad_up, grad_down, grad_gains, grad_table = sum_over_devices(mine, theirs, tables, sizes)

time: 132 us -> 115 us (0.87)
  local copies, waits for them, and re-layouts: 9.17 us -> 0.18 us
  starting transfers between devices: 15.4 us -> 9.8 us
  waiting for transfers between devices: 19.7 us -> 14.7 us
  Pallas kernels: 30.4 us -> 32 us
    unnamed x42 -> x26, local copies, waits for them, and re-layouts: 7.4 us -> 0.07 us
    ppermute x4 -> x2, waiting for transfers between devices: 6.8 us -> 0.61 us  [exchange(): side = lax.ppermute(side, both, neighbour(sizes, (0, step)))]
    ppermute x4 -> x2, starting transfers between devices: 4.76 us -> 0.08 us  [exchange(): corner = lax.ppermute(corner, both, neighbour(sizes, (step, step)))]
    ppermute x4 -> x2, starting transfers between devices: 7.25 us -> 3.65 us  [exchange(): side = lax.ppermute(side, both, neighbour(sizes, (0, step)))]
    ppermute x4 -> x2, starting transfers between devices: 3.31 us -> 5.98 us  [exchange(): rows = lax.ppermute(rows, both, neighbour(sizes, (step, 0)))]
    slice x4 -> x3, local copies, waits for them, and re-layouts: 1.66 us -> 0.02 us  [the longest x1 0.01 us: on_device(): rows = jnp.concatenate([y_rows[144:], y_own]).reshape(ROWS, COLS, 2 * DIM)]
    pallas_call x11, Pallas kernels: 30.4 us -> 32 us  [call(): pl.pallas_call(kernel, grid=(1,), out_shape=shapes, in_specs=specs, out_s...]
    ppermute x4 -> x2, waiting for transfers between devices: 8.68 us -> 9.89 us  [exchange(): corner = lax.ppermute(corner, both, neighbour(sizes, (step, step)))]
  transfers between devices with their start and end apart: 14 -> 8, of which waited for: 8 -> 5; matrix products, arithmetic and copies ran while one was open for 1% -> 1% of each run, Pallas kernels for 8% -> 2%
where the time goes in v4:
time: 115 us; the launch traced here: 113 us
  blocking collectives  55 us (48%)
  Pallas kernels  32 us (28%)
  waiting for transfers between devices  14.7 us (13%)
  starting transfers between devices  9.8 us (9%)
    pallas_call x11, Pallas kernels, call(): pl.pallas_call(kernel, grid=(1,), out_shape=shapes, in_specs=specs, out_s...  32 us
    all_to_all x1, blocking collectives, sum_over_devices(): parts = lax.all_to_all(sent, 'lon', 0, 0)  19.1 us
    all_to_all x1, blocking collectives, sum_over_devices(): parts = lax.all_to_all(spread, 'lat', 0, 0, axis_index_groups=groups)  18 us
    all_to_all x1, blocking collectives, sum_over_devices(): half = lax.all_to_all(spread, 'lon', 0, 0)  17.8 us
    ppermute x2, waiting for transfers between devices, exchange(): corner = lax.ppermute(corner, both, neighbour(sizes, (step, step)))  9.89 us
    ppermute x2, starting transfers between devices, exchange(): rows = lax.ppermute(rows, both, neighbour(sizes, (step, 0)))  5.98 us
    ppermute x2, starting transfers between devices, exchange(): side = lax.ppermute(side, both, neighbour(sizes, (0, step)))  3.65 us
    ppermute x1, waiting for transfers between devices, sum_over_devices(): other = lax.ppermute(theirs, 'lat', pairs)  2.46 us
  transfers between devices with their start and end apart: 8, of which 5 were waited for; matrix products, arithmetic and copies ran while one was open for 1% of the time, Pallas kernels for 2%

profile of v4, /device:TPU:0, one launch (start us, length us, event | category | flops | bytes accessed | tf_op | source)
XLA Modules:
  0.0 113.3 jit_solution(12086982707099609106)
XLA Ops:
  0.7 0.0 copy-start.7
  0.7 0.0 copy-start.12
  0.7 6.7 %shard_map.197 = (bf16[576,192]{1,0:T(8,128)(2,1)S(1)}, bf16[576,192]{1,0:T(8,128)(2,1)S(1)}, bf16[576,192]{1,0:T(8,128)(2,1)S(1)}, bf16[576,192]{1,0:T(8,128)(2...) custom-call(bf16[288,384]{1,0:T(8,128)(2,1)} %bitcast.16, ...), custom_call_target="tpu_custom_call" | custom-call | flops 7699999744 | bytes 4074528 | tf_op jit(solution)/shard_map/pallas_call | solution.py:571
  7.4 0.0 copy-done
  7.4 0.0 copy-done.1
  7.4 0.0 copy-done.3
  7.4 0.0 copy-done.6
  7.4 0.0 copy-done.7
  7.4 0.0 copy-done.12
  7.5 0.0 copy-start.5
  7.5 0.0 copy-start.10
  7.5 0.0 copy-start.11
  7.5 2.6 %shard_map.198 = (bf16[576,768]{1,0:T(8,128)(2,1)S(1)}, bf16[576,768]{1,0:T(8,128)(2,1)S(1)}, bf16[144,384]{1,0:T(8,128)(2,1)S(1)}, bf16[288,384]{1,0:T(8,128)(2...) custom-call(f32[576,192]{1,0:T(8,128)S(1)} %get-tuple-element.61.hidden_ref, ...), custom_call_target="tpu_custom_call" | custom-call | flops 4400000000 | bytes 4414464 | tf_op jit(solution)/shard_map/pallas_call | solution.py:571
  10.1 0.0 copy-start.2
  10.1 0.0 copy-start.4
  10.1 0.0 copy-start.9
  10.1 5.9 %collective-permute-start = (bf16[288,384]{1,0:T(8,128)(2,1)S(1)}, bf16[288,384]{1,0:T(8,128)(2,1)S(1)}, u32[]{:S(2)}, u32[]{:S(2)}) collective-permute-start(bf16[288,384]{1,0:T(8,128)(2,1)S(1)} %get-tuple-element.66), channel_id=1, source_target_pairs={{8,0},{9,1},{10,2},{11,3},{12,4},{13,5},{14,6},{15,7},{16,8},{17,9... | collective-permute-start | bytes 663560 | tf_op jit(solution)/shard_map/ppermute | solution.py:594
  16.0 3.2 %collective-permute-start.1 = (bf16[64,384]{1,0:T(8,128)(2,1)S(1)}, bf16[64,384]{1,0:T(8,128)(2,1)S(1)}, u32[]{:S(2)}, u32[]{:S(2)}) collective-permute-start(bf16[64,384]{1,0:T(8,128)(2,1)S(1)} %get-tuple-element.67), channel_id=1, source_target_pairs={{1,0},{2,1},{3,2},{4,3},{5,4},{6,5},{7,6},{0,7},{9,8},{10,9},{11,1... | collective-permute-start | bytes 147464 | tf_op jit(solution)/shard_map/ppermute | solution.py:595
  19.2 0.0 collective-permute-start.2
  19.2 0.0 copy-done.5
  19.2 1.1 %shard_map.199.bias_ref = f32[144,864]{1,0:T(8,128)S(1)} custom-call(f32[12,1,3312]{2,1,0:T(1,128)S(1)} %bitcast.14, bf16[2,96,192]{2,1,0:T(8,128)(2,1)S(1)} %copy-done.11, bf16[2,138,276]{2,1,0:T(8,128)(2,1)S(1)} %copy-done.10), custom_call_target="tpu_custom_call" | custom-call | flops 2200000000 | bytes 882720 | tf_op jit(solution)/shard_map/pallas_call | solution.py:571
  20.4 0.6 collective-permute-done.1.side_ref
  21.0 1.7 %collective-permute-done.2.corner_ref = bf16[64,384]{1,0:T(8,128)(2,1)S(1)} collective-permute-done((bf16[64,384]{1,0:T(8,128)(2,1)S(1)}, bf16[64,384]{1,0:T(8,128)(2,1)S(1)}, u32[]{:S(2)}, u32[]{:S(2)}) %collective-permute-start.2) | collective-permute-done | bytes 49184 | tf_op jit(solution)/shard_map/ppermute | solution.py:596
  22.7 0.0 collective-permute-done.row_ref
  22.7 0.0 copy-done.4
  22.8 9.3 %shard_map.200 = (bf16[144,384]{1,0:T(8,128)(2,1)S(1)}, bf16[144,384]{1,0:T(8,128)(2,1)S(1)}, bf16[288,384]{1,0:T(8,128)(2,1)S(1)}, bf16[64,384]{1,0:T(8,128)(2,...) custom-call(bf16[144,384]{1,0:T(8,128)(2,1)S(1)} %get-tuple-element., ...), custom_call_target="tpu_custom_call" | custom-call | flops 13200000000 | bytes 7905792 | tf_op jit(solution)/shard_map/pallas_call | solution.py:571
  32.1 0.1 collective-permute-start.5
  32.2 0.1 collective-permute-start.3
  32.3 0.4 collective-permute-start.4
  32.7 1.4 %shard_map.202 = (bf16[3456,128]{1,0:T(8,128)(2,1)S(1)}, bf16[208,128]{1,0:T(8,128)(2,1)S(1)}) custom-call(bf16[576,192]{1,0:T(8,128)(2,1)S(1)} %get-tuple-element.88.normed_ref, bf16[576,192]{1,0:T(8,128)(2,1)S(1)} %get-tuple-element.89.dq_ref, bf16[576,192]{1,0:T(8,128)(2,1)S(1)} %get-tuple-element.90.dk_ref, ...), custom_call_target="tpu_custom_call" | custom-call | flops 4400000000 | bytes 5200672 | tf_op jit(solution)/shard_map/pallas_call | solution.py:571
  34.1 8.2 %collective-permute-done.3.corner_ref = bf16[64,384]{1,0:T(8,128)(2,1)S(1)} collective-permute-done((bf16[64,384]{1,0:T(8,128)(2,1)S(1)}, bf16[64,384]{1,0:T(8,128)(2,1)S(1)}, u32[]{:S(2)}, u32[]{:S(2)}) %collective-permute-start.3) | collective-permute-done | bytes 49184 | tf_op jit(solution)/shard_map/ppermute | solution.py:596
  42.3 0.0 collective-permute-done.4.side_ref
  42.3 0.0 collective-permute-done.5.row_ref
  42.3 2.2 %shard_map.201 = (bf16[576,192]{1,0:T(8,128)(2,1)S(1)}, f32[576,192]{1,0:T(8,128)S(1)}, bf16[576,192]{1,0:T(8,128)(2,1)S(1)}, bf16[576,768]{1,0:T(8,128)(2,1)S(1)}, f32[1,192]{1,0:T(1,128)S(1)}) custom-call(bf16[144,384]{1,0:T(8,128)(2,1)S(1)} %get-tuple-element.74.back_ref, bf16[288,384]{1,0:T(8,128)(2,1)S(1)} %collective-permute-done.5.row_ref, ...), custom_call_target="tpu_custom_call" | custom-call | flops 3300000000 | bytes 5115648 | tf_op jit(solution)/shard_map/pallas_call | solution.py:571
  44.5 6.1 %shard_map.203 = (bf16[288,384]{1,0:T(8,128)(2,1)}, bf16[3584,128]{1,0:T(8,128)(2,1)S(1)}, bf16[3584,128]{1,0:T(8,128)(2,1)S(1)}, bf16[512,128]{1,0:T(8,128)(2,1)S(1)}) custom-call(f32[576,192]{1,0:T(8,128)S(1)} %get-tuple-element.76.ghid_ref, bf16[576,192]{1,0:T(8,128)(2,1)S(1)} %get-tuple-element.77.g_ref, ...), custom_call_target="tpu_custom_call" | custom-call | flops 8800000000 | bytes 9033760 | tf_op jit(solution)/shard_map/pallas_call | solution.py:571
  50.6 0.1 collective-permute-start.6
  50.7 2.5 %collective-permute-done.6.other_ref = bf16[3584,128]{1,0:T(8,128)(2,1)S(1)} collective-permute-done((bf16[3584,128]{1,0:T(8,128)(2,1)S(1)}, bf16[3584,128]{1,0:T(8,128)(2,1)S(1)}, u32[]{:S(2)}, u32[]{:S(2)}) %collective-permute-start.6) | collective-permute-done | bytes 917536 | tf_op jit(solution)/shard_map/ppermute | solution.py:607
  53.1 0.2 shard_map.204
  53.4 19.1 %all_to_all.15.parts_ref = bf16[8,512,128]{2,1,0:T(8,128)(2,1)S(1)} all-to-all(bf16[8,512,128]{2,1,0:T(8,128)(2,1)S(1)} %shard_map.204), channel_id=1, replica_groups=mesh['lat'=16,'lon'=8] {'lon'}, dimensions={0} | all-to-all | bytes 2097152 | tf_op jit(solution)/shard_map/all_to_all | solution.py:610
  72.5 0.1 shard_map.205
  72.6 18.0 %all_to_all.16.parts_ref = bf16[8,448,128]{2,1,0:T(8,128)(2,1)S(1)} all-to-all(bf16[8,448,128]{2,1,0:T(8,128)(2,1)S(1)} %get-tuple-element.106), channel_id=1, replica_groups={{0,16,32,48,64,80,96,112},{8,24,40,56,72,88,104,120},{1,17,33,49,65,81,..., dimensions={0} | all-to-all | bytes 1835008 | tf_op jit(solution)/shard_map/all_to_all | solution.py:612
  90.7 0.1 shard_map.206
  90.8 17.8 %all_to_all.17.mine_ref = bf16[8,512,128]{2,1,0:T(8,128)(2,1)S(1)} all-to-all(bf16[8,512,128]{2,1,0:T(8,128)(2,1)S(1)} %shard_map.206), channel_id=1, replica_groups=mesh['lat'=16,'lon'=8] {'lon'}, dimensions={0} | all-to-all | bytes 2097152 | tf_op jit(solution)/shard_map/all_to_all | solution.py:614
  108.6 0.0 collective-permute-start.7
  108.7 0.1 slice.19
  108.8 0.8 pad_maximum_fusion.1
  109.5 1.7 %collective-permute-done.7.other_ref = bf16[8,512,128]{2,1,0:T(8,128)(2,1)S(1)} collective-permute-done((bf16[8,512,128]{2,1,0:T(8,128)(2,1)S(1)}, bf16[8,512,128]{2,1,0:T(8,128)(2,1)S(1)}, u32[]{:S(2)}, u32[]{:S(2)}) %collective-permute-start.7) | collective-permute-done | bytes 1048608 | tf_op jit(solution)/shard_map/ppermute | solution.py:615
  111.3 2.1 %shard_map.207 = (f32[2,192,576]{2,1,0:T(8,128)}, f32[2,192,192]{2,1,0:T(8,128)}, f32[2,192,768]{2,1,0:T(8,128)}, f32[2,192,768]{2,1,0:T(8,128)}, f32[2,2,192]{2,1,0:T(2,128)}, /*index=5*/f32[12,1,3312]{2,1,0:T(1,128)}) custom-call(bf16[8,512,128]{2,1,0:T(8,128)(2,1)S(1)} %all_to_all.17.mine_ref, bf16[8,512,128]{2,1,0:T(8,128)(2,1)S(1)} %collective-permute-done.7.other_ref), custom_call_target="tpu_custom_call" | custom-call | flops 2200000000 | bytes 5798144 | tf_op jit(solution)/shard_map/pallas_call | solution.py:571
  (16 shorter events, 0.1 us)
Async XLA Ops:
  0.6 6.8 %copy-start = (bf16[2,192,768]{2,1,0:T(8,128)(2,1)S(1)}, bf16[2,192,768]{2,1,0:T(8,128)(2,1)}, u32[]{:S(2)}) copy-start(bf16[2,192,768]{2,1,0:T(8,128)(2,1)} %up_ref.5) | copy-start | bytes 1769476
  0.6 6.8 %copy-start.1 = (bf16[2,768,192]{1,2,0:T(8,128)(2,1)S(1)}, bf16[2,768,192]{1,2,0:T(8,128)(2,1)}, u32[]{:S(2)}) copy-start(bf16[2,768,192]{1,2,0:T(8,128)(2,1)} %param.20) | copy-start | bytes 1769476
  0.7 6.8 %copy-start.3 = (bf16[6,48,384]{2,1,0:T(8,128)(2,1)S(1)}, bf16[6,48,384]{2,1,0:T(8,128)(2,1)}, u32[]{:S(2)}) copy-start(bf16[6,48,384]{2,1,0:T(8,128)(2,1)} %param.15) | copy-start | bytes 663556
  0.7 6.8 %copy-start.6 = (f32[2,2,192]{2,1,0:T(2,128)S(1)}, f32[2,2,192]{2,1,0:T(2,128)}, u32[]{:S(2)}) copy-start(f32[2,2,192]{2,1,0:T(2,128)} %gains_ref.7) | copy-start | bytes 9220
  0.7 6.8 %copy-start.7 = (bf16[576,288]{1,0:T(8,128)(2,1)S(1)}, bf16[576,288]{1,0:T(8,128)(2,1)}, u32[]{:S(2)}) copy-start(bf16[576,288]{1,0:T(8,128)(2,1)} %constant.14.clone.far_pick.pick_ref) | copy-start | bytes 995332
  0.7 6.8 %copy-start.12 = (bf16[64,288]{1,0:T(8,128)(2,1)S(1)}, bf16[64,288]{1,0:T(8,128)(2,1)}, u32[]{:S(2)}) copy-start(bf16[64,288]{1,0:T(8,128)(2,1)} %constant.17.clone.strips_ref) | copy-start | bytes 110596
  7.5 11.8 %copy-start.5 = (f32[2,1,6,3312]{3,1,2,0:T(1,128)S(1)}, f32[2,1,6,3312]{3,1,2,0:T(1,128)}, u32[]{:S(2)}) copy-start(f32[2,1,6,3312]{3,1,2,0:T(1,128)} %param.21) | copy-start | bytes 476932
  7.5 11.8 %copy-start.10 = (bf16[2,138,276]{2,1,0:T(8,128)(2,1)S(1)}, bf16[2,138,276]{2,1,0:T(8,128)(2,1)}, u32[]{:S(2)}) copy-start(bf16[2,138,276]{2,1,0:T(8,128)(2,1)} %constant.13.clone.far_tcols.tcols_ref) | copy-start | bytes 457060
  7.5 11.8 %copy-start.11 = (bf16[2,96,192]{2,1,0:T(8,128)(2,1)S(1)}, bf16[2,96,192]{2,1,0:T(8,128)(2,1)}, u32[]{:S(2)}) copy-start(bf16[2,96,192]{2,1,0:T(8,128)(2,1)} %constant.12.clone.far_trows.trows_ref) | copy-start | bytes 221188
  10.1 12.7 %copy-start.2 = (bf16[2,192,576]{2,1,0:T(8,128)(2,1)S(1)}, bf16[2,192,576]{2,1,0:T(8,128)(2,1)}, u32[]{:S(2)}) copy-start(bf16[2,192,576]{2,1,0:T(8,128)(2,1)} %qkv_ref.3) | copy-start | bytes 1327108
  10.1 12.7 %copy-start.4 = (bf16[2,192,192]{2,1,0:T(8,128)(2,1)S(1)}, bf16[2,192,192]{2,1,0:T(8,128)(2,1)}, u32[]{:S(2)}) copy-start(bf16[2,192,192]{2,1,0:T(8,128)(2,1)} %out_ref.3) | copy-start | bytes 442372
  10.1 12.7 %copy-start.9 = (bf16[576,352]{1,0:T(8,128)(2,1)S(1)}, bf16[576,352]{1,0:T(8,128)(2,1)}, u32[]{:S(2)}) copy-start(bf16[576,352]{1,0:T(8,128)(2,1)} %constant.15.clone.pick_ref) | copy-start | bytes 1216516
  10.1 12.6 %collective-permute-start = (bf16[288,384]{1,0:T(8,128)(2,1)S(1)}, bf16[288,384]{1,0:T(8,128)(2,1)S(1)}, u32[]{:S(2)}, u32[]{:S(2)}) collective-permute-start(bf16[288,384]{1,0:T(8,128)(2,1)S(1)} %get-tuple-element.66), channel_id=1, source_target_pairs={{8,0},{9,1},{10,2},{11,3},{12,4},{13,5},{14,6},{15,7},{16,8},{17,9... | collective-permute-start | bytes 663560 | tf_op jit(solution)/shard_map/ppermute | solution.py:594
  16.0 5.0 %collective-permute-start.1 = (bf16[64,384]{1,0:T(8,128)(2,1)S(1)}, bf16[64,384]{1,0:T(8,128)(2,1)S(1)}, u32[]{:S(2)}, u32[]{:S(2)}) collective-permute-start(bf16[64,384]{1,0:T(8,128)(2,1)S(1)} %get-tuple-element.67), channel_id=1, source_target_pairs={{1,0},{2,1},{3,2},{4,3},{5,4},{6,5},{7,6},{0,7},{9,8},{10,9},{11,1... | collective-permute-start | bytes 147464 | tf_op jit(solution)/shard_map/ppermute | solution.py:595
  19.2 3.5 %collective-permute-start.2 = (bf16[64,384]{1,0:T(8,128)(2,1)S(1)}, bf16[64,384]{1,0:T(8,128)(2,1)S(1)}, u32[]{:S(2)}, u32[]{:S(2)}) collective-permute-start(bf16[64,384]{1,0:T(8,128)(2,1)S(1)} %get-tuple-element.68), channel_id=1, source_target_pairs={{9,0},{10,1},{11,2},{12,3},{13,4},{14,5},{15,6},{8,7},{17,8},{18,9... | collective-permute-start | bytes 147464 | tf_op jit(solution)/shard_map/ppermute | solution.py:596
  32.1 10.2 %collective-permute-start.5 = (bf16[288,384]{1,0:T(8,128)(2,1)S(1)}, bf16[288,384]{1,0:T(8,128)(2,1)S(1)}, u32[]{:S(2)}, u32[]{:S(2)}) collective-permute-start(bf16[288,384]{1,0:T(8,128)(2,1)S(1)} %get-tuple-element.72), channel_id=1, source_target_pairs={{120,0},{121,1},{122,2},{123,3},{124,4},{125,5},{126,6},{127,7},{0... | collective-permute-start | bytes 663560 | tf_op jit(solution)/shard_map/ppermute | solution.py:594
  32.2 10.1 %collective-permute-start.3 = (bf16[64,384]{1,0:T(8,128)(2,1)S(1)}, bf16[64,384]{1,0:T(8,128)(2,1)S(1)}, u32[]{:S(2)}, u32[]{:S(2)}) collective-permute-start(bf16[64,384]{1,0:T(8,128)(2,1)S(1)} %get-tuple-element.70), channel_id=1, source_target_pairs={{127,0},{120,1},{121,2},{122,3},{123,4},{124,5},{125,6},{126,7},{7... | collective-permute-start | bytes 147464 | tf_op jit(solution)/shard_map/ppermute | solution.py:596
  32.3 10.0 %collective-permute-start.4 = (bf16[64,384]{1,0:T(8,128)(2,1)S(1)}, bf16[64,384]{1,0:T(8,128)(2,1)S(1)}, u32[]{:S(2)}, u32[]{:S(2)}) collective-permute-start(bf16[64,384]{1,0:T(8,128)(2,1)S(1)} %get-tuple-element.71), channel_id=1, source_target_pairs={{7,0},{0,1},{1,2},{2,3},{3,4},{4,5},{5,6},{6,7},{15,8},{8,9},{9,10... | collective-permute-start | bytes 147464 | tf_op jit(solution)/shard_map/ppermute | solution.py:595
  32.7 9.6 %copy-start.8 = (bf16[576,352]{1,0:T(8,128)(2,1)S(1)}, bf16[576,352]{1,0:T(8,128)(2,1)}, u32[]{:S(2)}) copy-start(bf16[576,352]{1,0:T(8,128)(2,1)} %constant.16.clone.returned_ref) | copy-start | bytes 1216516
  50.6 2.6 %collective-permute-start.6 = (bf16[3584,128]{1,0:T(8,128)(2,1)S(1)}, bf16[3584,128]{1,0:T(8,128)(2,1)S(1)}, u32[]{:S(2)}, u32[]{:S(2)}) collective-permute-start(bf16[3584,128]{1,0:T(8,128)(2,1)S(1)} %get-tuple-element.104), channel_id=1, source_target_pairs={{8,0},{0,8},{24,16},{16,24},{40,32},{32,40},{56,48},{48,56},{72,64... | collective-permute-start | bytes 2752520 | tf_op jit(solution)/shard_map/ppermute | solution.py:607
  108.6 2.7 %collective-permute-start.7 = (bf16[8,512,128]{2,1,0:T(8,128)(2,1)S(1)}, bf16[8,512,128]{2,1,0:T(8,128)(2,1)S(1)}, u32[]{:S(2)}, u32[]{:S(2)}) collective-permute-start(bf16[8,512,128]{2,1,0:T(8,128)(2,1)S(1)} %all_to_all.17.mine_ref), channel_id=1, source_target_pairs={{8,0},{0,8},{24,16},{16,24},{40,32},{32,40},{56,48},{48,56},{72,64... | collective-permute-start | bytes 3145736 | tf_op jit(solution)/shard_map/ppermute | solution.py:615

commit v5 on v4

--- a/solution.py
+++ b/solution.py
@@ -32,9 +32,10 @@
 LOG2E = math.log2(math.e)
 SCALE = 1.0 / math.sqrt(HEAD_DIM)
 WBLOCK = 18 * DIM
-CHUNK = 448
-HALF = 8 * CHUNK
-TCHUNK = 64
+CHUNK = 224
+HALF = 16 * CHUNK
+PART = 9 * DIM
+EXTRA = HALF - 2 * PART
 TROWS = 208
 
 F32 = jnp.float32
@@ -259,7 +260,8 @@
 def put_weights(wbuf_ref, offset, value):
     tiles = value.shape[1] // 128
     for j in range(tiles):
-        wbuf_ref[(offset + j) * DIM : (offset + j + 1) * DIM, :] = value[:, j * 128 : (j + 1) * 128].astype(BF16)
+        half, place = divmod(offset + j, 9)
+        wbuf_ref[half, place * DIM : (place + 1) * DIM, :] = value[:, j * 128 : (j + 1) * 128].astype(BF16)
 
 
 def weight_grads(wbuf_ref, normed, dq, dk, dv, ctx, gbranch, normed_mlp, gpre_ref, expanded_ref, g):
@@ -294,21 +296,21 @@
     bias_ref, x_ref, pick_ref, gains_ref, qkv_ref, table_ref, trows_ref, tcols_ref, out_ref, sems,
 ):
     pairs = [
-        (far_x, x_ref), (far_pick, pick_ref), (far_gains.at[0], gains_ref), (far_qkv.at[0], qkv_ref),
-        (far_table.at[pl.ds(0, HEADS)], table_ref), (far_trows, trows_ref), (far_tcols, tcols_ref), (far_out.at[0], out_ref),
+        (far_table.at[pl.ds(0, HEADS)], table_ref), (far_trows, trows_ref), (far_tcols, tcols_ref),
+        (far_x, x_ref), (far_pick, pick_ref), (far_gains.at[0], gains_ref), (far_qkv.at[0], qkv_ref), (far_out.at[0], out_ref),
     ]
     fetches = [pltpu.make_async_copy(far, near, sems.at[i]) for i, (far, near) in enumerate(pairs)]
     for fetch in fetches:
         fetch.start()
-    for fetch in fetches[:4]:
+    for fetch in fetches[:3]:
+        fetch.wait()
+    expand_table(table_ref, trows_ref, tcols_ref, bias_ref)
+    for fetch in fetches[3:]:
         fetch.wait()
     x = gather_tokens(pick_ref[...], x_ref[...])
     xw_ref[...] = x.astype(BF16)
     hat, _ = normalize(x)
     project((hat * gains_ref[0:1, :]).astype(BF16), qkv_ref, q_ref, k_ref, v_ref)
-    for fetch in fetches[4:]:
-        fetch.wait()
-    expand_table(table_ref, trows_ref, tcols_ref, bias_ref)
     attention(q_ref, k_ref, v_ref, bias_ref, probs_ref, ctx_ref, head_rows())
     branch = nn(ctx_ref[...], out_ref[...]).astype(BF16)
     hidden_ref[...] = xw_ref[...].astype(F32) + branch.astype(F32)
@@ -354,6 +356,16 @@
     row_ref[part * 144 : (part + 1) * 144, :] = value[144:288]
     side_ref[part * STRIP : (part + 1) * STRIP, :] = value[288 : 288 + STRIP]
     corner_ref[part * STRIP : (part + 1) * STRIP, :] = value[288 + STRIP :]
+
+
+def split_halves(wbuf_ref, mine_ref, theirs_ref, sems):
+    core = lax.rem(lax.axis_index("lat"), 2)
+    send = pltpu.make_async_copy(wbuf_ref.at[1 - core], theirs_ref, sems.at[0])
+    keep = pltpu.make_async_copy(wbuf_ref.at[core], mine_ref, sems.at[1])
+    send.start()
+    keep.start()
+    send.wait()
+    keep.wait()
 
 
 def second_bias(table_ref, trows_ref, tcols_ref, bias_ref):
@@ -412,13 +424,14 @@
 
 def second_weights(
     normed_ref, dq_ref, dk_ref, dv_ref, ctx_ref, gbranch_ref, normed_mlp_ref, gpre_ref, expanded_ref, grad_ref, g_ref,
-    trows_ref, tcols_ref, wbuf_ref, table_grad_ref,
+    trows_ref, tcols_ref, mine_ref, theirs_ref, table_grad_ref, wbuf_ref, sems,
 ):
     weight_grads(
         wbuf_ref, normed_ref[...], dq_ref[...], dk_ref[...], dv_ref[...], ctx_ref[...], gbranch_ref[...],
         normed_mlp_ref[...], gpre_ref, expanded_ref, g_ref[...],
     )
     table_grad_ref[...] = collapse_table(grad_ref, trows_ref, tcols_ref)
+    split_halves(wbuf_ref, mine_ref, theirs_ref, sems)
 
 
 def first_mlp_back(
@@ -445,87 +458,79 @@
 
 def first_attention_back(
     ghid_ref, g_ref, normed_mlp_ref, gpre_ref, mlp_gain_ref, xw_ref, q_ref, k_ref, v_ref, probs_ref, ctx_ref, expanded_ref,
-    gains_ref, qkv_ref, out_ref, trows_ref, tcols_ref, pick_ref, last_wbuf_ref, last_gain_ref, last_table_ref,
-    gin_ref, mine_ref, theirs_ref, tables_ref,
-    gctx_ref, dq_ref, dk_ref, dv_ref, grad_ref, wbuf_ref, sems,
+    gains_ref, qkv_ref, out_ref, last_gain_ref,
+    gblock_ref, grad_ref, mine_ref, theirs_ref,
+    gctx_ref, dq_ref, dk_ref, dv_ref, wbuf_ref, sems,
 ):
     masks = head_rows()
-    fetch = pltpu.make_async_copy(last_wbuf_ref, wbuf_ref.at[pl.ds(WBLOCK, WBLOCK), :], sems.at[0])
-    fetch.start()
     gblock, normed, gbranch, gain_grad = attention_backward_part(
         xw_ref[...].astype(F32), gains_ref[0:1, :], qkv_ref, out_ref, ghid_ref[...],
         q_ref, k_ref, v_ref, probs_ref, ctx_ref, gctx_ref, dq_ref, dk_ref, dv_ref, grad_ref, masks,
     )
-    gin_ref[...] = scatter_tokens(pick_ref[...], gblock.astype(BF16)).astype(BF16)
+    gblock_ref[...] = gblock.astype(BF16)
     weight_grads(
         wbuf_ref, normed, dq_ref[...], dk_ref[...], dv_ref[...], ctx_ref[...], gbranch,
         normed_mlp_ref[...], gpre_ref, expanded_ref, g_ref[...],
     )
+    gains = jnp.concatenate([gain_grad, mlp_gain_ref[...], last_gain_ref[0:1, :], last_gain_ref[1:2, :]], axis=1)
+    for h in range(2):
+        wbuf_ref[h, PART:, :] = jnp.zeros((EXTRA, 128), BF16)
+    for j in range(6):
+        tile = jnp.concatenate([gains[:, j * 128 : (j + 1) * 128], jnp.zeros((15, 128), F32)], axis=0)
+        wbuf_ref[0, PART + j * 16 : PART + (j + 1) * 16, :] = tile.astype(BF16)
+    split_halves(wbuf_ref, mine_ref, theirs_ref, sems)
+
+
+def first_finish(gblock_ref, grad_ref, last_table_ref, trows_ref, tcols_ref, pick_ref, gin_ref, tables_ref):
     tables_ref[0:TROWS, :] = collapse_table(grad_ref, trows_ref, tcols_ref)
     tables_ref[TROWS : 2 * TROWS, :] = last_table_ref[...]
-    tables_ref[2 * TROWS :, :] = jnp.zeros((8 * TCHUNK - 2 * TROWS, 128), BF16)
-    gains = jnp.concatenate([gain_grad, mlp_gain_ref[...], last_gain_ref[0:1, :], last_gain_ref[1:2, :]], axis=1)
-    wbuf_ref[2 * WBLOCK :, :] = jnp.zeros((2 * HALF - 2 * WBLOCK, 128), BF16)
-    for j in range(6):
-        tile = jnp.concatenate([gains[:, j * 128 : (j + 1) * 128], jnp.zeros((15, 128), F32)], axis=0)
-        wbuf_ref[2 * WBLOCK + j * 16 : 2 * WBLOCK + (j + 1) * 16, :] = tile.astype(BF16)
-    fetch.wait()
+    gin_ref[...] = scatter_tokens(pick_ref[...], gblock_ref[...].astype(F32)).astype(BF16)
+
+
+def pack(first_ref, first_other_ref, last_ref, last_other_ref, packed_ref):
+    first = (first_ref[...].astype(F32) + first_other_ref[...].astype(F32)).astype(BF16)
+    packed_ref[:PART, :] = first[:PART]
+    packed_ref[PART : 2 * PART, :] = (last_ref[...].astype(F32) + last_other_ref[...].astype(F32)).astype(BF16)
+    packed_ref[2 * PART :, :] = first[PART:]
+
+
+def add_two(mine_ref, other_ref, total_ref):
+    total_ref[...] = (mine_ref[...].astype(F32) + other_ref[...].astype(F32)).astype(BF16)
+
+
+def sum_parts(parts_ref, total_ref):
+    total = parts_ref[0].astype(F32)
+    for j in range(1, 16):
+        total += parts_ref[j].astype(F32)
+    total_ref[...] = total.astype(BF16)
+
+
+def sum_and_spread(*refs):
+    total = refs[0][...].astype(F32)
+    for ref in refs[1:-1]:
+        total += ref[...].astype(F32)
+    total = total.astype(BF16)
+    for j in range(16):
+        refs[-1][j] = total
+
+
+def unpack(
+    mine_ref, other_ref, t0_ref, t1_ref, t2_ref, t3_ref, qkv_ref, out_ref, up_ref, down_ref, gains_ref, table_ref, sum_ref
+):
     core = lax.rem(lax.axis_index("lat"), 2)
-    keep = pltpu.make_async_copy(wbuf_ref.at[pl.ds(core * HALF, HALF), :], mine_ref, sems.at[1])
-    send = pltpu.make_async_copy(wbuf_ref.at[pl.ds((1 - core) * HALF, HALF), :], theirs_ref, sems.at[2])
-    send.start()
-    keep.start()
-    send.wait()
-    keep.wait()
-
-
-def pack_core(mine_ref, other_ref, tables_ref, packed_ref):
-    for j in range(8):
-        rows = slice(j * CHUNK, (j + 1) * CHUNK)
-        total = mine_ref[rows, :].astype(F32) + other_ref[rows, :].astype(F32)
-        packed_ref[j, 0:CHUNK, :] = total.astype(BF16)
-        packed_ref[j, CHUNK:, :] = tables_ref[j * TCHUNK : (j + 1) * TCHUNK, :]
-
-
-def sum_eight(ref, rows):
-    total = ref[0, rows, :].astype(F32)
-    for j in range(1, 8):
-        total += ref[j, rows, :].astype(F32)
-    return total.astype(BF16)
-
-
-def sum_lon(parts_ref, spread_ref, table_ref):
-    total = sum_eight(parts_ref, slice(0, CHUNK))
-    for j in range(8):
-        spread_ref[j] = total
-    table_ref[...] = sum_eight(parts_ref, slice(CHUNK, CHUNK + TCHUNK))
-
-
-def sum_lat(parts_ref, table_ref, spread_ref):
-    total = sum_eight(parts_ref, slice(0, CHUNK))
-    for j in range(8):
-        spread_ref[j, 0:CHUNK, :] = total
-        spread_ref[j, CHUNK:, :] = table_ref[...]
-
-
-def unpack(mine_ref, other_ref, qkv_ref, out_ref, up_ref, down_ref, gains_ref, table_ref):
-    core = lax.rem(lax.axis_index("lat"), 2)
-
-    def load(start, count):
-        pieces = []
-        while count:
-            half, place = divmod(start, HALF)
-            j, place = divmod(place, CHUNK)
-            size = min(count, CHUNK - place)
-            here = mine_ref[j, place : place + size, :].astype(F32)
-            there = other_ref[j, place : place + size, :].astype(F32)
-            pieces.append(jnp.where(core == half, here, there))
-            start, count = start + size, count - size
-        return pieces[0] if len(pieces) == 1 else jnp.concatenate(pieces, axis=0)
-
+
+    def load(half, start, count):
+        here = mine_ref[start : start + count, :].astype(F32)
+        there = other_ref[start : start + count, :].astype(F32)
+        return jnp.where(core == half, here, there)
+
+    total = t0_ref[...].astype(F32)
+    for ref in (t1_ref, t2_ref, t3_ref):
+        total += ref[...].astype(F32)
+    sum_ref[...] = total
     for b in range(2):
         for j in range(18):
-            tile = load(b * WBLOCK + j * DIM, DIM)
+            tile = load(j // 9, b * PART + j % 9 * DIM, DIM)
             if j < 6:
                 up_ref[b, :, j * 128 : (j + 1) * 128] = tile
             elif j < 12:
@@ -538,14 +543,12 @@
             else:
                 out_ref[b, :, 64:192] = tile
         for j in range(26):
-            k, place = divmod(b * TROWS + j * 8, TCHUNK)
-            base = CHUNK + place // 16 * 16
-            pair = mine_ref[k, base : base + 16, :].astype(F32)
-            piece = pair[place % 16 : place % 16 + HEADS]
+            place = b * TROWS + j * 8
+            piece = sum_ref[place : place + HEADS, :]
             width = min(128, TABLE - j * 128)
             for h in range(HEADS):
                 table_ref[b * HEADS + h, :, j * 128 : j * 128 + width] = piece[h : h + 1, :width]
-    gains = jnp.concatenate([load(2 * WBLOCK + j * 16, 16)[0:1] for j in range(6)], axis=1)
+    gains = jnp.concatenate([load(0, 2 * PART + j * 16, 16)[0:1] for j in range(6)], axis=1)
     for b in range(2):
         for i in range(2):
             k = b * 2 + i
@@ -601,21 +604,59 @@
     return pltpu.VMEM(shape, dtype)
 
 
-def sum_over_devices(mine, theirs, tables, sizes):
-    pairs = [(i ^ 1, i) for i in range(sizes[0])]
-    groups = [[core + 2 * k for k in range(sizes[0] // 2)] for core in range(2)]
-    other = lax.ppermute(theirs, "lat", pairs)
-    packed = (8, CHUNK + TCHUNK, 128)
-    [sent] = call(pack_core, [mine, other, tables], [whole(a) for a in (mine, other, tables)], [(packed, BF16)])
-    parts = lax.all_to_all(sent, "lon", 0, 0)
-    spread, table = call(sum_lon, [parts], [whole(parts)], [((8, CHUNK, 128), BF16), ((TCHUNK, 128), BF16)])
-    parts = lax.all_to_all(spread, "lat", 0, 0, axis_index_groups=groups)
-    [spread] = call(sum_lat, [parts, table], [whole(parts), whole(table)], [(packed, BF16)])
-    half = lax.all_to_all(spread, "lon", 0, 0)
-    other = lax.ppermute(half, "lat", pairs)
+def device_place(i):
+    lat, lon = divmod(i, 8)
+    return lat // 8, lat // 2 % 4, lat % 2, lon // 2, lon % 2
+
+
+def flat_device(z_hi, y, core, x, z_lo):
+    return ((z_hi * 4 + y) * 2 + core) * 8 + x * 2 + z_lo
+
+
+def shifted_pairs(core=0, x=0, z_lo=0):
+    pairs = []
+    for i in range(128):
+        h, y, c, a, b = device_place(i)
+        pairs.append((flat_device(h, y, (c + core) % 2, (a + x) % 4, (b + z_lo) % 2), i))
+    return pairs
+
+
+def moved(array, **steps):
+    return lax.ppermute(array, ("lat", "lon"), shifted_pairs(**steps))
+
+
+def sum_over_devices(first, last, finish):
+    both = ("lat", "lon")
+    planes = {}
+    for i in range(128):
+        _, _, c, a, _ = device_place(i)
+        planes.setdefault((c, a), []).append(i)
+    groups = list(planes.values())
+
+    def run(kernel, operands, shape):
+        [result] = call(kernel, operands, [whole(a) for a in operands], [(shape, BF16)])
+        return result
+
+    sent = run(pack, [first[0], moved(first[1], core=1), *last], (HALF, 128))
+    sent, finish = lax.optimization_barrier((sent, finish))
+    parts = lax.all_to_all(sent.reshape(16, CHUNK, 128), both, 0, 0, axis_index_groups=groups)
+    outs = [((GRID, 2 * DIM), BF16), ((2 * TROWS, 128), BF16)]
+    grad_inputs, tables = call(first_finish, finish, [whole(a) for a in finish], outs)
+    other = moved(tables, z_lo=1)
+    parts, other = lax.optimization_barrier((parts, other))
+    tables = run(add_two, [tables, other], tables.shape)
+    total = run(sum_parts, [parts], (CHUNK, 128))
+    spread = run(sum_and_spread, [total] + [moved(total, x=k) for k in (1, 2, 3)], (16, CHUNK, 128))
+    spread, tables = lax.optimization_barrier((spread, tables))
+    half = lax.all_to_all(spread, both, 0, 0, axis_index_groups=groups)
+    table_terms = [tables] + [moved(tables, x=k) for k in (1, 2, 3)]
+    half, table_terms = lax.optimization_barrier((half, table_terms))
+    half = half.reshape(HALF, 128)
+    operands = [half, moved(half, core=1), *table_terms]
     outs = [((2, DIM, 3 * DIM), F32), ((2, DIM, DIM), F32), ((2, DIM, UNITS), F32), ((2, DIM, UNITS), F32)]
     outs += [((2, 2, DIM), F32), ((2 * HEADS, 1, TABLE), F32)]
-    return call(unpack, [half, other], [whole(half), whole(other)], outs)
+    grads = call(unpack, operands, [whole(a) for a in operands], outs, [vmem((2 * TROWS, 128), F32)])
+    return grad_inputs, grads
 
 
 def on_device(sizes, inputs, cotangent, norm_gains, qkv_weight, out_weight, up_weight, down_weight, bias_table):
@@ -679,32 +720,37 @@
     arrived = exchange(*sent, sizes, -1)
     g, *terms = terms
     operands = [*terms, g, trows, tcols]
-    outs = [((WBLOCK, 128), BF16), ((TROWS, 128), BF16)]
-    last_wbuf, last_table = call(second_weights, operands, specs_for(operands, 1), outs, (), 4, mebibytes=14)
+    outs = [((PART, 128), BF16)] * 2 + [((TROWS, 128), BF16)]
+    out_specs = [in_place()] * 2 + [whole(jax.ShapeDtypeStruct(*o)) for o in outs[2:]]
+    scratch = [vmem((2, PART, 128), BF16), pltpu.SemaphoreType.DMA((2,))]
+    results = call(second_weights, operands, specs_for(operands, 1), outs, scratch, 4, out_specs, 14)
+    last_mine, last_theirs, last_table = results
 
     operands = [back_own, *arrived, hidden, slope, gains, up, down, pick_back]
     outs = [wide_tok, (tok, F32), wide_tok, wide_hid, ((1, DIM), F32)]
     results = call(first_mlp_back, operands, specs_for(operands, 0), outs, [vmem(src, BF16)], 3, mebibytes=14)
     g, ghid, normed_mlp, gpre, mlp_gain = results
+    ghid, last_theirs = lax.optimization_barrier((ghid, last_theirs))
+    last = [last_mine, moved(last_theirs, core=1)]
 
     operands = [ghid, g, normed_mlp, gpre, mlp_gain, xw, q, k, v, probs_first, ctx, expanded, gains, qkv, out]
-    operands += [trows, tcols, pick_grid, last_wbuf, last_gain, last_table]
-    specs = specs_for(operands, 0)
-    specs[-3] = in_place()
-    outs = [((GRID, 2 * DIM), BF16), ((HALF, 128), BF16), ((HALF, 128), BF16), ((8 * TCHUNK, 128), BF16)]
-    out_specs = [pl.BlockSpec((GRID, 2 * DIM), lambda i: (0, 0)), in_place(), in_place()]
-    out_specs += [pl.BlockSpec((8 * TCHUNK, 128), lambda i: (0, 0))]
-    scratch = [vmem(tok, BF16)] * 4 + [vmem(bias, F32), vmem((2 * HALF, 128), BF16), pltpu.SemaphoreType.DMA((3,))]
-    grad_inputs, mine, theirs, tables = call(
-        first_attention_back, operands, specs, outs, scratch, 8, out_specs, 14
+    operands += [last_gain]
+    first_shape = (PART + EXTRA, 128)
+    outs = [wide_tok, (bias, F32), (first_shape, BF16), (first_shape, BF16)]
+    out_specs = [whole(jax.ShapeDtypeStruct(*o)) for o in outs[:2]] + [in_place()] * 2
+    scratch = [vmem(tok, BF16)] * 4 + [vmem((2, *first_shape), BF16), pltpu.SemaphoreType.DMA((2,))]
+    gblock, grad_scores, *first = call(
+        first_attention_back, operands, specs_for(operands, 0), outs, scratch, 8, out_specs, 14
     )
-
+    last, first = lax.optimization_barrier((last, first))
+    finish = [gblock, grad_scores, last_table, trows, tcols, pick_grid]
+    grad_inputs, grads = sum_over_devices(first, last, finish)
     y_rows, y_side, y_corner = arrived
     rows = jnp.concatenate([y_rows[144:], y_own]).reshape(ROWS, COLS, 2 * DIM)
     edge = jnp.concatenate([a[STRIP : STRIP + 18].reshape(3, 6, 2 * DIM) for a in (y_corner, y_side)])
     output = jnp.concatenate([edge, rows[:, 6:]], axis=1)
 
-    grad_qkv, grad_out, grad_up, grad_down, grad_gains, grad_table = sum_over_devices(mine, theirs, tables, sizes)
+    grad_qkv, grad_out, grad_up, grad_down, grad_gains, grad_table = grads
     grad_down = jnp.swapaxes(grad_down, 1, 2)
     grad_table = grad_table.reshape(2, 1, HEADS, TABLE)
     return (output, grad_inputs.reshape(ROWS, COLS, 2 * DIM), grad_gains, grad_qkv, grad_out, grad_up, grad_down, grad_table)

time: 115 us -> 107 us (0.930)
  blocking collectives: 55 us -> 0 us
  waiting for transfers between devices: 14.7 us -> 44.6 us
  starting transfers between devices: 9.8 us -> 24.9 us
  Pallas kernels: 32 us -> 33.9 us
    all_to_all x3 -> x0, blocking collectives: 55 us -> none  [the longest x1 19.1 us: sum_over_devices(): parts = lax.all_to_all(sent, 'lon', 0, 0)]
    ppermute x2 -> x10, waiting for transfers between devices: 4.19 us -> 21 us  [moved(): return lax.ppermute(array, ('lat', 'lon'), shifted_pairs(**steps))]
    all_to_all x0 -> x2, waiting for transfers between devices: none -> 12.9 us  [the longest x1 7.31 us: sum_over_devices(): lax.all_to_all(sent.reshape(16, CHUNK, 128), both, 0, 0, axis_index_group...]
    all_to_all x0 -> x2, starting transfers between devices: none -> 7.71 us  [the longest x1 4.07 us: sum_over_devices(): half = lax.all_to_all(spread, both, 0, 0, axis_index_groups=groups)]
    ppermute x2 -> x10, starting transfers between devices: 0.09 us -> 7.62 us  [moved(): return lax.ppermute(array, ('lat', 'lon'), shifted_pairs(**steps))]
    ppermute x2, waiting for transfers between devices: 0.61 us -> 5.08 us  [exchange(): side = lax.ppermute(side, both, neighbour(sizes, (0, step)))]
    ppermute x2, waiting for transfers between devices: 9.89 us -> 5.65 us  [exchange(): corner = lax.ppermute(corner, both, neighbour(sizes, (step, step)))]
    pallas_call x11 -> x13, Pallas kernels: 32 us -> 33.9 us  [call(): pl.pallas_call(kernel, grid=(1,), out_shape=shapes, in_specs=specs, out_s...]
  transfers between devices with their start and end apart: 8 -> 18, of which waited for: 5 -> 15; matrix products, arithmetic and copies ran while one was open for 1% -> 1% of each run, Pallas kernels for 2% -> 9%
where the time goes in v5:
time: 107 us; the launch traced here: 105 us
  waiting for transfers between devices  44.6 us (42%)
  Pallas kernels  33.9 us (32%)
  starting transfers between devices  24.9 us (23%)
    pallas_call x13, Pallas kernels, call(): pl.pallas_call(kernel, grid=(1,), out_shape=shapes, in_specs=specs, out_s...  33.9 us
    ppermute x10, waiting for transfers between devices, moved(): return lax.ppermute(array, ('lat', 'lon'), shifted_pairs(**steps))  21 us
    ppermute x10, starting transfers between devices, moved(): return lax.ppermute(array, ('lat', 'lon'), shifted_pairs(**steps))  7.62 us
    all_to_all x1, waiting for transfers between devices, sum_over_devices(): lax.all_to_all(sent.reshape(16, CHUNK, 128), both, 0, 0, axis_index_group...  7.31 us
    ppermute x2, starting transfers between devices, exchange(): rows = lax.ppermute(rows, both, neighbour(sizes, (step, 0)))  5.98 us
    ppermute x2, waiting for transfers between devices, exchange(): corner = lax.ppermute(corner, both, neighbour(sizes, (step, step)))  5.65 us
    all_to_all x1, waiting for transfers between devices, sum_over_devices(): half = lax.all_to_all(spread, both, 0, 0, axis_index_groups=groups)  5.55 us
    ppermute x2, waiting for transfers between devices, exchange(): side = lax.ppermute(side, both, neighbour(sizes, (0, step)))  5.08 us
  transfers between devices with their start and end apart: 18, of which 15 were waited for; matrix products, arithmetic and copies ran while one was open for 1% of the time, Pallas kernels for 9%

profile of v5, /device:TPU:0, one launch (start us, length us, event | category | flops | bytes accessed | tf_op | source)
XLA Modules:
  0.0 105.3 jit_solution(17357909776298079561)
XLA Ops:
  0.7 0.0 copy-start.7
  0.7 6.5 %shard_map.197 = (bf16[576,192]{1,0:T(8,128)(2,1)S(1)}, bf16[576,192]{1,0:T(8,128)(2,1)S(1)}, bf16[576,192]{1,0:T(8,128)(2,1)S(1)}, bf16[576,192]{1,0:T(8,128)(2...) custom-call(bf16[288,384]{1,0:T(8,128)(2,1)} %bitcast.20, ...), custom_call_target="tpu_custom_call" | custom-call | flops 7699999744 | bytes 4074528 | tf_op jit(solution)/shard_map/pallas_call | solution.py:574
  7.3 0.0 copy-start.10
  7.3 0.0 copy-start.11
  7.3 2.6 %shard_map.198 = (bf16[576,768]{1,0:T(8,128)(2,1)S(1)}, bf16[576,768]{1,0:T(8,128)(2,1)S(1)}, bf16[144,384]{1,0:T(8,128)(2,1)S(1)}, bf16[288,384]{1,0:T(8,128)(2...) custom-call(f32[576,192]{1,0:T(8,128)S(1)} %get-tuple-element.84.hidden_ref, ...), custom_call_target="tpu_custom_call" | custom-call | flops 4400000000 | bytes 4414464 | tf_op jit(solution)/shard_map/pallas_call | solution.py:574
  9.9 0.0 copy-start.9
  9.9 5.9 %collective-permute-start = (bf16[288,384]{1,0:T(8,128)(2,1)S(1)}, bf16[288,384]{1,0:T(8,128)(2,1)S(1)}, u32[]{:S(2)}, u32[]{:S(2)}) collective-permute-start(bf16[288,384]{1,0:T(8,128)(2,1)S(1)} %get-tuple-element.89), channel_id=1, source_target_pairs={{8,0},{9,1},{10,2},{11,3},{12,4},{13,5},{14,6},{15,7},{16,8},{17,9... | collective-permute-start | bytes 663560 | tf_op jit(solution)/shard_map/ppermute | solution.py:597
  15.8 3.2 %collective-permute-start.1 = (bf16[64,384]{1,0:T(8,128)(2,1)S(1)}, bf16[64,384]{1,0:T(8,128)(2,1)S(1)}, u32[]{:S(2)}, u32[]{:S(2)}) collective-permute-start(bf16[64,384]{1,0:T(8,128)(2,1)S(1)} %get-tuple-element.90), channel_id=1, source_target_pairs={{1,0},{2,1},{3,2},{4,3},{5,4},{6,5},{7,6},{0,7},{9,8},{10,9},{11,1... | collective-permute-start | bytes 147464 | tf_op jit(solution)/shard_map/ppermute | solution.py:598
  19.1 1.1 %shard_map.199.bias_ref = f32[144,864]{1,0:T(8,128)S(1)} custom-call(f32[12,1,3312]{2,1,0:T(1,128)S(1)} %bitcast.18, bf16[2,96,192]{2,1,0:T(8,128)(2,1)S(1)} %copy-done.11, bf16[2,138,276]{2,1,0:T(8,128)(2,1)S(1)} %copy-done.10), custom_call_target="tpu_custom_call" | custom-call | flops 2200000000 | bytes 882720 | tf_op jit(solution)/shard_map/pallas_call | solution.py:574
  20.2 0.6 collective-permute-done.1.side_ref
  20.8 1.8 %collective-permute-done.2.corner_ref = bf16[64,384]{1,0:T(8,128)(2,1)S(1)} collective-permute-done((bf16[64,384]{1,0:T(8,128)(2,1)S(1)}, bf16[64,384]{1,0:T(8,128)(2,1)S(1)}, u32[]{:S(2)}, u32[]{:S(2)}) %collective-permute-start.2) | collective-permute-done | bytes 49184 | tf_op jit(solution)/shard_map/ppermute | solution.py:599
  22.6 9.3 %shard_map.200 = (bf16[144,384]{1,0:T(8,128)(2,1)S(1)}, bf16[144,384]{1,0:T(8,128)(2,1)S(1)}, bf16[288,384]{1,0:T(8,128)(2,1)S(1)}, bf16[64,384]{1,0:T(8,128)(2,...) custom-call(bf16[144,384]{1,0:T(8,128)(2,1)S(1)} %get-tuple-element., ...), custom_call_target="tpu_custom_call" | custom-call | flops 13200000000 | bytes 7905792 | tf_op jit(solution)/shard_map/pallas_call | solution.py:574
  31.9 0.1 collective-permute-start.5
  32.0 0.2 collective-permute-start.4
  32.2 0.2 collective-permute-start.3
  32.4 1.9 %shard_map.201 = (bf16[1728,128]{1,0:T(8,128)(2,1)S(1)}, bf16[1728,128]{1,0:T(8,128)(2,1)S(1)}, bf16[208,128]{1,0:T(8,128)(2,1)S(1)}) custom-call(bf16[576,192]{1,0:T(8,128)(2,1)S(1)} %get-tuple-element.97.normed_ref, bf16[576,192]{1,0:T(8,128)(2,1)S(1)} %get-tuple-element.98.dq_ref, bf16[576,192]{1,0:T(8,128)(2,1)S(1)} %get-tuple-element.99.dk_ref, ...), custom_call_target="tpu_custom_call" | custom-call | flops 4400000000 | bytes 5200672 | tf_op jit(solution)/shard_map/pallas_call | solution.py:574
  34.3 4.5 %collective-permute-done.4.side_ref = bf16[64,384]{1,0:T(8,128)(2,1)S(1)} collective-permute-done((bf16[64,384]{1,0:T(8,128)(2,1)S(1)}, bf16[64,384]{1,0:T(8,128)(2,1)S(1)}, u32[]{:S(2)}, u32[]{:S(2)}) %collective-permute-start.4) | collective-permute-done | bytes 49184 | tf_op jit(solution)/shard_map/ppermute | solution.py:598
  38.8 3.9 %collective-permute-done.3.corner_ref = bf16[64,384]{1,0:T(8,128)(2,1)S(1)} collective-permute-done((bf16[64,384]{1,0:T(8,128)(2,1)S(1)}, bf16[64,384]{1,0:T(8,128)(2,1)S(1)}, u32[]{:S(2)}, u32[]{:S(2)}) %collective-permute-start.3) | collective-permute-done | bytes 49184 | tf_op jit(solution)/shard_map/ppermute | solution.py:599
  42.7 2.2 %shard_map.202 = (bf16[576,192]{1,0:T(8,128)(2,1)S(1)}, f32[576,192]{1,0:T(8,128)S(1)}, bf16[576,192]{1,0:T(8,128)(2,1)S(1)}, bf16[576,768]{1,0:T(8,128)(2,1)S(1)}, f32[1,192]{1,0:T(1,128)S(1)}) custom-call(bf16[144,384]{1,0:T(8,128)(2,1)S(1)} %get-tuple-element.109.back_ref, bf16[288,384]{1,0:T(8,128)(2,1)S(1)} %collective-permute-done.5.row_ref, ...), custom_call_target="tpu_custom_call" | custom-call | flops 3300000000 | bytes 5115648 | tf_op jit(solution)/shard_map/pallas_call | solution.py:574
  44.9 0.1 collective-permute-start.6
  45.0 4.3 %shard_map.203 = (bf16[576,192]{1,0:T(8,128)(2,1)S(1)}, f32[144,864]{1,0:T(8,128)S(1)}, bf16[1856,128]{1,0:T(8,128)(2,1)S(1)}, bf16[1856,128]{1,0:T(8,128)(2,1)S(1)}) custom-call(f32[576,192]{1,0:T(8,128)S(1)} %get-tuple-element.114.ghid_ref, bf16[576,192]{1,0:T(8,128)(2,1)S(1)} %get-tuple-element.115.g_ref, ...), custom_call_target="tpu_custom_call" | custom-call | flops 8800000000 | bytes 7019776 | tf_op jit(solution)/shard_map/pallas_call | solution.py:574
  49.3 0.6 collective-permute-start.7
  49.9 1.5 %collective-permute-done.7.first_other_ref = bf16[1856,128]{1,0:T(8,128)(2,1)S(1)} collective-permute-done((bf16[1856,128]{1,0:T(8,128)(2,1)S(1)}, bf16[1856,128]{1,0:T(8,128)(2,1)S(1)}, u32[]{:S(2)}, u32[]{:S(2)}) %collective-permute-start.7) | collective-permute-done | bytes 475168 | tf_op jit(solution)/shard_map/ppermute | solution.py:625
  51.3 1.1 %shard_map.204 = bf16[3584,128]{1,0:T(8,128)(2,1)} custom-call(bf16[1856,128]{1,0:T(8,128)(2,1)S(1)} %get-tuple-element.129.first_ref, bf16[1856,128]{1,0:T(8,128)(2,1)S(1)} %collective-permute-done.7.first_other_ref, bf16[1728,128]{1,0:T(8,128)(2,1)S(1)} %get-tuple-element.131.last_ref, bf16[1728,128]{1,0:T(8,128)(2,1)S(1)} %collective-permute-done.6.last_other_ref), custom_call_target="tpu_custom_call" | custom-call | flops 2200000000 | bytes 2752512 | tf_op jit(solution)/shard_map/pallas_call | solution.py:574
  52.5 3.6 %all-to-all-start = ((bf16[16,224,128]{2,1,0:T(8,128)(2,1)}), bf16[16,224,128]{2,1,0:T(8,128)(2,1)S(1)}, u32[]{:S(2)}, u32[]{:S(2)}) async-start(bf16[16,224,128]{2,1,0:T(8,128)(2,1)} %bitcast.6), calls=%async_computation | async-start | bytes 1835008 | tf_op jit(solution)/shard_map/all_to_all | solution.py:642
  56.1 1.6 %shard_map.205 = (bf16[288,384]{1,0:T(8,128)(2,1)}, bf16[416,128]{1,0:T(8,128)(2,1)S(1)}) custom-call(bf16[576,192]{1,0:T(8,128)(2,1)S(1)} %get-tuple-element.136.gblock_ref, f32[144,864]{1,0:T(8,128)S(1)} %get-tuple-element.137.grad_ref, bf16[208,128]{1,0:T(8,128)(2,1)S(1)} %get-tuple-element.138.last_table_ref, bf16[2,96,192]{2,1,0:T(8,128)(2,1)S(1)} %copy-done.11, ...), custom_call_target="tpu_custom_call" | custom-call | flops 2200000000 | bytes 1657632 | tf_op jit(solution)/shard_map/pallas_call | solution.py:574
  57.7 1.8 %collective-permute-start.8 = (bf16[416,128]{1,0:T(8,128)(2,1)S(1)}, bf16[416,128]{1,0:T(8,128)(2,1)S(1)}, u32[]{:S(2)}, u32[]{:S(2)}) collective-permute-start(bf16[416,128]{1,0:T(8,128)(2,1)S(1)} %get-tuple-element.144.mine_ref), channel_id=1, source_target_pairs={{1,0},{0,1},{3,2},{2,3},{5,4},{4,5},{7,6},{6,7},{9,8},{8,9},{11,10... | collective-permute-start | bytes 319496 | tf_op jit(solution)/shard_map/ppermute | solution.py:625
  59.6 6.9 %collective-permute-done.8.other_ref = bf16[416,128]{1,0:T(8,128)(2,1)S(1)} collective-permute-done((bf16[416,128]{1,0:T(8,128)(2,1)S(1)}, bf16[416,128]{1,0:T(8,128)(2,1)S(1)}, u32[]{:S(2)}, u32[]{:S(2)}) %collective-permute-start.8) | collective-permute-done | bytes 106528 | tf_op jit(solution)/shard_map/ppermute | solution.py:625
  66.4 7.3 %all-to-all-done.parts_ref = bf16[16,224,128]{2,1,0:T(8,128)(2,1)S(1)} async-done(((bf16[16,224,128]{2,1,0:T(8,128)(2,1)}), bf16[16,224,128]{2,1,0:T(8,128)(2,1)S(1)}, u32[]{:S(2)}, u32[]{:S(2)}) %all-to-all-start) | async-done | bytes 917536 | tf_op jit(solution)/shard_map/all_to_all | solution.py:642
  73.7 0.1 shard_map.206.refs_0_
  73.9 1.1 %collective-permute-start.9 = (bf16[224,128]{1,0:T(8,128)(2,1)S(1)}, bf16[224,128]{1,0:T(8,128)(2,1)S(1)}, u32[]{:S(2)}, u32[]{:S(2)}) collective-permute-start(bf16[224,128]{1,0:T(8,128)(2,1)S(1)} %shard_map.206.refs_0_), channel_id=1, source_target_pairs={{2,0},{3,1},{4,2},{5,3},{6,4},{7,5},{0,6},{1,7},{10,8},{11,9},{12,... | collective-permute-start | bytes 172040 | tf_op jit(solution)/shard_map/ppermute | solution.py:625
  75.0 1.0 collective-permute-start.11
  76.0 2.1 %collective-permute-done.9.refs_1_ = bf16[224,128]{1,0:T(8,128)(2,1)S(1)} collective-permute-done((bf16[224,128]{1,0:T(8,128)(2,1)S(1)}, bf16[224,128]{1,0:T(8,128)(2,1)S(1)}, u32[]{:S(2)}, u32[]{:S(2)}) %collective-permute-start.9) | collective-permute-done | bytes 57376 | tf_op jit(solution)/shard_map/ppermute | solution.py:625
  78.1 2.8 %collective-permute-done.10.refs_2_ = bf16[224,128]{1,0:T(8,128)(2,1)S(1)} collective-permute-done((bf16[224,128]{1,0:T(8,128)(2,1)S(1)}, bf16[224,128]{1,0:T(8,128)(2,1)S(1)}, u32[]{:S(2)}, u32[]{:S(2)}) %collective-permute-start.10) | collective-permute-done | bytes 57376 | tf_op jit(solution)/shard_map/ppermute | solution.py:625
  80.9 0.4 collective-permute-done.11.refs_3_
  81.3 1.0 shard_map.207
  82.3 4.1 %all-to-all-start.1 = ((bf16[16,224,128]{2,1,0:T(8,128)(2,1)}), bf16[16,224,128]{2,1,0:T(8,128)(2,1)S(1)}, u32[]{:S(2)}, u32[]{:S(2)}) async-start(bf16[16,224,128]{2,1,0:T(8,128)(2,1)} %shard_map.207), calls=%async_computation.1 | async-start | bytes 1835008 | tf_op jit(solution)/shard_map/all_to_all | solution.py:651
  86.4 1.5 %collective-permute-start.12 = (bf16[416,128]{1,0:T(8,128)(2,1)S(1)}, bf16[416,128]{1,0:T(8,128)(2,1)S(1)}, u32[]{:S(2)}, u32[]{:S(2)}) collective-permute-start(bf16[416,128]{1,0:T(8,128)(2,1)S(1)} %shard_map.208.t0_ref), channel_id=1, source_target_pairs={{2,0},{3,1},{4,2},{5,3},{6,4},{7,5},{0,6},{1,7},{10,8},{11,9},{12,... | collective-permute-start | bytes 319496 | tf_op jit(solution)/shard_map/ppermute | solution.py:625
  87.9 0.9 collective-permute-start.13
  88.8 0.7 collective-permute-start.14
  89.4 1.7 %collective-permute-done.12.t1_ref = bf16[416,128]{1,0:T(8,128)(2,1)S(1)} collective-permute-done((bf16[416,128]{1,0:T(8,128)(2,1)S(1)}, bf16[416,128]{1,0:T(8,128)(2,1)S(1)}, u32[]{:S(2)}, u32[]{:S(2)}) %collective-permute-start.12) | collective-permute-done | bytes 106528 | tf_op jit(solution)/shard_map/ppermute | solution.py:625
  91.2 3.0 %collective-permute-done.13.t2_ref = bf16[416,128]{1,0:T(8,128)(2,1)S(1)} collective-permute-done((bf16[416,128]{1,0:T(8,128)(2,1)S(1)}, bf16[416,128]{1,0:T(8,128)(2,1)S(1)}, u32[]{:S(2)}, u32[]{:S(2)}) %collective-permute-start.13) | collective-permute-done | bytes 106528 | tf_op jit(solution)/shard_map/ppermute | solution.py:625
  94.1 1.1 %collective-permute-done.14.t3_ref = bf16[416,128]{1,0:T(8,128)(2,1)S(1)} collective-permute-done((bf16[416,128]{1,0:T(8,128)(2,1)S(1)}, bf16[416,128]{1,0:T(8,128)(2,1)S(1)}, u32[]{:S(2)}, u32[]{:S(2)}) %collective-permute-start.14) | collective-permute-done | bytes 106528 | tf_op jit(solution)/shard_map/ppermute | solution.py:625
  95.2 5.5 %all-to-all-done.1 = bf16[16,224,128]{2,1,0:T(8,128)(2,1)S(1)} async-done(((bf16[16,224,128]{2,1,0:T(8,128)(2,1)}), bf16[16,224,128]{2,1,0:T(8,128)(2,1)S(1)}, u32[]{:S(2)}, u32[]{:S(2)}) %all-to-all-start.1) | async-done | bytes 917536 | tf_op jit(solution)/shard_map/all_to_all | solution.py:651
  100.9 0.1 slice.19
  100.9 0.8 pad_maximum_fusion.1
  101.7 1.5 %collective-permute-done.15.other_ref = bf16[3584,128]{1,0:T(8,128)(2,1)S(1)} collective-permute-done((bf16[3584,128]{1,0:T(8,128)(2,1)S(1)}, bf16[3584,128]{1,0:T(8,128)(2,1)S(1)}, u32[]{:S(2)}, u32[]{:S(2)}) %collective-permute-start.15) | collective-permute-done | bytes 917536 | tf_op jit(solution)/shard_map/ppermute | solution.py:625
  103.2 2.1 %shard_map.209 = (f32[2,192,576]{2,1,0:T(8,128)}, f32[2,192,192]{2,1,0:T(8,128)}, f32[2,192,768]{2,1,0:T(8,128)}, f32[2,192,768]{2,1,0:T(8,128)}, f32[2,2,192]{2,1,0:T(2,128)}, /*index=5*/f32[12,1,3312]{2,1,0:T(1,128)}) custom-call(bf16[3584,128]{1,0:T(8,128)(2,1)S(1)} %bitcast.11, bf16[3584,128]{1,0:T(8,128)(2,1)S(1)} %collective-permute-done.15.other_ref, ...), custom_call_target="tpu_custom_call" | custom-call | flops 2200000000 | bytes 5961984 | tf_op jit(solution)/shard_map/pallas_call | solution.py:574
  (35 shorter events, 0.2 us)
Async XLA Ops:
  0.6 6.6 %copy-start = (bf16[2,192,768]{2,1,0:T(8,128)(2,1)S(1)}, bf16[2,192,768]{2,1,0:T(8,128)(2,1)}, u32[]{:S(2)}) copy-start(bf16[2,192,768]{2,1,0:T(8,128)(2,1)} %up_ref.5) | copy-start | bytes 1769476
  0.6 6.6 %copy-start.1 = (bf16[2,768,192]{1,2,0:T(8,128)(2,1)S(1)}, bf16[2,768,192]{1,2,0:T(8,128)(2,1)}, u32[]{:S(2)}) copy-start(bf16[2,768,192]{1,2,0:T(8,128)(2,1)} %param.20) | copy-start | bytes 1769476
  0.7 6.6 %copy-start.3 = (bf16[6,48,384]{2,1,0:T(8,128)(2,1)S(1)}, bf16[6,48,384]{2,1,0:T(8,128)(2,1)}, u32[]{:S(2)}) copy-start(bf16[6,48,384]{2,1,0:T(8,128)(2,1)} %param.15) | copy-start | bytes 663556
  0.7 6.6 %copy-start.6 = (f32[2,2,192]{2,1,0:T(2,128)S(1)}, f32[2,2,192]{2,1,0:T(2,128)}, u32[]{:S(2)}) copy-start(f32[2,2,192]{2,1,0:T(2,128)} %gains_ref.7) | copy-start | bytes 9220
  0.7 6.6 %copy-start.7 = (bf16[576,288]{1,0:T(8,128)(2,1)S(1)}, bf16[576,288]{1,0:T(8,128)(2,1)}, u32[]{:S(2)}) copy-start(bf16[576,288]{1,0:T(8,128)(2,1)} %constant.14.clone.far_pick.pick_ref) | copy-start | bytes 995332
  0.7 6.6 %copy-start.12 = (bf16[64,288]{1,0:T(8,128)(2,1)S(1)}, bf16[64,288]{1,0:T(8,128)(2,1)}, u32[]{:S(2)}) copy-start(bf16[64,288]{1,0:T(8,128)(2,1)} %constant.17.clone.strips_ref) | copy-start | bytes 110596
  7.3 11.8 %copy-start.5 = (f32[2,1,6,3312]{3,1,2,0:T(1,128)S(1)}, f32[2,1,6,3312]{3,1,2,0:T(1,128)}, u32[]{:S(2)}) copy-start(f32[2,1,6,3312]{3,1,2,0:T(1,128)} %param.21) | copy-start | bytes 476932
  7.3 11.8 %copy-start.10 = (bf16[2,138,276]{2,1,0:T(8,128)(2,1)S(1)}, bf16[2,138,276]{2,1,0:T(8,128)(2,1)}, u32[]{:S(2)}) copy-start(bf16[2,138,276]{2,1,0:T(8,128)(2,1)} %constant.13.clone.far_tcols.tcols_ref) | copy-start | bytes 457060
  7.3 11.8 %copy-start.11 = (bf16[2,96,192]{2,1,0:T(8,128)(2,1)S(1)}, bf16[2,96,192]{2,1,0:T(8,128)(2,1)}, u32[]{:S(2)}) copy-start(bf16[2,96,192]{2,1,0:T(8,128)(2,1)} %constant.12.clone.far_trows.trows_ref) | copy-start | bytes 221188
  9.9 12.7 %copy-start.2 = (bf16[2,192,576]{2,1,0:T(8,128)(2,1)S(1)}, bf16[2,192,576]{2,1,0:T(8,128)(2,1)}, u32[]{:S(2)}) copy-start(bf16[2,192,576]{2,1,0:T(8,128)(2,1)} %qkv_ref.3) | copy-start | bytes 1327108
  9.9 12.7 %copy-start.4 = (bf16[2,192,192]{2,1,0:T(8,128)(2,1)S(1)}, bf16[2,192,192]{2,1,0:T(8,128)(2,1)}, u32[]{:S(2)}) copy-start(bf16[2,192,192]{2,1,0:T(8,128)(2,1)} %out_ref.3) | copy-start | bytes 442372
  9.9 12.7 %copy-start.9 = (bf16[576,352]{1,0:T(8,128)(2,1)S(1)}, bf16[576,352]{1,0:T(8,128)(2,1)}, u32[]{:S(2)}) copy-start(bf16[576,352]{1,0:T(8,128)(2,1)} %constant.15.clone.pick_ref) | copy-start | bytes 1216516
  9.9 12.6 %collective-permute-start = (bf16[288,384]{1,0:T(8,128)(2,1)S(1)}, bf16[288,384]{1,0:T(8,128)(2,1)S(1)}, u32[]{:S(2)}, u32[]{:S(2)}) collective-permute-start(bf16[288,384]{1,0:T(8,128)(2,1)S(1)} %get-tuple-element.89), channel_id=1, source_target_pairs={{8,0},{9,1},{10,2},{11,3},{12,4},{13,5},{14,6},{15,7},{16,8},{17,9... | collective-permute-start | bytes 663560 | tf_op jit(solution)/shard_map/ppermute | solution.py:597
  15.8 5.0 %collective-permute-start.1 = (bf16[64,384]{1,0:T(8,128)(2,1)S(1)}, bf16[64,384]{1,0:T(8,128)(2,1)S(1)}, u32[]{:S(2)}, u32[]{:S(2)}) collective-permute-start(bf16[64,384]{1,0:T(8,128)(2,1)S(1)} %get-tuple-element.90), channel_id=1, source_target_pairs={{1,0},{2,1},{3,2},{4,3},{5,4},{6,5},{7,6},{0,7},{9,8},{10,9},{11,1... | collective-permute-start | bytes 147464 | tf_op jit(solution)/shard_map/ppermute | solution.py:598
  19.0 3.5 %collective-permute-start.2 = (bf16[64,384]{1,0:T(8,128)(2,1)S(1)}, bf16[64,384]{1,0:T(8,128)(2,1)S(1)}, u32[]{:S(2)}, u32[]{:S(2)}) collective-permute-start(bf16[64,384]{1,0:T(8,128)(2,1)S(1)} %get-tuple-element.91), channel_id=1, source_target_pairs={{9,0},{10,1},{11,2},{12,3},{13,4},{14,5},{15,6},{8,7},{17,8},{18,9... | collective-permute-start | bytes 147464 | tf_op jit(solution)/shard_map/ppermute | solution.py:599
  31.9 10.8 %collective-permute-start.5 = (bf16[288,384]{1,0:T(8,128)(2,1)S(1)}, bf16[288,384]{1,0:T(8,128)(2,1)S(1)}, u32[]{:S(2)}, u32[]{:S(2)}) collective-permute-start(bf16[288,384]{1,0:T(8,128)(2,1)S(1)} %get-tuple-element.95), channel_id=1, source_target_pairs={{120,0},{121,1},{122,2},{123,3},{124,4},{125,5},{126,6},{127,7},{0... | collective-permute-start | bytes 663560 | tf_op jit(solution)/shard_map/ppermute | solution.py:597
  32.0 6.8 %collective-permute-start.4 = (bf16[64,384]{1,0:T(8,128)(2,1)S(1)}, bf16[64,384]{1,0:T(8,128)(2,1)S(1)}, u32[]{:S(2)}, u32[]{:S(2)}) collective-permute-start(bf16[64,384]{1,0:T(8,128)(2,1)S(1)} %get-tuple-element.94), channel_id=1, source_target_pairs={{7,0},{0,1},{1,2},{2,3},{3,4},{4,5},{5,6},{6,7},{15,8},{8,9},{9,10... | collective-permute-start | bytes 147464 | tf_op jit(solution)/shard_map/ppermute | solution.py:598
  32.2 10.5 %collective-permute-start.3 = (bf16[64,384]{1,0:T(8,128)(2,1)S(1)}, bf16[64,384]{1,0:T(8,128)(2,1)S(1)}, u32[]{:S(2)}, u32[]{:S(2)}) collective-permute-start(bf16[64,384]{1,0:T(8,128)(2,1)S(1)} %get-tuple-element.93), channel_id=1, source_target_pairs={{127,0},{120,1},{121,2},{122,3},{123,4},{124,5},{125,6},{126,7},{7... | collective-permute-start | bytes 147464 | tf_op jit(solution)/shard_map/ppermute | solution.py:599
  32.4 10.3 %copy-start.8 = (bf16[576,352]{1,0:T(8,128)(2,1)S(1)}, bf16[576,352]{1,0:T(8,128)(2,1)}, u32[]{:S(2)}) copy-start(bf16[576,352]{1,0:T(8,128)(2,1)} %constant.16.clone.returned_ref) | copy-start | bytes 1216516
  44.9 4.4 %collective-permute-start.6 = (bf16[1728,128]{1,0:T(8,128)(2,1)S(1)}, bf16[1728,128]{1,0:T(8,128)(2,1)S(1)}, u32[]{:S(2)}, u32[]{:S(2)}) collective-permute-start(bf16[1728,128]{1,0:T(8,128)(2,1)S(1)} %get-tuple-element.113), channel_id=1, source_target_pairs={{8,0},{9,1},{10,2},{11,3},{12,4},{13,5},{14,6},{15,7},{0,8},{1,9},... | collective-permute-start | bytes 1327112 | tf_op jit(solution)/shard_map/ppermute | solution.py:625
  49.3 2.0 %collective-permute-start.7 = (bf16[1856,128]{1,0:T(8,128)(2,1)S(1)}, bf16[1856,128]{1,0:T(8,128)(2,1)S(1)}, u32[]{:S(2)}, u32[]{:S(2)}) collective-permute-start(bf16[1856,128]{1,0:T(8,128)(2,1)S(1)} %get-tuple-element.130), channel_id=1, source_target_pairs={{8,0},{9,1},{10,2},{11,3},{12,4},{13,5},{14,6},{15,7},{0,8},{1,9},... | collective-permute-start | bytes 1425416 | tf_op jit(solution)/shard_map/ppermute | solution.py:625
  52.5 21.3 %all-to-all-start = ((bf16[16,224,128]{2,1,0:T(8,128)(2,1)}), bf16[16,224,128]{2,1,0:T(8,128)(2,1)S(1)}, u32[]{:S(2)}, u32[]{:S(2)}) async-start(bf16[16,224,128]{2,1,0:T(8,128)(2,1)} %bitcast.6), calls=%async_computation | async-start | bytes 1835008 | tf_op jit(solution)/shard_map/all_to_all | solution.py:642
  57.7 8.7 %collective-permute-start.8 = (bf16[416,128]{1,0:T(8,128)(2,1)S(1)}, bf16[416,128]{1,0:T(8,128)(2,1)S(1)}, u32[]{:S(2)}, u32[]{:S(2)}) collective-permute-start(bf16[416,128]{1,0:T(8,128)(2,1)S(1)} %get-tuple-element.144.mine_ref), channel_id=1, source_target_pairs={{1,0},{0,1},{3,2},{2,3},{5,4},{4,5},{7,6},{6,7},{9,8},{8,9},{11,10... | collective-permute-start | bytes 319496 | tf_op jit(solution)/shard_map/ppermute | solution.py:625
  73.9 4.2 %collective-permute-start.9 = (bf16[224,128]{1,0:T(8,128)(2,1)S(1)}, bf16[224,128]{1,0:T(8,128)(2,1)S(1)}, u32[]{:S(2)}, u32[]{:S(2)}) collective-permute-start(bf16[224,128]{1,0:T(8,128)(2,1)S(1)} %shard_map.206.refs_0_), channel_id=1, source_target_pairs={{2,0},{3,1},{4,2},{5,3},{6,4},{7,5},{0,6},{1,7},{10,8},{11,9},{12,... | collective-permute-start | bytes 172040 | tf_op jit(solution)/shard_map/ppermute | solution.py:625
  75.0 5.9 %collective-permute-start.10 = (bf16[224,128]{1,0:T(8,128)(2,1)S(1)}, bf16[224,128]{1,0:T(8,128)(2,1)S(1)}, u32[]{:S(2)}, u32[]{:S(2)}) collective-permute-start(bf16[224,128]{1,0:T(8,128)(2,1)S(1)} %shard_map.206.refs_0_), channel_id=1, source_target_pairs={{4,0},{5,1},{6,2},{7,3},{0,4},{1,5},{2,6},{3,7},{12,8},{13,9},{14,... | collective-permute-start | bytes 172040 | tf_op jit(solution)/shard_map/ppermute | solution.py:625
  75.0 6.3 %collective-permute-start.11 = (bf16[224,128]{1,0:T(8,128)(2,1)S(1)}, bf16[224,128]{1,0:T(8,128)(2,1)S(1)}, u32[]{:S(2)}, u32[]{:S(2)}) collective-permute-start(bf16[224,128]{1,0:T(8,128)(2,1)S(1)} %shard_map.206.refs_0_), channel_id=1, source_target_pairs={{6,0},{7,1},{0,2},{1,3},{2,4},{3,5},{4,6},{5,7},{14,8},{15,9},{8,1... | collective-permute-start | bytes 172040 | tf_op jit(solution)/shard_map/ppermute | solution.py:625
  82.3 18.5 %all-to-all-start.1 = ((bf16[16,224,128]{2,1,0:T(8,128)(2,1)}), bf16[16,224,128]{2,1,0:T(8,128)(2,1)S(1)}, u32[]{:S(2)}, u32[]{:S(2)}) async-start(bf16[16,224,128]{2,1,0:T(8,128)(2,1)} %shard_map.207), calls=%async_computation.1 | async-start | bytes 1835008 | tf_op jit(solution)/shard_map/all_to_all | solution.py:651
  86.4 4.8 %collective-permute-start.12 = (bf16[416,128]{1,0:T(8,128)(2,1)S(1)}, bf16[416,128]{1,0:T(8,128)(2,1)S(1)}, u32[]{:S(2)}, u32[]{:S(2)}) collective-permute-start(bf16[416,128]{1,0:T(8,128)(2,1)S(1)} %shard_map.208.t0_ref), channel_id=1, source_target_pairs={{2,0},{3,1},{4,2},{5,3},{6,4},{7,5},{0,6},{1,7},{10,8},{11,9},{12,... | collective-permute-start | bytes 319496 | tf_op jit(solution)/shard_map/ppermute | solution.py:625
  87.9 6.3 %collective-permute-start.13 = (bf16[416,128]{1,0:T(8,128)(2,1)S(1)}, bf16[416,128]{1,0:T(8,128)(2,1)S(1)}, u32[]{:S(2)}, u32[]{:S(2)}) collective-permute-start(bf16[416,128]{1,0:T(8,128)(2,1)S(1)} %shard_map.208.t0_ref), channel_id=1, source_target_pairs={{4,0},{5,1},{6,2},{7,3},{0,4},{1,5},{2,6},{3,7},{12,8},{13,9},{14,... | collective-permute-start | bytes 319496 | tf_op jit(solution)/shard_map/ppermute | solution.py:625
  88.8 6.4 %collective-permute-start.14 = (bf16[416,128]{1,0:T(8,128)(2,1)S(1)}, bf16[416,128]{1,0:T(8,128)(2,1)S(1)}, u32[]{:S(2)}, u32[]{:S(2)}) collective-permute-start(bf16[416,128]{1,0:T(8,128)(2,1)S(1)} %shard_map.208.t0_ref), channel_id=1, source_target_pairs={{6,0},{7,1},{0,2},{1,3},{2,4},{3,5},{4,6},{5,7},{14,8},{15,9},{8,1... | collective-permute-start | bytes 319496 | tf_op jit(solution)/shard_map/ppermute | solution.py:625
  100.8 2.5 %collective-permute-start.15 = (bf16[3584,128]{1,0:T(8,128)(2,1)S(1)}, bf16[3584,128]{1,0:T(8,128)(2,1)S(1)}, u32[]{:S(2)}, u32[]{:S(2)}) collective-permute-start(bf16[3584,128]{1,0:T(8,128)(2,1)S(1)} %bitcast.10), channel_id=1, source_target_pairs={{8,0},{9,1},{10,2},{11,3},{12,4},{13,5},{14,6},{15,7},{0,8},{1,9},... | collective-permute-start | bytes 2752520 | tf_op jit(solution)/shard_map/ppermute | solution.py:625

commit v6 on v5

--- a/solution.py
+++ b/solution.py
@@ -147,12 +147,8 @@
 
 
 def gelu_parts(x):
-    bell = jnp.exp2(x * x * (-0.5 * LOG2E))
-    t = 1.0 / (1.0 + (0.3275911 * math.sqrt(0.5)) * jnp.abs(x))
-    poly = t * (0.254829592 + t * (-0.284496736 + t * (1.421413741 + t * (-1.453152027 + t * 1.061405429))))
-    tail = 0.5 * poly * bell
-    below = jnp.where(x >= 0, 1.0 - tail, tail)
-    return below, bell * (1.0 / math.sqrt(2.0 * math.pi))
+    below = 0.5 + 0.5 * lax.erf(x * math.sqrt(0.5))
+    return below, jnp.exp2(x * x * (-0.5 * LOG2E)) * (1.0 / math.sqrt(2.0 * math.pi))
 
 
 def head_rows():
@@ -274,7 +270,7 @@
 
 
 def attention_backward_part(
-    x, gain, qkv_ref, out_ref, ghid, q_ref, k_ref, v_ref, probs_ref, ctx_ref, gctx_ref, dq_ref, dk_ref, dv_ref, grad_ref, masks
+    hat, inv, gain, qkv_ref, out_ref, ghid, q_ref, k_ref, v_ref, probs_ref, ctx_ref, gctx_ref, dq_ref, dk_ref, dv_ref, grad_ref, masks
 ):
     gbranch = ghid.astype(BF16)
     gctx_ref[...] = nt(gbranch, out_ref[...]).astype(BF16)
@@ -283,11 +279,9 @@
     gnormed += nt(dk_ref[...], qkv_ref[:, DIM : 2 * DIM])
     gnormed += nt(dv_ref[...], qkv_ref[:, 2 * DIM :])
     gnormed = gnormed.astype(BF16).astype(F32)
-    hat, inv = normalize(x)
     gain_grad = jnp.sum(gnormed * hat, axis=0, keepdims=True)
     gblock = norm_backward(gnormed, gain, hat, inv) + ghid
-    normed = (hat * gain).astype(BF16)
-    return gblock, normed, gbranch, gain_grad
+    return gblock, gbranch, gain_grad
 
 
 def first_attention(
@@ -378,15 +372,17 @@
     gains_ref, qkv_ref, out_ref, up_ref, down_ref, pick_ref,
     back_own_ref, y_own_ref, sent_row_ref, sent_side_ref, sent_corner_ref,
     g_ref, normed_ref, dq_ref, dk_ref, dv_ref, ctx_ref, gbranch_ref, normed_mlp_ref, gpre_ref, expanded_ref, grad_ref, gain_grad_ref,
-    source_ref, x_ref, q_ref, k_ref, v_ref, probs_ref, gctx_ref,
+    source_ref, x_ref, hat_ref, q_ref, k_ref, v_ref, probs_ref, gctx_ref,
 ):
     masks = head_rows()
     fill_source(source_ref, own_ref[...], row_ref, side_ref, corner_ref, 0)
     x_ref[...] = gather_tokens(pick_ref[...], source_ref[...])
     fill_source(source_ref, cot_ref[144:288, :], row_ref, side_ref, corner_ref, 1)
     g_ref[...] = gather_tokens(pick_ref[...], source_ref[...]).astype(BF16)
-    hat, _ = normalize(x_ref[...])
-    project((hat * gains_ref[0:1, :]).astype(BF16), qkv_ref, q_ref, k_ref, v_ref)
+    hat, inv = normalize(x_ref[...])
+    normed_ref[...] = (hat * gains_ref[0:1, :]).astype(BF16)
+    hat_ref[...] = hat
+    project(normed_ref[...], qkv_ref, q_ref, k_ref, v_ref)
     attention(q_ref, k_ref, v_ref, bias_ref, probs_ref, ctx_ref, masks)
     branch = nn(ctx_ref[...], out_ref[...]).astype(BF16)
     hidden = x_ref[...] + branch.astype(F32)
@@ -411,14 +407,13 @@
     gnormed = gnormed.astype(BF16).astype(F32)
     gain_grad_ref[1:2, :] = jnp.sum(gnormed * hat_mlp, axis=0, keepdims=True)
     ghid = g_ref[...].astype(F32) + norm_backward(gnormed, gains_ref[1:2, :], hat_mlp, inv_mlp)
-    gblock, normed, gbranch, gain_grad = attention_backward_part(
-        x_ref[...], gains_ref[0:1, :], qkv_ref, out_ref, ghid,
+    gblock, gbranch, gain_grad = attention_backward_part(
+        hat_ref[...], inv, gains_ref[0:1, :], qkv_ref, out_ref, ghid,
         q_ref, k_ref, v_ref, probs_ref, ctx_ref, gctx_ref, dq_ref, dk_ref, dv_ref, grad_ref, masks,
     )
     gain_grad_ref[0:1, :] = gain_grad
     back = scatter_tokens(pick_ref[...], gblock.astype(BF16)).astype(BF16)
     put_source(back_own_ref, sent_row_ref, sent_side_ref, sent_corner_ref, 0, back)
-    normed_ref[...] = normed
     gbranch_ref[...] = gbranch
 
 
@@ -434,16 +429,26 @@
     split_halves(wbuf_ref, mine_ref, theirs_ref, sems)
 
 
+def first_norms(xw_ref, hidden_ref, gains_ref, hat_ref, inv_ref, normed_ref, hat_mlp_ref, inv_mlp_ref, normed_mlp_ref):
+    hat, inv = normalize(xw_ref[...].astype(F32))
+    hat_ref[...] = hat
+    inv_ref[...] = inv
+    normed_ref[...] = (hat * gains_ref[0:1, :]).astype(BF16)
+    hat, inv = normalize(hidden_ref[...])
+    hat_mlp_ref[...] = hat
+    inv_mlp_ref[...] = inv
+    normed_mlp_ref[...] = (hat * gains_ref[1:2, :]).astype(BF16)
+
+
 def first_mlp_back(
-    back_ref, row_ref, side_ref, corner_ref, hidden_ref, slope_ref, gains_ref, up_ref, down_ref, returned_ref,
-    g_ref, ghid_ref, normed_mlp_ref, gpre_ref, gain_grad_ref, source_ref,
+    back_ref, row_ref, side_ref, corner_ref, hat_mlp_ref, inv_mlp_ref, slope_ref, gains_ref, up_ref, down_ref, returned_ref,
+    g_ref, ghid_ref, gpre_ref, gain_grad_ref, source_ref,
 ):
     fill_source(source_ref, back_ref[...], row_ref, side_ref, corner_ref, 0)
     g32 = gather_tokens(returned_ref[...], source_ref[...])
     g = g32.astype(BF16)
     g_ref[...] = g
-    hat_mlp, inv_mlp = normalize(hidden_ref[...])
-    normed_mlp_ref[...] = (hat_mlp * gains_ref[1:2, :]).astype(BF16)
+    hat_mlp, inv_mlp = hat_mlp_ref[...], inv_mlp_ref[...]
     gnormed = jnp.zeros((TOKENS, DIM), F32)
     for j in range(3):
         cols = slice(j * 256, (j + 1) * 256)
@@ -457,19 +462,19 @@
 
 
 def first_attention_back(
-    ghid_ref, g_ref, normed_mlp_ref, gpre_ref, mlp_gain_ref, xw_ref, q_ref, k_ref, v_ref, probs_ref, ctx_ref, expanded_ref,
+    ghid_ref, g_ref, gpre_ref, mlp_gain_ref, hat_ref, inv_ref, normed_ref, normed_mlp_ref, q_ref, k_ref, v_ref, probs_ref, ctx_ref, expanded_ref,
     gains_ref, qkv_ref, out_ref, last_gain_ref,
     gblock_ref, grad_ref, mine_ref, theirs_ref,
     gctx_ref, dq_ref, dk_ref, dv_ref, wbuf_ref, sems,
 ):
     masks = head_rows()
-    gblock, normed, gbranch, gain_grad = attention_backward_part(
-        xw_ref[...].astype(F32), gains_ref[0:1, :], qkv_ref, out_ref, ghid_ref[...],
+    gblock, gbranch, gain_grad = attention_backward_part(
+        hat_ref[...], inv_ref[...], gains_ref[0:1, :], qkv_ref, out_ref, ghid_ref[...],
         q_ref, k_ref, v_ref, probs_ref, ctx_ref, gctx_ref, dq_ref, dk_ref, dv_ref, grad_ref, masks,
     )
     gblock_ref[...] = gblock.astype(BF16)
     weight_grads(
-        wbuf_ref, normed, dq_ref[...], dk_ref[...], dv_ref[...], ctx_ref[...], gbranch,
+        wbuf_ref, normed_ref[...], dq_ref[...], dk_ref[...], dv_ref[...], ctx_ref[...], gbranch,
         normed_mlp_ref[...], gpre_ref, expanded_ref, g_ref[...],
     )
     gains = jnp.concatenate([gain_grad, mlp_gain_ref[...], last_gain_ref[0:1, :], last_gain_ref[1:2, :]], axis=1)
@@ -642,11 +647,10 @@
     parts = lax.all_to_all(sent.reshape(16, CHUNK, 128), both, 0, 0, axis_index_groups=groups)
     outs = [((GRID, 2 * DIM), BF16), ((2 * TROWS, 128), BF16)]
     grad_inputs, tables = call(first_finish, finish, [whole(a) for a in finish], outs)
-    other = moved(tables, z_lo=1)
-    parts, other = lax.optimization_barrier((parts, other))
-    tables = run(add_two, [tables, other], tables.shape)
+    parts, tables = lax.optimization_barrier((parts, tables))
     total = run(sum_parts, [parts], (CHUNK, 128))
     spread = run(sum_and_spread, [total] + [moved(total, x=k) for k in (1, 2, 3)], (16, CHUNK, 128))
+    tables = run(add_two, [tables, moved(tables, z_lo=1)], tables.shape)
     spread, tables = lax.optimization_barrier((spread, tables))
     half = lax.all_to_all(spread, both, 0, 0, axis_index_groups=groups)
     table_terms = [tables] + [moved(tables, x=k) for k in (1, 2, 3)]
@@ -705,15 +709,20 @@
     outs = [wide_hid, wide_hid, ((144, 2 * DIM), BF16)] + strip_outs
     results = call(first_mlp, operands, specs_for(operands, 0), outs, (), 4, mebibytes=14)
     expanded, slope, bottom, *sent = results
-    sent, bias_table = lax.optimization_barrier((sent, bias_table))
+    sent, bias_table, xw = lax.optimization_barrier((sent, bias_table, xw))
 
     arrived = exchange(*sent, sizes, 1)
     operands = [bias_table, trows, tcols]
     [bias_last] = call(second_bias, operands, specs_for(operands, 1), [(bias, F32)], (), 2, mebibytes=14)
 
+    operands = [xw, hidden, gains]
+    norm_outs = [(tok, F32), ((TOKENS, 1), F32), wide_tok]
+    norms = call(first_norms, operands, specs_for(operands, 0), norm_outs * 2, (), 1, mebibytes=14)
+    hat, inv, normed_first, hat_mlp, inv_mlp, normed_mlp = norms
+
     operands = [bottom, *arrived, cot, bias_last, *weights, pick_shift]
     outs = [((144, 2 * DIM), BF16)] * 2 + strip_outs + [wide_tok] * 8 + [wide_hid] * 2 + [(bias, F32), ((2, DIM), F32)]
-    scratch = [vmem(src, BF16), vmem(tok, F32)] + [vmem(tok, BF16)] * 3 + [vmem(probs, BF16), vmem(tok, BF16)]
+    scratch = [vmem(src, BF16), vmem(tok, F32), vmem(tok, F32)] + [vmem(tok, BF16)] * 3 + [vmem(probs, BF16), vmem(tok, BF16)]
     results = call(second_both, operands, specs_for(operands, 1), outs, scratch, 12, mebibytes=14)
     back_own, y_own, sent, terms, last_gain = results[0], results[1], results[2:5], results[5:16], results[16]
 
@@ -726,14 +735,14 @@
     results = call(second_weights, operands, specs_for(operands, 1), outs, scratch, 4, out_specs, 14)
     last_mine, last_theirs, last_table = results
 
-    operands = [back_own, *arrived, hidden, slope, gains, up, down, pick_back]
-    outs = [wide_tok, (tok, F32), wide_tok, wide_hid, ((1, DIM), F32)]
+    operands = [back_own, *arrived, hat_mlp, inv_mlp, slope, gains, up, down, pick_back]
+    outs = [wide_tok, (tok, F32), wide_hid, ((1, DIM), F32)]
     results = call(first_mlp_back, operands, specs_for(operands, 0), outs, [vmem(src, BF16)], 3, mebibytes=14)
-    g, ghid, normed_mlp, gpre, mlp_gain = results
+    g, ghid, gpre, mlp_gain = results
     ghid, last_theirs = lax.optimization_barrier((ghid, last_theirs))
     last = [last_mine, moved(last_theirs, core=1)]
 
-    operands = [ghid, g, normed_mlp, gpre, mlp_gain, xw, q, k, v, probs_first, ctx, expanded, gains, qkv, out]
+    operands = [ghid, g, gpre, mlp_gain, hat, inv, normed_first, normed_mlp, q, k, v, probs_first, ctx, expanded, gains, qkv, out]
     operands += [last_gain]
     first_shape = (PART + EXTRA, 128)
     outs = [wide_tok, (bias, F32), (first_shape, BF16), (first_shape, BF16)]

time: 107 us -> 104 us (0.972)
  Pallas kernels: 33.9 us -> 32.6 us
    all_to_all x1, waiting for transfers between devices: 7.31 us -> 16 us  [sum_over_devices(): lax.all_to_all(sent.reshape(16, CHUNK, 128), both, 0, 0, axis_index_group...]
    ppermute x10, waiting for transfers between devices: 21 us -> 12.7 us  [moved(): return lax.ppermute(array, ('lat', 'lon'), shifted_pairs(**steps))]
    pallas_call x13 -> x14, Pallas kernels: 33.9 us -> 32.6 us  [call(): pl.pallas_call(kernel, grid=(1,), out_shape=shapes, in_specs=specs, out_s...]
  transfers between devices with their start and end apart: 18 -> 18, of which waited for: 15 -> 14; matrix products, arithmetic and copies ran while one was open for 1% -> 1% of each run, Pallas kernels for 9% -> 10%
where the time goes in v6:
time: 104 us; the launch traced here: 103 us
  waiting for transfers between devices  43.7 us (42%)
  Pallas kernels  32.6 us (31%)
  starting transfers between devices  24.8 us (24%)
    pallas_call x14, Pallas kernels, call(): pl.pallas_call(kernel, grid=(1,), out_shape=shapes, in_specs=specs, out_s...  32.6 us
    all_to_all x1, waiting for transfers between devices, sum_over_devices(): lax.all_to_all(sent.reshape(16, CHUNK, 128), both, 0, 0, axis_index_group...  16 us
    ppermute x10, waiting for transfers between devices, moved(): return lax.ppermute(array, ('lat', 'lon'), shifted_pairs(**steps))  12.7 us
    ppermute x10, starting transfers between devices, moved(): return lax.ppermute(array, ('lat', 'lon'), shifted_pairs(**steps))  7.31 us
    ppermute x2, starting transfers between devices, exchange(): rows = lax.ppermute(rows, both, neighbour(sizes, (step, 0)))  5.98 us
    ppermute x2, waiting for transfers between devices, exchange(): corner = lax.ppermute(corner, both, neighbour(sizes, (step, step)))  5.58 us
    all_to_all x1, waiting for transfers between devices, sum_over_devices(): half = lax.all_to_all(spread, both, 0, 0, axis_index_groups=groups)  5.31 us
    ppermute x2, starting transfers between devices, exchange(): side = lax.ppermute(side, both, neighbour(sizes, (0, step)))  4.24 us
  transfers between devices with their start and end apart: 18, of which 14 were waited for; matrix products, arithmetic and copies ran while one was open for 1% of the time, Pallas kernels for 10%

profile of v6, /device:TPU:0, one launch (start us, length us, event | category | flops | bytes accessed | tf_op | source)
XLA Modules:
  0.0 103.0 jit_solution(3404798298133495239)
XLA Ops:
  0.7 0.0 copy-start.7
  0.7 0.0 copy-start.12
  0.7 6.5 %shard_map.197 = (bf16[576,192]{1,0:T(8,128)(2,1)S(1)}, bf16[576,192]{1,0:T(8,128)(2,1)S(1)}, bf16[576,192]{1,0:T(8,128)(2,1)S(1)}, bf16[576,192]{1,0:T(8,128)(2...) custom-call(bf16[288,384]{1,0:T(8,128)(2,1)} %bitcast.20, ...), custom_call_target="tpu_custom_call" | custom-call | flops 7699999744 | bytes 4074528 | tf_op jit(solution)/shard_map/pallas_call | solution.py:579
  7.3 0.0 copy-start.10
  7.3 0.0 copy-start.11
  7.3 1.8 %shard_map.198 = (bf16[576,768]{1,0:T(8,128)(2,1)S(1)}, bf16[576,768]{1,0:T(8,128)(2,1)S(1)}, bf16[144,384]{1,0:T(8,128)(2,1)S(1)}, bf16[288,384]{1,0:T(8,128)(2...) custom-call(f32[576,192]{1,0:T(8,128)S(1)} %get-tuple-element.90.hidden_ref, ...), custom_call_target="tpu_custom_call" | custom-call | flops 4400000000 | bytes 4414464 | tf_op jit(solution)/shard_map/pallas_call | solution.py:579
  9.1 5.9 %collective-permute-start = (bf16[288,384]{1,0:T(8,128)(2,1)S(1)}, bf16[288,384]{1,0:T(8,128)(2,1)S(1)}, u32[]{:S(2)}, u32[]{:S(2)}) collective-permute-start(bf16[288,384]{1,0:T(8,128)(2,1)S(1)} %get-tuple-element.96), channel_id=1, source_target_pairs={{8,0},{9,1},{10,2},{11,3},{12,4},{13,5},{14,6},{15,7},{16,8},{17,9... | collective-permute-start | bytes 663560 | tf_op jit(solution)/shard_map/ppermute | solution.py:602
  15.0 3.2 %collective-permute-start.1 = (bf16[64,384]{1,0:T(8,128)(2,1)S(1)}, bf16[64,384]{1,0:T(8,128)(2,1)S(1)}, u32[]{:S(2)}, u32[]{:S(2)}) collective-permute-start(bf16[64,384]{1,0:T(8,128)(2,1)S(1)} %get-tuple-element.97), channel_id=1, source_target_pairs={{1,0},{2,1},{3,2},{4,3},{5,4},{6,5},{7,6},{0,7},{9,8},{10,9},{11,1... | collective-permute-start | bytes 147464 | tf_op jit(solution)/shard_map/ppermute | solution.py:603
  18.2 1.1 %shard_map.199.bias_ref = f32[144,864]{1,0:T(8,128)S(1)} custom-call(f32[12,1,3312]{2,1,0:T(1,128)S(1)} %bitcast.18, bf16[2,96,192]{2,1,0:T(8,128)(2,1)S(1)} %copy-done.11, bf16[2,138,276]{2,1,0:T(8,128)(2,1)S(1)} %copy-done.10), custom_call_target="tpu_custom_call" | custom-call | flops 2200000000 | bytes 882720 | tf_op jit(solution)/shard_map/pallas_call | solution.py:579
  19.4 0.0 copy-start.9
  19.4 0.4 shard_map.202
  19.9 0.1 collective-permute-done.1.side_ref
  20.0 1.7 %collective-permute-done.2.corner_ref = bf16[64,384]{1,0:T(8,128)(2,1)S(1)} collective-permute-done((bf16[64,384]{1,0:T(8,128)(2,1)S(1)}, bf16[64,384]{1,0:T(8,128)(2,1)S(1)}, u32[]{:S(2)}, u32[]{:S(2)}) %collective-permute-start.2) | collective-permute-done | bytes 49184 | tf_op jit(solution)/shard_map/ppermute | solution.py:604
  21.8 8.5 %shard_map.200 = (bf16[144,384]{1,0:T(8,128)(2,1)S(1)}, bf16[144,384]{1,0:T(8,128)(2,1)S(1)}, bf16[288,384]{1,0:T(8,128)(2,1)S(1)}, bf16[64,384]{1,0:T(8,128)(2,...) custom-call(bf16[144,384]{1,0:T(8,128)(2,1)S(1)} %get-tuple-element., ...), custom_call_target="tpu_custom_call" | custom-call | flops 13200000000 | bytes 7905792 | tf_op jit(solution)/shard_map/pallas_call | solution.py:579
  30.2 0.1 collective-permute-start.5
  30.3 1.0 collective-permute-start.4
  31.3 1.9 %shard_map.201 = (bf16[1728,128]{1,0:T(8,128)(2,1)S(1)}, bf16[1728,128]{1,0:T(8,128)(2,1)S(1)}, bf16[208,128]{1,0:T(8,128)(2,1)S(1)}) custom-call(bf16[576,192]{1,0:T(8,128)(2,1)S(1)} %get-tuple-element.104.normed_ref, bf16[576,192]{1,0:T(8,128)(2,1)S(1)} %get-tuple-element.105.dq_ref, bf16[576,192]{1,0:T(8,128)(2,1)S(1)} %get-tuple-element.106.dk_ref, ...), custom_call_target="tpu_custom_call" | custom-call | flops 4400000000 | bytes 5200672 | tf_op jit(solution)/shard_map/pallas_call | solution.py:579
  33.3 3.9 %collective-permute-done.4.side_ref = bf16[64,384]{1,0:T(8,128)(2,1)S(1)} collective-permute-done((bf16[64,384]{1,0:T(8,128)(2,1)S(1)}, bf16[64,384]{1,0:T(8,128)(2,1)S(1)}, u32[]{:S(2)}, u32[]{:S(2)}) %collective-permute-start.4) | collective-permute-done | bytes 49184 | tf_op jit(solution)/shard_map/ppermute | solution.py:603
  37.2 3.8 %collective-permute-done.3.corner_ref = bf16[64,384]{1,0:T(8,128)(2,1)S(1)} collective-permute-done((bf16[64,384]{1,0:T(8,128)(2,1)S(1)}, bf16[64,384]{1,0:T(8,128)(2,1)S(1)}, u32[]{:S(2)}, u32[]{:S(2)}) %collective-permute-start.3) | collective-permute-done | bytes 49184 | tf_op jit(solution)/shard_map/ppermute | solution.py:604
  41.0 2.2 %shard_map.203 = (bf16[576,192]{1,0:T(8,128)(2,1)S(1)}, f32[576,192]{1,0:T(8,128)S(1)}, bf16[576,768]{1,0:T(8,128)(2,1)S(1)}, f32[1,192]{1,0:T(1,128)S(1)}) custom-call(bf16[144,384]{1,0:T(8,128)(2,1)S(1)} %get-tuple-element.116.back_ref, bf16[288,384]{1,0:T(8,128)(2,1)S(1)} %collective-permute-done.5.row_ref, ...), custom_call_target="tpu_custom_call" | custom-call | flops 3300000000 | bytes 4896768 | tf_op jit(solution)/shard_map/pallas_call | solution.py:579
  43.2 0.1 collective-permute-start.6
  43.3 4.2 %shard_map.204 = (bf16[576,192]{1,0:T(8,128)(2,1)S(1)}, f32[144,864]{1,0:T(8,128)S(1)}, bf16[1856,128]{1,0:T(8,128)(2,1)S(1)}, bf16[1856,128]{1,0:T(8,128)(2,1)S(1)}) custom-call(f32[576,192]{1,0:T(8,128)S(1)} %get-tuple-element.124.ghid_ref, bf16[576,192]{1,0:T(8,128)(2,1)S(1)} %get-tuple-element.125.g_ref, ...), custom_call_target="tpu_custom_call" | custom-call | flops 8800000000 | bytes 7464448 | tf_op jit(solution)/shard_map/pallas_call | solution.py:579
  47.5 0.6 collective-permute-start.7
  48.1 1.5 %collective-permute-done.7.first_other_ref = bf16[1856,128]{1,0:T(8,128)(2,1)S(1)} collective-permute-done((bf16[1856,128]{1,0:T(8,128)(2,1)S(1)}, bf16[1856,128]{1,0:T(8,128)(2,1)S(1)}, u32[]{:S(2)}, u32[]{:S(2)}) %collective-permute-start.7) | collective-permute-done | bytes 475168 | tf_op jit(solution)/shard_map/ppermute | solution.py:630
  49.5 1.1 %shard_map.205 = bf16[3584,128]{1,0:T(8,128)(2,1)} custom-call(bf16[1856,128]{1,0:T(8,128)(2,1)S(1)} %get-tuple-element.141.first_ref, bf16[1856,128]{1,0:T(8,128)(2,1)S(1)} %collective-permute-done.7.first_other_ref, bf16[1728,128]{1,0:T(8,128)(2,1)S(1)} %get-tuple-element.143.last_ref, bf16[1728,128]{1,0:T(8,128)(2,1)S(1)} %collective-permute-done.6.last_other_ref), custom_call_target="tpu_custom_call" | custom-call | flops 2200000000 | bytes 2752512 | tf_op jit(solution)/shard_map/pallas_call | solution.py:579
  50.7 3.6 %all-to-all-start = ((bf16[16,224,128]{2,1,0:T(8,128)(2,1)}), bf16[16,224,128]{2,1,0:T(8,128)(2,1)S(1)}, u32[]{:S(2)}, u32[]{:S(2)}) async-start(bf16[16,224,128]{2,1,0:T(8,128)(2,1)} %bitcast.6), calls=%async_computation | async-start | bytes 1835008 | tf_op jit(solution)/shard_map/all_to_all | solution.py:647
  54.3 1.6 %shard_map.206 = (bf16[288,384]{1,0:T(8,128)(2,1)}, bf16[416,128]{1,0:T(8,128)(2,1)S(1)}) custom-call(bf16[576,192]{1,0:T(8,128)(2,1)S(1)} %get-tuple-element.148.gblock_ref, f32[144,864]{1,0:T(8,128)S(1)} %get-tuple-element.149.grad_ref, bf16[208,128]{1,0:T(8,128)(2,1)S(1)} %get-tuple-element.150.last_table_ref, bf16[2,96,192]{2,1,0:T(8,128)(2,1)S(1)} %copy-done.11, ...), custom_call_target="tpu_custom_call" | custom-call | flops 2200000000 | bytes 1657632 | tf_op jit(solution)/shard_map/pallas_call | solution.py:579
  56.0 16.0 %all-to-all-done.parts_ref = bf16[16,224,128]{2,1,0:T(8,128)(2,1)S(1)} async-done(((bf16[16,224,128]{2,1,0:T(8,128)(2,1)}), bf16[16,224,128]{2,1,0:T(8,128)(2,1)S(1)}, u32[]{:S(2)}, u32[]{:S(2)}) %all-to-all-start) | async-done | bytes 917536 | tf_op jit(solution)/shard_map/all_to_all | solution.py:647
  72.0 0.1 shard_map.207.refs_0_
  72.1 1.1 %collective-permute-start.8 = (bf16[224,128]{1,0:T(8,128)(2,1)S(1)}, bf16[224,128]{1,0:T(8,128)(2,1)S(1)}, u32[]{:S(2)}, u32[]{:S(2)}) collective-permute-start(bf16[224,128]{1,0:T(8,128)(2,1)S(1)} %shard_map.207.refs_0_), channel_id=1, source_target_pairs={{2,0},{3,1},{4,2},{5,3},{6,4},{7,5},{0,6},{1,7},{10,8},{11,9},{12,... | collective-permute-start | bytes 172040 | tf_op jit(solution)/shard_map/ppermute | solution.py:630
  73.2 1.0 collective-permute-start.10
  74.2 0.6 collective-permute-start.11
  74.7 1.6 %collective-permute-done.8.refs_1_ = bf16[224,128]{1,0:T(8,128)(2,1)S(1)} collective-permute-done((bf16[224,128]{1,0:T(8,128)(2,1)S(1)}, bf16[224,128]{1,0:T(8,128)(2,1)S(1)}, u32[]{:S(2)}, u32[]{:S(2)}) %collective-permute-start.8) | collective-permute-done | bytes 57376 | tf_op jit(solution)/shard_map/ppermute | solution.py:630
  76.3 2.8 %collective-permute-done.9.refs_2_ = bf16[224,128]{1,0:T(8,128)(2,1)S(1)} collective-permute-done((bf16[224,128]{1,0:T(8,128)(2,1)S(1)}, bf16[224,128]{1,0:T(8,128)(2,1)S(1)}, u32[]{:S(2)}, u32[]{:S(2)}) %collective-permute-start.9) | collective-permute-done | bytes 57376 | tf_op jit(solution)/shard_map/ppermute | solution.py:630
  79.2 0.4 collective-permute-done.10.refs_3_
  79.5 1.0 shard_map.208
  80.5 3.6 %all-to-all-start.1 = ((bf16[16,224,128]{2,1,0:T(8,128)(2,1)}), bf16[16,224,128]{2,1,0:T(8,128)(2,1)S(1)}, u32[]{:S(2)}, u32[]{:S(2)}) async-start(bf16[16,224,128]{2,1,0:T(8,128)(2,1)} %shard_map.208), calls=%async_computation.1 | async-start | bytes 1835008 | tf_op jit(solution)/shard_map/all_to_all | solution.py:655
  84.2 1.6 %collective-permute-start.12 = (bf16[416,128]{1,0:T(8,128)(2,1)S(1)}, bf16[416,128]{1,0:T(8,128)(2,1)S(1)}, u32[]{:S(2)}, u32[]{:S(2)}) collective-permute-start(bf16[416,128]{1,0:T(8,128)(2,1)S(1)} %shard_map.209.t0_ref), channel_id=1, source_target_pairs={{2,0},{3,1},{4,2},{5,3},{6,4},{7,5},{0,6},{1,7},{10,8},{11,9},{12,... | collective-permute-start | bytes 319496 | tf_op jit(solution)/shard_map/ppermute | solution.py:630
  85.8 1.5 %collective-permute-start.13 = (bf16[416,128]{1,0:T(8,128)(2,1)S(1)}, bf16[416,128]{1,0:T(8,128)(2,1)S(1)}, u32[]{:S(2)}, u32[]{:S(2)}) collective-permute-start(bf16[416,128]{1,0:T(8,128)(2,1)S(1)} %shard_map.209.t0_ref), channel_id=1, source_target_pairs={{4,0},{5,1},{6,2},{7,3},{0,4},{1,5},{2,6},{3,7},{12,8},{13,9},{14,... | collective-permute-start | bytes 319496 | tf_op jit(solution)/shard_map/ppermute | solution.py:630
  87.2 1.0 collective-permute-start.14
  88.2 0.8 collective-permute-done.12.t1_ref
  89.0 3.0 %collective-permute-done.13.t2_ref = bf16[416,128]{1,0:T(8,128)(2,1)S(1)} collective-permute-done((bf16[416,128]{1,0:T(8,128)(2,1)S(1)}, bf16[416,128]{1,0:T(8,128)(2,1)S(1)}, u32[]{:S(2)}, u32[]{:S(2)}) %collective-permute-start.13) | collective-permute-done | bytes 106528 | tf_op jit(solution)/shard_map/ppermute | solution.py:630
  92.0 1.2 %collective-permute-done.14.t3_ref = bf16[416,128]{1,0:T(8,128)(2,1)S(1)} collective-permute-done((bf16[416,128]{1,0:T(8,128)(2,1)S(1)}, bf16[416,128]{1,0:T(8,128)(2,1)S(1)}, u32[]{:S(2)}, u32[]{:S(2)}) %collective-permute-start.14) | collective-permute-done | bytes 106528 | tf_op jit(solution)/shard_map/ppermute | solution.py:630
  93.1 5.3 %all-to-all-done.1 = bf16[16,224,128]{2,1,0:T(8,128)(2,1)S(1)} async-done(((bf16[16,224,128]{2,1,0:T(8,128)(2,1)}), bf16[16,224,128]{2,1,0:T(8,128)(2,1)S(1)}, u32[]{:S(2)}, u32[]{:S(2)}) %all-to-all-start.1) | async-done | bytes 917536 | tf_op jit(solution)/shard_map/all_to_all | solution.py:655
  98.6 0.1 slice.19
  98.6 0.8 pad_maximum_fusion.1
  99.4 1.5 %collective-permute-done.15.other_ref = bf16[3584,128]{1,0:T(8,128)(2,1)S(1)} collective-permute-done((bf16[3584,128]{1,0:T(8,128)(2,1)S(1)}, bf16[3584,128]{1,0:T(8,128)(2,1)S(1)}, u32[]{:S(2)}, u32[]{:S(2)}) %collective-permute-start.15) | collective-permute-done | bytes 917536 | tf_op jit(solution)/shard_map/ppermute | solution.py:630
  100.9 2.1 %shard_map.210 = (f32[2,192,576]{2,1,0:T(8,128)}, f32[2,192,192]{2,1,0:T(8,128)}, f32[2,192,768]{2,1,0:T(8,128)}, f32[2,192,768]{2,1,0:T(8,128)}, f32[2,2,192]{2,1,0:T(2,128)}, /*index=5*/f32[12,1,3312]{2,1,0:T(1,128)}) custom-call(bf16[3584,128]{1,0:T(8,128)(2,1)S(1)} %bitcast.11, bf16[3584,128]{1,0:T(8,128)(2,1)S(1)} %collective-permute-done.15.other_ref, ...), custom_call_target="tpu_custom_call" | custom-call | flops 2200000000 | bytes 5961984 | tf_op jit(solution)/shard_map/pallas_call | solution.py:579
  (36 shorter events, 0.2 us)
Async XLA Ops:
  0.6 6.6 %copy-start = (bf16[2,192,768]{2,1,0:T(8,128)(2,1)S(1)}, bf16[2,192,768]{2,1,0:T(8,128)(2,1)}, u32[]{:S(2)}) copy-start(bf16[2,192,768]{2,1,0:T(8,128)(2,1)} %up_ref.5) | copy-start | bytes 1769476
  0.6 6.6 %copy-start.1 = (bf16[2,768,192]{1,2,0:T(8,128)(2,1)S(1)}, bf16[2,768,192]{1,2,0:T(8,128)(2,1)}, u32[]{:S(2)}) copy-start(bf16[2,768,192]{1,2,0:T(8,128)(2,1)} %param.20) | copy-start | bytes 1769476
  0.7 6.6 %copy-start.3 = (bf16[6,48,384]{2,1,0:T(8,128)(2,1)S(1)}, bf16[6,48,384]{2,1,0:T(8,128)(2,1)}, u32[]{:S(2)}) copy-start(bf16[6,48,384]{2,1,0:T(8,128)(2,1)} %param.15) | copy-start | bytes 663556
  0.7 6.6 %copy-start.6 = (f32[2,2,192]{2,1,0:T(2,128)S(1)}, f32[2,2,192]{2,1,0:T(2,128)}, u32[]{:S(2)}) copy-start(f32[2,2,192]{2,1,0:T(2,128)} %gains_ref.9) | copy-start | bytes 9220
  0.7 6.6 %copy-start.7 = (bf16[576,288]{1,0:T(8,128)(2,1)S(1)}, bf16[576,288]{1,0:T(8,128)(2,1)}, u32[]{:S(2)}) copy-start(bf16[576,288]{1,0:T(8,128)(2,1)} %constant.14.clone.far_pick.pick_ref) | copy-start | bytes 995332
  0.7 6.6 %copy-start.12 = (bf16[64,288]{1,0:T(8,128)(2,1)S(1)}, bf16[64,288]{1,0:T(8,128)(2,1)}, u32[]{:S(2)}) copy-start(bf16[64,288]{1,0:T(8,128)(2,1)} %constant.17.clone.strips_ref) | copy-start | bytes 110596
  7.3 11.0 %copy-start.5 = (f32[2,1,6,3312]{3,1,2,0:T(1,128)S(1)}, f32[2,1,6,3312]{3,1,2,0:T(1,128)}, u32[]{:S(2)}) copy-start(f32[2,1,6,3312]{3,1,2,0:T(1,128)} %param.21) | copy-start | bytes 476932
  7.3 11.0 %copy-start.10 = (bf16[2,138,276]{2,1,0:T(8,128)(2,1)S(1)}, bf16[2,138,276]{2,1,0:T(8,128)(2,1)}, u32[]{:S(2)}) copy-start(bf16[2,138,276]{2,1,0:T(8,128)(2,1)} %constant.13.clone.far_tcols.tcols_ref) | copy-start | bytes 457060
  7.3 10.9 %copy-start.11 = (bf16[2,96,192]{2,1,0:T(8,128)(2,1)S(1)}, bf16[2,96,192]{2,1,0:T(8,128)(2,1)}, u32[]{:S(2)}) copy-start(bf16[2,96,192]{2,1,0:T(8,128)(2,1)} %constant.12.clone.far_trows.trows_ref) | copy-start | bytes 221188
  9.1 12.6 %collective-permute-start = (bf16[288,384]{1,0:T(8,128)(2,1)S(1)}, bf16[288,384]{1,0:T(8,128)(2,1)S(1)}, u32[]{:S(2)}, u32[]{:S(2)}) collective-permute-start(bf16[288,384]{1,0:T(8,128)(2,1)S(1)} %get-tuple-element.96), channel_id=1, source_target_pairs={{8,0},{9,1},{10,2},{11,3},{12,4},{13,5},{14,6},{15,7},{16,8},{17,9... | collective-permute-start | bytes 663560 | tf_op jit(solution)/shard_map/ppermute | solution.py:602
  15.0 5.0 %collective-permute-start.1 = (bf16[64,384]{1,0:T(8,128)(2,1)S(1)}, bf16[64,384]{1,0:T(8,128)(2,1)S(1)}, u32[]{:S(2)}, u32[]{:S(2)}) collective-permute-start(bf16[64,384]{1,0:T(8,128)(2,1)S(1)} %get-tuple-element.97), channel_id=1, source_target_pairs={{1,0},{2,1},{3,2},{4,3},{5,4},{6,5},{7,6},{0,7},{9,8},{10,9},{11,1... | collective-permute-start | bytes 147464 | tf_op jit(solution)/shard_map/ppermute | solution.py:603
  18.2 3.5 %collective-permute-start.2 = (bf16[64,384]{1,0:T(8,128)(2,1)S(1)}, bf16[64,384]{1,0:T(8,128)(2,1)S(1)}, u32[]{:S(2)}, u32[]{:S(2)}) collective-permute-start(bf16[64,384]{1,0:T(8,128)(2,1)S(1)} %get-tuple-element.98), channel_id=1, source_target_pairs={{9,0},{10,1},{11,2},{12,3},{13,4},{14,5},{15,6},{8,7},{17,8},{18,9... | collective-permute-start | bytes 147464 | tf_op jit(solution)/shard_map/ppermute | solution.py:604
  19.4 2.4 %copy-start.2 = (bf16[2,192,576]{2,1,0:T(8,128)(2,1)S(1)}, bf16[2,192,576]{2,1,0:T(8,128)(2,1)}, u32[]{:S(2)}) copy-start(bf16[2,192,576]{2,1,0:T(8,128)(2,1)} %qkv_ref.3) | copy-start | bytes 1327108
  19.4 2.3 %copy-start.4 = (bf16[2,192,192]{2,1,0:T(8,128)(2,1)S(1)}, bf16[2,192,192]{2,1,0:T(8,128)(2,1)}, u32[]{:S(2)}) copy-start(bf16[2,192,192]{2,1,0:T(8,128)(2,1)} %out_ref.3) | copy-start | bytes 442372
  19.4 2.3 %copy-start.9 = (bf16[576,352]{1,0:T(8,128)(2,1)S(1)}, bf16[576,352]{1,0:T(8,128)(2,1)}, u32[]{:S(2)}) copy-start(bf16[576,352]{1,0:T(8,128)(2,1)} %constant.15.clone.pick_ref) | copy-start | bytes 1216516
  30.2 10.8 %collective-permute-start.5 = (bf16[288,384]{1,0:T(8,128)(2,1)S(1)}, bf16[288,384]{1,0:T(8,128)(2,1)S(1)}, u32[]{:S(2)}, u32[]{:S(2)}) collective-permute-start(bf16[288,384]{1,0:T(8,128)(2,1)S(1)} %get-tuple-element.102), channel_id=1, source_target_pairs={{120,0},{121,1},{122,2},{123,3},{124,4},{125,5},{126,6},{127,7},{0... | collective-permute-start | bytes 663560 | tf_op jit(solution)/shard_map/ppermute | solution.py:602
  30.3 6.9 %collective-permute-start.4 = (bf16[64,384]{1,0:T(8,128)(2,1)S(1)}, bf16[64,384]{1,0:T(8,128)(2,1)S(1)}, u32[]{:S(2)}, u32[]{:S(2)}) collective-permute-start(bf16[64,384]{1,0:T(8,128)(2,1)S(1)} %get-tuple-element.101), channel_id=1, source_target_pairs={{7,0},{0,1},{1,2},{2,3},{3,4},{4,5},{5,6},{6,7},{15,8},{8,9},{9,10... | collective-permute-start | bytes 147464 | tf_op jit(solution)/shard_map/ppermute | solution.py:603
  31.3 9.7 %collective-permute-start.3 = (bf16[64,384]{1,0:T(8,128)(2,1)S(1)}, bf16[64,384]{1,0:T(8,128)(2,1)S(1)}, u32[]{:S(2)}, u32[]{:S(2)}) collective-permute-start(bf16[64,384]{1,0:T(8,128)(2,1)S(1)} %get-tuple-element.100), channel_id=1, source_target_pairs={{127,0},{120,1},{121,2},{122,3},{123,4},{124,5},{125,6},{126,7},{7... | collective-permute-start | bytes 147464 | tf_op jit(solution)/shard_map/ppermute | solution.py:604
  31.3 9.7 %copy-start.8 = (bf16[576,352]{1,0:T(8,128)(2,1)S(1)}, bf16[576,352]{1,0:T(8,128)(2,1)}, u32[]{:S(2)}) copy-start(bf16[576,352]{1,0:T(8,128)(2,1)} %constant.16.clone.returned_ref) | copy-start | bytes 1216516
  43.2 4.3 %collective-permute-start.6 = (bf16[1728,128]{1,0:T(8,128)(2,1)S(1)}, bf16[1728,128]{1,0:T(8,128)(2,1)S(1)}, u32[]{:S(2)}, u32[]{:S(2)}) collective-permute-start(bf16[1728,128]{1,0:T(8,128)(2,1)S(1)} %get-tuple-element.123), channel_id=1, source_target_pairs={{8,0},{9,1},{10,2},{11,3},{12,4},{13,5},{14,6},{15,7},{0,8},{1,9},... | collective-permute-start | bytes 1327112 | tf_op jit(solution)/shard_map/ppermute | solution.py:630
  47.5 2.0 %collective-permute-start.7 = (bf16[1856,128]{1,0:T(8,128)(2,1)S(1)}, bf16[1856,128]{1,0:T(8,128)(2,1)S(1)}, u32[]{:S(2)}, u32[]{:S(2)}) collective-permute-start(bf16[1856,128]{1,0:T(8,128)(2,1)S(1)} %get-tuple-element.142), channel_id=1, source_target_pairs={{8,0},{9,1},{10,2},{11,3},{12,4},{13,5},{14,6},{15,7},{0,8},{1,9},... | collective-permute-start | bytes 1425416 | tf_op jit(solution)/shard_map/ppermute | solution.py:630
  50.7 21.3 %all-to-all-start = ((bf16[16,224,128]{2,1,0:T(8,128)(2,1)}), bf16[16,224,128]{2,1,0:T(8,128)(2,1)S(1)}, u32[]{:S(2)}, u32[]{:S(2)}) async-start(bf16[16,224,128]{2,1,0:T(8,128)(2,1)} %bitcast.6), calls=%async_computation | async-start | bytes 1835008 | tf_op jit(solution)/shard_map/all_to_all | solution.py:647
  72.1 4.2 %collective-permute-start.8 = (bf16[224,128]{1,0:T(8,128)(2,1)S(1)}, bf16[224,128]{1,0:T(8,128)(2,1)S(1)}, u32[]{:S(2)}, u32[]{:S(2)}) collective-permute-start(bf16[224,128]{1,0:T(8,128)(2,1)S(1)} %shard_map.207.refs_0_), channel_id=1, source_target_pairs={{2,0},{3,1},{4,2},{5,3},{6,4},{7,5},{0,6},{1,7},{10,8},{11,9},{12,... | collective-permute-start | bytes 172040 | tf_op jit(solution)/shard_map/ppermute | solution.py:630
  73.2 5.9 %collective-permute-start.9 = (bf16[224,128]{1,0:T(8,128)(2,1)S(1)}, bf16[224,128]{1,0:T(8,128)(2,1)S(1)}, u32[]{:S(2)}, u32[]{:S(2)}) collective-permute-start(bf16[224,128]{1,0:T(8,128)(2,1)S(1)} %shard_map.207.refs_0_), channel_id=1, source_target_pairs={{4,0},{5,1},{6,2},{7,3},{0,4},{1,5},{2,6},{3,7},{12,8},{13,9},{14,... | collective-permute-start | bytes 172040 | tf_op jit(solution)/shard_map/ppermute | solution.py:630
  73.2 6.3 %collective-permute-start.10 = (bf16[224,128]{1,0:T(8,128)(2,1)S(1)}, bf16[224,128]{1,0:T(8,128)(2,1)S(1)}, u32[]{:S(2)}, u32[]{:S(2)}) collective-permute-start(bf16[224,128]{1,0:T(8,128)(2,1)S(1)} %shard_map.207.refs_0_), channel_id=1, source_target_pairs={{6,0},{7,1},{0,2},{1,3},{2,4},{3,5},{4,6},{5,7},{14,8},{15,9},{8,1... | collective-permute-start | bytes 172040 | tf_op jit(solution)/shard_map/ppermute | solution.py:630
  74.2 6.3 %collective-permute-start.11 = (bf16[416,128]{1,0:T(8,128)(2,1)S(1)}, bf16[416,128]{1,0:T(8,128)(2,1)S(1)}, u32[]{:S(2)}, u32[]{:S(2)}) collective-permute-start(bf16[416,128]{1,0:T(8,128)(2,1)S(1)} %get-tuple-element.158.mine_ref), channel_id=1, source_target_pairs={{1,0},{0,1},{3,2},{2,3},{5,4},{4,5},{7,6},{6,7},{9,8},{8,9},{11,10... | collective-permute-start | bytes 319496 | tf_op jit(solution)/shard_map/ppermute | solution.py:630
  80.5 17.9 %all-to-all-start.1 = ((bf16[16,224,128]{2,1,0:T(8,128)(2,1)}), bf16[16,224,128]{2,1,0:T(8,128)(2,1)S(1)}, u32[]{:S(2)}, u32[]{:S(2)}) async-start(bf16[16,224,128]{2,1,0:T(8,128)(2,1)} %shard_map.208), calls=%async_computation.1 | async-start | bytes 1835008 | tf_op jit(solution)/shard_map/all_to_all | solution.py:655
  84.2 4.8 %collective-permute-start.12 = (bf16[416,128]{1,0:T(8,128)(2,1)S(1)}, bf16[416,128]{1,0:T(8,128)(2,1)S(1)}, u32[]{:S(2)}, u32[]{:S(2)}) collective-permute-start(bf16[416,128]{1,0:T(8,128)(2,1)S(1)} %shard_map.209.t0_ref), channel_id=1, source_target_pairs={{2,0},{3,1},{4,2},{5,3},{6,4},{7,5},{0,6},{1,7},{10,8},{11,9},{12,... | collective-permute-start | bytes 319496 | tf_op jit(solution)/shard_map/ppermute | solution.py:630
  85.8 6.2 %collective-permute-start.13 = (bf16[416,128]{1,0:T(8,128)(2,1)S(1)}, bf16[416,128]{1,0:T(8,128)(2,1)S(1)}, u32[]{:S(2)}, u32[]{:S(2)}) collective-permute-start(bf16[416,128]{1,0:T(8,128)(2,1)S(1)} %shard_map.209.t0_ref), channel_id=1, source_target_pairs={{4,0},{5,1},{6,2},{7,3},{0,4},{1,5},{2,6},{3,7},{12,8},{13,9},{14,... | collective-permute-start | bytes 319496 | tf_op jit(solution)/shard_map/ppermute | solution.py:630
  87.2 5.9 %collective-permute-start.14 = (bf16[416,128]{1,0:T(8,128)(2,1)S(1)}, bf16[416,128]{1,0:T(8,128)(2,1)S(1)}, u32[]{:S(2)}, u32[]{:S(2)}) collective-permute-start(bf16[416,128]{1,0:T(8,128)(2,1)S(1)} %shard_map.209.t0_ref), channel_id=1, source_target_pairs={{6,0},{7,1},{0,2},{1,3},{2,4},{3,5},{4,6},{5,7},{14,8},{15,9},{8,1... | collective-permute-start | bytes 319496 | tf_op jit(solution)/shard_map/ppermute | solution.py:630
  98.5 2.5 %collective-permute-start.15 = (bf16[3584,128]{1,0:T(8,128)(2,1)S(1)}, bf16[3584,128]{1,0:T(8,128)(2,1)S(1)}, u32[]{:S(2)}, u32[]{:S(2)}) collective-permute-start(bf16[3584,128]{1,0:T(8,128)(2,1)S(1)} %bitcast.10), channel_id=1, source_target_pairs={{8,0},{9,1},{10,2},{11,3},{12,4},{13,5},{14,6},{15,7},{0,8},{1,9},... | collective-permute-start | bytes 2752520 | tf_op jit(solution)/shard_map/ppermute | solution.py:630

commit v7 on v6

--- a/solution.py
+++ b/solution.py
@@ -120,15 +120,15 @@
 
 
 def gather_tokens(picker, source):
-    both = nn(picker, source)
-    return jnp.where(level_mask(), both[:, DIM:], both[:, :DIM])
+    return jnp.where(level_mask(), nn(picker, source[:, DIM:]), nn(picker, source[:, :DIM]))
 
 
 def scatter_tokens(picker, tokens):
     upper = level_mask()
     zero = jnp.zeros_like(tokens)
-    both = jnp.concatenate([jnp.where(upper, zero, tokens), jnp.where(upper, tokens, zero)], axis=1)
-    return tn(picker, both.astype(BF16))
+    low = tn(picker, jnp.where(upper, zero, tokens).astype(BF16))
+    high = tn(picker, jnp.where(upper, tokens, zero).astype(BF16))
+    return jnp.concatenate([low, high], axis=1)
 
 
 def normalize(x):
@@ -522,42 +522,39 @@
 def unpack(
     mine_ref, other_ref, t0_ref, t1_ref, t2_ref, t3_ref, qkv_ref, out_ref, up_ref, down_ref, gains_ref, table_ref, sum_ref
 ):
+    block = pl.program_id(0)
     core = lax.rem(lax.axis_index("lat"), 2)
 
     def load(half, start, count):
-        here = mine_ref[start : start + count, :].astype(F32)
-        there = other_ref[start : start + count, :].astype(F32)
-        return jnp.where(core == half, here, there)
-
-    total = t0_ref[...].astype(F32)
+        rows = pl.ds(pl.multiple_of(start, 16), count)
+        return jnp.where(core == half, mine_ref[rows, :].astype(F32), other_ref[rows, :].astype(F32))
+
+    for j in range(18):
+        tile = load(j // 9, block * PART + j % 9 * DIM, DIM)
+        if j < 6:
+            up_ref[:, j * 128 : (j + 1) * 128] = tile
+        elif j < 12:
+            down_ref[:, (j - 6) * 128 : (j - 5) * 128] = tile
+        elif j < 16:
+            qkv_ref[:, (j - 12) * 128 : (j - 11) * 128] = tile
+        elif j == 16:
+            qkv_ref[:, 512:576] = tile[:, :64]
+            out_ref[:, 0:64] = tile[:, 64:]
+        else:
+            out_ref[:, 64:192] = tile
+    rows = pl.ds(pl.multiple_of(block * TROWS, 16), TROWS)
+    total = t0_ref[rows, :].astype(F32)
     for ref in (t1_ref, t2_ref, t3_ref):
-        total += ref[...].astype(F32)
+        total += ref[rows, :].astype(F32)
     sum_ref[...] = total
-    for b in range(2):
-        for j in range(18):
-            tile = load(j // 9, b * PART + j % 9 * DIM, DIM)
-            if j < 6:
-                up_ref[b, :, j * 128 : (j + 1) * 128] = tile
-            elif j < 12:
-                down_ref[b, :, (j - 6) * 128 : (j - 5) * 128] = tile
-            elif j < 16:
-                qkv_ref[b, :, (j - 12) * 128 : (j - 11) * 128] = tile
-            elif j == 16:
-                qkv_ref[b, :, 512:576] = tile[:, :64]
-                out_ref[b, :, 0:64] = tile[:, 64:]
-            else:
-                out_ref[b, :, 64:192] = tile
-        for j in range(26):
-            place = b * TROWS + j * 8
-            piece = sum_ref[place : place + HEADS, :]
-            width = min(128, TABLE - j * 128)
-            for h in range(HEADS):
-                table_ref[b * HEADS + h, :, j * 128 : j * 128 + width] = piece[h : h + 1, :width]
-    gains = jnp.concatenate([load(0, 2 * PART + j * 16, 16)[0:1] for j in range(6)], axis=1)
-    for b in range(2):
-        for i in range(2):
-            k = b * 2 + i
-            gains_ref[b, i : i + 1, :] = gains[:, k * DIM : (k + 1) * DIM]
+    for j in range(26):
+        piece = sum_ref[j * 8 : j * 8 + HEADS, :]
+        width = min(128, TABLE - j * 128)
+        for h in range(HEADS):
+            table_ref[h, :, j * 128 : j * 128 + width] = piece[h : h + 1, :width]
+    gains = jnp.concatenate([load(0, 2 * PART + (block * 3 + j) * 16, 16)[0:1] for j in range(3)], axis=1)
+    for i in range(2):
+        gains_ref[i : i + 1, :] = gains[:, i * DIM : (i + 1) * DIM]
 
 
 def whole(array):
@@ -573,12 +570,12 @@
     return pl.BlockSpec(memory_space=pl.ANY)
 
 
-def call(kernel, operands, specs, outs, scratch=(), micros=2, out_specs=None, mebibytes=10):
+def call(kernel, operands, specs, outs, scratch=(), micros=2, out_specs=None, mebibytes=10, steps=1):
     shapes = [jax.ShapeDtypeStruct(shape, dtype) for shape, dtype in outs]
     moved = sum(a.size * a.dtype.itemsize for a in (*operands, *shapes))
     return pl.pallas_call(
         kernel,
-        grid=(1,),
+        grid=(steps,),
         out_shape=shapes,
         in_specs=specs,
         out_specs=out_specs or [whole(s) for s in shapes],
@@ -659,7 +656,11 @@
     operands = [half, moved(half, core=1), *table_terms]
     outs = [((2, DIM, 3 * DIM), F32), ((2, DIM, DIM), F32), ((2, DIM, UNITS), F32), ((2, DIM, UNITS), F32)]
     outs += [((2, 2, DIM), F32), ((2 * HEADS, 1, TABLE), F32)]
-    grads = call(unpack, operands, [whole(a) for a in operands], outs, [vmem((2 * TROWS, 128), F32)])
+    out_specs = [pl.BlockSpec((None,) + shape[1:], lambda b: (b, 0, 0)) for shape, _ in outs[:-1]]
+    out_specs.append(pl.BlockSpec((HEADS, 1, TABLE), lambda b: (b, 0, 0)))
+    grads = call(
+        unpack, operands, [whole(a) for a in operands], outs, [vmem((TROWS, 128), F32)], 2, out_specs, steps=2
+    )
     return grad_inputs, grads
 
 
@@ -739,8 +740,6 @@
     outs = [wide_tok, (tok, F32), wide_hid, ((1, DIM), F32)]
     results = call(first_mlp_back, operands, specs_for(operands, 0), outs, [vmem(src, BF16)], 3, mebibytes=14)
     g, ghid, gpre, mlp_gain = results
-    ghid, last_theirs = lax.optimization_barrier((ghid, last_theirs))
-    last = [last_mine, moved(last_theirs, core=1)]
 
     operands = [ghid, g, gpre, mlp_gain, hat, inv, normed_first, normed_mlp, q, k, v, probs_first, ctx, expanded, gains, qkv, out]
     operands += [last_gain]
@@ -751,7 +750,8 @@
     gblock, grad_scores, *first = call(
         first_attention_back, operands, specs_for(operands, 0), outs, scratch, 8, out_specs, 14
     )
-    last, first = lax.optimization_barrier((last, first))
+    last_theirs, first = lax.optimization_barrier((last_theirs, first))
+    last = [last_mine, moved(last_theirs, core=1)]
     finish = [gblock, grad_scores, last_table, trows, tcols, pick_grid]
     grad_inputs, grads = sum_over_devices(first, last, finish)
     y_rows, y_side, y_corner = arrived

time: 104 us -> 101 us (0.971)
  Pallas kernels: 32.6 us -> 29.6 us
    pallas_call x14, Pallas kernels: 32.6 us -> 29.6 us  [call(): pl.pallas_call(kernel, grid=(steps,), out_shape=shapes, in_specs=specs, o...]
  transfers between devices with their start and end apart: 18 -> 18, of which waited for: 14 -> 14; matrix products, arithmetic and copies ran while one was open for 1% -> 1% of each run, Pallas kernels for 10% -> 6%
where the time goes in v7:
time: 101 us; the launch traced here: 99.9 us
  waiting for transfers between devices  43.6 us (43%)
  Pallas kernels  29.6 us (29%)
  starting transfers between devices  24.9 us (25%)
    pallas_call x14, Pallas kernels, call(): pl.pallas_call(kernel, grid=(steps,), out_shape=shapes, in_specs=specs, o...  29.6 us
    all_to_all x1, waiting for transfers between devices, sum_over_devices(): lax.all_to_all(sent.reshape(16, CHUNK, 128), both, 0, 0, axis_index_group...  15.4 us
    ppermute x10, waiting for transfers between devices, moved(): return lax.ppermute(array, ('lat', 'lon'), shifted_pairs(**steps))  13.3 us
    ppermute x10, starting transfers between devices, moved(): return lax.ppermute(array, ('lat', 'lon'), shifted_pairs(**steps))  7.36 us
    ppermute x2, starting transfers between devices, exchange(): rows = lax.ppermute(rows, both, neighbour(sizes, (step, 0)))  5.98 us
    ppermute x2, waiting for transfers between devices, exchange(): corner = lax.ppermute(corner, both, neighbour(sizes, (step, step)))  5.59 us
    all_to_all x1, waiting for transfers between devices, sum_over_devices(): half = lax.all_to_all(spread, both, 0, 0, axis_index_groups=groups)  5.19 us
    ppermute x2, starting transfers between devices, exchange(): side = lax.ppermute(side, both, neighbour(sizes, (0, step)))  4.24 us
  transfers between devices with their start and end apart: 18, of which 14 were waited for; matrix products, arithmetic and copies ran while one was open for 1% of the time, Pallas kernels for 6%

profile of v7, /device:TPU:0, one launch (start us, length us, event | category | flops | bytes accessed | tf_op | source)
XLA Modules:
  0.0 99.9 jit_solution(16591819561206525170)
XLA Ops:
  0.7 0.0 copy-start.7
  0.7 0.0 copy-start.12
  0.7 4.9 %shard_map.197 = (bf16[576,192]{1,0:T(8,128)(2,1)S(1)}, bf16[576,192]{1,0:T(8,128)(2,1)S(1)}, bf16[576,192]{1,0:T(8,128)(2,1)S(1)}, bf16[576,192]{1,0:T(8,128)(2...) custom-call(bf16[288,384]{1,0:T(8,128)(2,1)} %bitcast.20, ...), custom_call_target="tpu_custom_call" | custom-call | flops 7699999744 | bytes 4074528 | tf_op jit(solution)/shard_map/pallas_call | solution.py:576
  5.6 0.0 copy-start.10
  5.7 0.0 copy-start.11
  5.7 1.8 %shard_map.198 = (bf16[576,768]{1,0:T(8,128)(2,1)S(1)}, bf16[576,768]{1,0:T(8,128)(2,1)S(1)}, bf16[144,384]{1,0:T(8,128)(2,1)S(1)}, bf16[288,384]{1,0:T(8,128)(2...) custom-call(f32[576,192]{1,0:T(8,128)S(1)} %get-tuple-element.87.hidden_ref, ...), custom_call_target="tpu_custom_call" | custom-call | flops 4400000000 | bytes 4414464 | tf_op jit(solution)/shard_map/pallas_call | solution.py:576
  7.5 5.9 %collective-permute-start = (bf16[288,384]{1,0:T(8,128)(2,1)S(1)}, bf16[288,384]{1,0:T(8,128)(2,1)S(1)}, u32[]{:S(2)}, u32[]{:S(2)}) collective-permute-start(bf16[288,384]{1,0:T(8,128)(2,1)S(1)} %get-tuple-element.93), channel_id=1, source_target_pairs={{8,0},{9,1},{10,2},{11,3},{12,4},{13,5},{14,6},{15,7},{16,8},{17,9... | collective-permute-start | bytes 663560 | tf_op jit(solution)/shard_map/ppermute | solution.py:599
  13.4 3.2 %collective-permute-start.1 = (bf16[64,384]{1,0:T(8,128)(2,1)S(1)}, bf16[64,384]{1,0:T(8,128)(2,1)S(1)}, u32[]{:S(2)}, u32[]{:S(2)}) collective-permute-start(bf16[64,384]{1,0:T(8,128)(2,1)S(1)} %get-tuple-element.94), channel_id=1, source_target_pairs={{1,0},{2,1},{3,2},{4,3},{5,4},{6,5},{7,6},{0,7},{9,8},{10,9},{11,1... | collective-permute-start | bytes 147464 | tf_op jit(solution)/shard_map/ppermute | solution.py:600
  16.6 1.1 %shard_map.199.bias_ref = f32[144,864]{1,0:T(8,128)S(1)} custom-call(f32[12,1,3312]{2,1,0:T(1,128)S(1)} %bitcast.18, bf16[2,96,192]{2,1,0:T(8,128)(2,1)S(1)} %copy-done.11, bf16[2,138,276]{2,1,0:T(8,128)(2,1)S(1)} %copy-done.10), custom_call_target="tpu_custom_call" | custom-call | flops 2200000000 | bytes 882720 | tf_op jit(solution)/shard_map/pallas_call | solution.py:576
  17.8 0.0 copy-start.9
  17.8 0.4 shard_map.202
  18.2 0.1 collective-permute-done.1.side_ref
  18.4 1.7 %collective-permute-done.2.corner_ref = bf16[64,384]{1,0:T(8,128)(2,1)S(1)} collective-permute-done((bf16[64,384]{1,0:T(8,128)(2,1)S(1)}, bf16[64,384]{1,0:T(8,128)(2,1)S(1)}, u32[]{:S(2)}, u32[]{:S(2)}) %collective-permute-start.2) | collective-permute-done | bytes 49184 | tf_op jit(solution)/shard_map/ppermute | solution.py:601
  20.1 7.6 %shard_map.200 = (bf16[144,384]{1,0:T(8,128)(2,1)S(1)}, bf16[144,384]{1,0:T(8,128)(2,1)S(1)}, bf16[288,384]{1,0:T(8,128)(2,1)S(1)}, bf16[64,384]{1,0:T(8,128)(2,...) custom-call(bf16[144,384]{1,0:T(8,128)(2,1)S(1)} %get-tuple-element., ...), custom_call_target="tpu_custom_call" | custom-call | flops 13200000000 | bytes 7905792 | tf_op jit(solution)/shard_map/pallas_call | solution.py:576
  27.7 0.1 collective-permute-start.5
  27.8 1.0 %collective-permute-start.4 = (bf16[64,384]{1,0:T(8,128)(2,1)S(1)}, bf16[64,384]{1,0:T(8,128)(2,1)S(1)}, u32[]{:S(2)}, u32[]{:S(2)}) collective-permute-start(bf16[64,384]{1,0:T(8,128)(2,1)S(1)} %get-tuple-element.98), channel_id=1, source_target_pairs={{7,0},{0,1},{1,2},{2,3},{3,4},{4,5},{5,6},{6,7},{15,8},{8,9},{9,10... | collective-permute-start | bytes 147464 | tf_op jit(solution)/shard_map/ppermute | solution.py:600
  28.9 1.9 %shard_map.201 = (bf16[1728,128]{1,0:T(8,128)(2,1)S(1)}, bf16[1728,128]{1,0:T(8,128)(2,1)S(1)}, bf16[208,128]{1,0:T(8,128)(2,1)S(1)}) custom-call(bf16[576,192]{1,0:T(8,128)(2,1)S(1)} %get-tuple-element.101.normed_ref, bf16[576,192]{1,0:T(8,128)(2,1)S(1)} %get-tuple-element.102.dq_ref, bf16[576,192]{1,0:T(8,128)(2,1)S(1)} %get-tuple-element.103.dk_ref, ...), custom_call_target="tpu_custom_call" | custom-call | flops 4400000000 | bytes 5200672 | tf_op jit(solution)/shard_map/pallas_call | solution.py:576
  30.8 3.9 %collective-permute-done.4.side_ref = bf16[64,384]{1,0:T(8,128)(2,1)S(1)} collective-permute-done((bf16[64,384]{1,0:T(8,128)(2,1)S(1)}, bf16[64,384]{1,0:T(8,128)(2,1)S(1)}, u32[]{:S(2)}, u32[]{:S(2)}) %collective-permute-start.4) | collective-permute-done | bytes 49184 | tf_op jit(solution)/shard_map/ppermute | solution.py:600
  34.7 3.9 %collective-permute-done.3.corner_ref = bf16[64,384]{1,0:T(8,128)(2,1)S(1)} collective-permute-done((bf16[64,384]{1,0:T(8,128)(2,1)S(1)}, bf16[64,384]{1,0:T(8,128)(2,1)S(1)}, u32[]{:S(2)}, u32[]{:S(2)}) %collective-permute-start.3) | collective-permute-done | bytes 49184 | tf_op jit(solution)/shard_map/ppermute | solution.py:601
  38.5 1.5 %shard_map.203 = (bf16[576,192]{1,0:T(8,128)(2,1)S(1)}, f32[576,192]{1,0:T(8,128)S(1)}, bf16[576,768]{1,0:T(8,128)(2,1)S(1)}, f32[1,192]{1,0:T(1,128)S(1)}) custom-call(bf16[144,384]{1,0:T(8,128)(2,1)S(1)} %get-tuple-element.113.back_ref, bf16[288,384]{1,0:T(8,128)(2,1)S(1)} %collective-permute-done.5.row_ref, ...), custom_call_target="tpu_custom_call" | custom-call | flops 3300000000 | bytes 4896768 | tf_op jit(solution)/shard_map/pallas_call | solution.py:576
  40.0 4.2 %shard_map.204 = (bf16[576,192]{1,0:T(8,128)(2,1)S(1)}, f32[144,864]{1,0:T(8,128)S(1)}, bf16[1856,128]{1,0:T(8,128)(2,1)S(1)}, bf16[1856,128]{1,0:T(8,128)(2,1)S(1)}) custom-call(f32[576,192]{1,0:T(8,128)S(1)} %get-tuple-element.118.ghid_ref, bf16[576,192]{1,0:T(8,128)(2,1)S(1)} %get-tuple-element.119.g_ref, ...), custom_call_target="tpu_custom_call" | custom-call | flops 8800000000 | bytes 7464448 | tf_op jit(solution)/shard_map/pallas_call | solution.py:576
  44.2 0.1 collective-permute-start.6
  44.3 0.5 collective-permute-start.7
  44.8 2.0 %collective-permute-done.7.last_other_ref = bf16[1728,128]{1,0:T(8,128)(2,1)S(1)} collective-permute-done((bf16[1728,128]{1,0:T(8,128)(2,1)S(1)}, bf16[1728,128]{1,0:T(8,128)(2,1)S(1)}, u32[]{:S(2)}, u32[]{:S(2)}) %collective-permute-start.7) | collective-permute-done | bytes 442400 | tf_op jit(solution)/shard_map/ppermute | solution.py:627
  46.7 1.1 %shard_map.205 = bf16[3584,128]{1,0:T(8,128)(2,1)} custom-call(bf16[1856,128]{1,0:T(8,128)(2,1)S(1)} %get-tuple-element.135.first_ref, bf16[1856,128]{1,0:T(8,128)(2,1)S(1)} %collective-permute-done.6.first_other_ref, bf16[1728,128]{1,0:T(8,128)(2,1)S(1)} %get-tuple-element.137.last_ref, bf16[1728,128]{1,0:T(8,128)(2,1)S(1)} %collective-permute-done.7.last_other_ref), custom_call_target="tpu_custom_call" | custom-call | flops 2200000000 | bytes 2752512 | tf_op jit(solution)/shard_map/pallas_call | solution.py:576
  47.9 3.6 %all-to-all-start = ((bf16[16,224,128]{2,1,0:T(8,128)(2,1)}), bf16[16,224,128]{2,1,0:T(8,128)(2,1)S(1)}, u32[]{:S(2)}, u32[]{:S(2)}) async-start(bf16[16,224,128]{2,1,0:T(8,128)(2,1)} %bitcast.6), calls=%async_computation | async-start | bytes 1835008 | tf_op jit(solution)/shard_map/all_to_all | solution.py:644
  51.5 1.7 %shard_map.206 = (bf16[288,384]{1,0:T(8,128)(2,1)}, bf16[416,128]{1,0:T(8,128)(2,1)S(1)}) custom-call(bf16[576,192]{1,0:T(8,128)(2,1)S(1)} %get-tuple-element.142.gblock_ref, f32[144,864]{1,0:T(8,128)S(1)} %get-tuple-element.143.grad_ref, bf16[208,128]{1,0:T(8,128)(2,1)S(1)} %get-tuple-element.144.last_table_ref, bf16[2,96,192]{2,1,0:T(8,128)(2,1)S(1)} %copy-done.11, ...), custom_call_target="tpu_custom_call" | custom-call | flops 2200000000 | bytes 1657632 | tf_op jit(solution)/shard_map/pallas_call | solution.py:576
  53.2 15.4 %all-to-all-done.parts_ref = bf16[16,224,128]{2,1,0:T(8,128)(2,1)S(1)} async-done(((bf16[16,224,128]{2,1,0:T(8,128)(2,1)}), bf16[16,224,128]{2,1,0:T(8,128)(2,1)S(1)}, u32[]{:S(2)}, u32[]{:S(2)}) %all-to-all-start) | async-done | bytes 917536 | tf_op jit(solution)/shard_map/all_to_all | solution.py:644
  68.7 0.1 shard_map.207.refs_0_
  68.8 1.4 %collective-permute-start.8 = (bf16[224,128]{1,0:T(8,128)(2,1)S(1)}, bf16[224,128]{1,0:T(8,128)(2,1)S(1)}, u32[]{:S(2)}, u32[]{:S(2)}) collective-permute-start(bf16[224,128]{1,0:T(8,128)(2,1)S(1)} %shard_map.207.refs_0_), channel_id=1, source_target_pairs={{2,0},{3,1},{4,2},{5,3},{6,4},{7,5},{0,6},{1,7},{10,8},{11,9},{12,... | collective-permute-start | bytes 172040 | tf_op jit(solution)/shard_map/ppermute | solution.py:627
  70.1 0.9 collective-permute-start.10
  71.1 0.6 collective-permute-start.11
  71.7 1.4 %collective-permute-done.8.refs_1_ = bf16[224,128]{1,0:T(8,128)(2,1)S(1)} collective-permute-done((bf16[224,128]{1,0:T(8,128)(2,1)S(1)}, bf16[224,128]{1,0:T(8,128)(2,1)S(1)}, u32[]{:S(2)}, u32[]{:S(2)}) %collective-permute-start.8) | collective-permute-done | bytes 57376 | tf_op jit(solution)/shard_map/ppermute | solution.py:627
  73.0 2.9 %collective-permute-done.9.refs_2_ = bf16[224,128]{1,0:T(8,128)(2,1)S(1)} collective-permute-done((bf16[224,128]{1,0:T(8,128)(2,1)S(1)}, bf16[224,128]{1,0:T(8,128)(2,1)S(1)}, u32[]{:S(2)}, u32[]{:S(2)}) %collective-permute-start.9) | collective-permute-done | bytes 57376 | tf_op jit(solution)/shard_map/ppermute | solution.py:627
  75.9 0.4 collective-permute-done.10.refs_3_
  76.3 1.0 shard_map.208
  77.3 3.6 %all-to-all-start.1 = ((bf16[16,224,128]{2,1,0:T(8,128)(2,1)}), bf16[16,224,128]{2,1,0:T(8,128)(2,1)S(1)}, u32[]{:S(2)}, u32[]{:S(2)}) async-start(bf16[16,224,128]{2,1,0:T(8,128)(2,1)} %shard_map.208), calls=%async_computation.1 | async-start | bytes 1835008 | tf_op jit(solution)/shard_map/all_to_all | solution.py:652
  81.0 1.5 %collective-permute-start.12 = (bf16[416,128]{1,0:T(8,128)(2,1)S(1)}, bf16[416,128]{1,0:T(8,128)(2,1)S(1)}, u32[]{:S(2)}, u32[]{:S(2)}) collective-permute-start(bf16[416,128]{1,0:T(8,128)(2,1)S(1)} %shard_map.209.t0_ref), channel_id=1, source_target_pairs={{2,0},{3,1},{4,2},{5,3},{6,4},{7,5},{0,6},{1,7},{10,8},{11,9},{12,... | collective-permute-start | bytes 319496 | tf_op jit(solution)/shard_map/ppermute | solution.py:627
  82.5 1.7 %collective-permute-start.13 = (bf16[416,128]{1,0:T(8,128)(2,1)S(1)}, bf16[416,128]{1,0:T(8,128)(2,1)S(1)}, u32[]{:S(2)}, u32[]{:S(2)}) collective-permute-start(bf16[416,128]{1,0:T(8,128)(2,1)S(1)} %shard_map.209.t0_ref), channel_id=1, source_target_pairs={{4,0},{5,1},{6,2},{7,3},{0,4},{1,5},{2,6},{3,7},{12,8},{13,9},{14,... | collective-permute-start | bytes 319496 | tf_op jit(solution)/shard_map/ppermute | solution.py:627
  84.2 0.7 collective-permute-start.14
  84.9 0.9 collective-permute-done.12.t1_ref
  85.8 2.9 %collective-permute-done.13.t2_ref = bf16[416,128]{1,0:T(8,128)(2,1)S(1)} collective-permute-done((bf16[416,128]{1,0:T(8,128)(2,1)S(1)}, bf16[416,128]{1,0:T(8,128)(2,1)S(1)}, u32[]{:S(2)}, u32[]{:S(2)}) %collective-permute-start.13) | collective-permute-done | bytes 106528 | tf_op jit(solution)/shard_map/ppermute | solution.py:627
  88.7 1.4 %collective-permute-done.14.t3_ref = bf16[416,128]{1,0:T(8,128)(2,1)S(1)} collective-permute-done((bf16[416,128]{1,0:T(8,128)(2,1)S(1)}, bf16[416,128]{1,0:T(8,128)(2,1)S(1)}, u32[]{:S(2)}, u32[]{:S(2)}) %collective-permute-start.14) | collective-permute-done | bytes 106528 | tf_op jit(solution)/shard_map/ppermute | solution.py:627
  90.1 5.2 %all-to-all-done.1 = bf16[16,224,128]{2,1,0:T(8,128)(2,1)S(1)} async-done(((bf16[16,224,128]{2,1,0:T(8,128)(2,1)}), bf16[16,224,128]{2,1,0:T(8,128)(2,1)S(1)}, u32[]{:S(2)}, u32[]{:S(2)}) %all-to-all-start.1) | async-done | bytes 917536 | tf_op jit(solution)/shard_map/all_to_all | solution.py:652
  95.4 0.1 slice.19
  95.4 0.8 pad_maximum_fusion.1
  96.2 1.5 %collective-permute-done.15.other_ref = bf16[3584,128]{1,0:T(8,128)(2,1)S(1)} collective-permute-done((bf16[3584,128]{1,0:T(8,128)(2,1)S(1)}, bf16[3584,128]{1,0:T(8,128)(2,1)S(1)}, u32[]{:S(2)}, u32[]{:S(2)}) %collective-permute-start.15) | collective-permute-done | bytes 917536 | tf_op jit(solution)/shard_map/ppermute | solution.py:627
  97.7 2.2 %shard_map.210 = (f32[2,192,576]{2,1,0:T(8,128)}, f32[2,192,192]{2,1,0:T(8,128)}, f32[2,192,768]{2,1,0:T(8,128)}, f32[2,192,768]{2,1,0:T(8,128)}, f32[2,2,192]{2,1,0:T(2,128)}, /*index=5*/f32[12,1,3312]{2,1,0:T(1,128)}) custom-call(bf16[3584,128]{1,0:T(8,128)(2,1)S(1)} %bitcast.11, bf16[3584,128]{1,0:T(8,128)(2,1)S(1)} %collective-permute-done.15.other_ref, ...), custom_call_target="tpu_custom_call" | custom-call | flops 2200000000 | bytes 5961984 | tf_op jit(solution)/shard_map/pallas_call | solution.py:576
  (36 shorter events, 0.2 us)
Async XLA Ops:
  0.6 4.9 %copy-start = (bf16[2,192,768]{2,1,0:T(8,128)(2,1)S(1)}, bf16[2,192,768]{2,1,0:T(8,128)(2,1)}, u32[]{:S(2)}) copy-start(bf16[2,192,768]{2,1,0:T(8,128)(2,1)} %up_ref.5) | copy-start | bytes 1769476
  0.6 4.9 %copy-start.1 = (bf16[2,768,192]{1,2,0:T(8,128)(2,1)S(1)}, bf16[2,768,192]{1,2,0:T(8,128)(2,1)}, u32[]{:S(2)}) copy-start(bf16[2,768,192]{1,2,0:T(8,128)(2,1)} %param.20) | copy-start | bytes 1769476
  0.7 4.9 %copy-start.3 = (bf16[6,48,384]{2,1,0:T(8,128)(2,1)S(1)}, bf16[6,48,384]{2,1,0:T(8,128)(2,1)}, u32[]{:S(2)}) copy-start(bf16[6,48,384]{2,1,0:T(8,128)(2,1)} %param.15) | copy-start | bytes 663556
  0.7 4.9 %copy-start.6 = (f32[2,2,192]{2,1,0:T(2,128)S(1)}, f32[2,2,192]{2,1,0:T(2,128)}, u32[]{:S(2)}) copy-start(f32[2,2,192]{2,1,0:T(2,128)} %gains_ref.9) | copy-start | bytes 9220
  0.7 4.9 %copy-start.7 = (bf16[576,288]{1,0:T(8,128)(2,1)S(1)}, bf16[576,288]{1,0:T(8,128)(2,1)}, u32[]{:S(2)}) copy-start(bf16[576,288]{1,0:T(8,128)(2,1)} %constant.14.clone.far_pick.pick_ref) | copy-start | bytes 995332
  0.7 4.9 %copy-start.12 = (bf16[64,288]{1,0:T(8,128)(2,1)S(1)}, bf16[64,288]{1,0:T(8,128)(2,1)}, u32[]{:S(2)}) copy-start(bf16[64,288]{1,0:T(8,128)(2,1)} %constant.17.clone.strips_ref) | copy-start | bytes 110596
  5.6 11.0 %copy-start.5 = (f32[2,1,6,3312]{3,1,2,0:T(1,128)S(1)}, f32[2,1,6,3312]{3,1,2,0:T(1,128)}, u32[]{:S(2)}) copy-start(f32[2,1,6,3312]{3,1,2,0:T(1,128)} %param.21) | copy-start | bytes 476932
  5.6 11.0 %copy-start.10 = (bf16[2,138,276]{2,1,0:T(8,128)(2,1)S(1)}, bf16[2,138,276]{2,1,0:T(8,128)(2,1)}, u32[]{:S(2)}) copy-start(bf16[2,138,276]{2,1,0:T(8,128)(2,1)} %constant.13.clone.far_tcols.tcols_ref) | copy-start | bytes 457060
  5.7 10.9 %copy-start.11 = (bf16[2,96,192]{2,1,0:T(8,128)(2,1)S(1)}, bf16[2,96,192]{2,1,0:T(8,128)(2,1)}, u32[]{:S(2)}) copy-start(bf16[2,96,192]{2,1,0:T(8,128)(2,1)} %constant.12.clone.far_trows.trows_ref) | copy-start | bytes 221188
  7.5 12.6 %collective-permute-start = (bf16[288,384]{1,0:T(8,128)(2,1)S(1)}, bf16[288,384]{1,0:T(8,128)(2,1)S(1)}, u32[]{:S(2)}, u32[]{:S(2)}) collective-permute-start(bf16[288,384]{1,0:T(8,128)(2,1)S(1)} %get-tuple-element.93), channel_id=1, source_target_pairs={{8,0},{9,1},{10,2},{11,3},{12,4},{13,5},{14,6},{15,7},{16,8},{17,9... | collective-permute-start | bytes 663560 | tf_op jit(solution)/shard_map/ppermute | solution.py:599
  13.4 5.0 %collective-permute-start.1 = (bf16[64,384]{1,0:T(8,128)(2,1)S(1)}, bf16[64,384]{1,0:T(8,128)(2,1)S(1)}, u32[]{:S(2)}, u32[]{:S(2)}) collective-permute-start(bf16[64,384]{1,0:T(8,128)(2,1)S(1)} %get-tuple-element.94), channel_id=1, source_target_pairs={{1,0},{2,1},{3,2},{4,3},{5,4},{6,5},{7,6},{0,7},{9,8},{10,9},{11,1... | collective-permute-start | bytes 147464 | tf_op jit(solution)/shard_map/ppermute | solution.py:600
  16.6 3.5 %collective-permute-start.2 = (bf16[64,384]{1,0:T(8,128)(2,1)S(1)}, bf16[64,384]{1,0:T(8,128)(2,1)S(1)}, u32[]{:S(2)}, u32[]{:S(2)}) collective-permute-start(bf16[64,384]{1,0:T(8,128)(2,1)S(1)} %get-tuple-element.95), channel_id=1, source_target_pairs={{9,0},{10,1},{11,2},{12,3},{13,4},{14,5},{15,6},{8,7},{17,8},{18,9... | collective-permute-start | bytes 147464 | tf_op jit(solution)/shard_map/ppermute | solution.py:601
  17.8 2.4 %copy-start.2 = (bf16[2,192,576]{2,1,0:T(8,128)(2,1)S(1)}, bf16[2,192,576]{2,1,0:T(8,128)(2,1)}, u32[]{:S(2)}) copy-start(bf16[2,192,576]{2,1,0:T(8,128)(2,1)} %qkv_ref.3) | copy-start | bytes 1327108
  17.8 2.3 %copy-start.4 = (bf16[2,192,192]{2,1,0:T(8,128)(2,1)S(1)}, bf16[2,192,192]{2,1,0:T(8,128)(2,1)}, u32[]{:S(2)}) copy-start(bf16[2,192,192]{2,1,0:T(8,128)(2,1)} %out_ref.3) | copy-start | bytes 442372
  17.8 2.3 %copy-start.9 = (bf16[576,352]{1,0:T(8,128)(2,1)S(1)}, bf16[576,352]{1,0:T(8,128)(2,1)}, u32[]{:S(2)}) copy-start(bf16[576,352]{1,0:T(8,128)(2,1)} %constant.15.clone.pick_ref) | copy-start | bytes 1216516
  27.7 10.8 %collective-permute-start.5 = (bf16[288,384]{1,0:T(8,128)(2,1)S(1)}, bf16[288,384]{1,0:T(8,128)(2,1)S(1)}, u32[]{:S(2)}, u32[]{:S(2)}) collective-permute-start(bf16[288,384]{1,0:T(8,128)(2,1)S(1)} %get-tuple-element.99), channel_id=1, source_target_pairs={{120,0},{121,1},{122,2},{123,3},{124,4},{125,5},{126,6},{127,7},{0... | collective-permute-start | bytes 663560 | tf_op jit(solution)/shard_map/ppermute | solution.py:599
  27.8 6.9 %collective-permute-start.4 = (bf16[64,384]{1,0:T(8,128)(2,1)S(1)}, bf16[64,384]{1,0:T(8,128)(2,1)S(1)}, u32[]{:S(2)}, u32[]{:S(2)}) collective-permute-start(bf16[64,384]{1,0:T(8,128)(2,1)S(1)} %get-tuple-element.98), channel_id=1, source_target_pairs={{7,0},{0,1},{1,2},{2,3},{3,4},{4,5},{5,6},{6,7},{15,8},{8,9},{9,10... | collective-permute-start | bytes 147464 | tf_op jit(solution)/shard_map/ppermute | solution.py:600
  28.8 9.7 %collective-permute-start.3 = (bf16[64,384]{1,0:T(8,128)(2,1)S(1)}, bf16[64,384]{1,0:T(8,128)(2,1)S(1)}, u32[]{:S(2)}, u32[]{:S(2)}) collective-permute-start(bf16[64,384]{1,0:T(8,128)(2,1)S(1)} %get-tuple-element.97), channel_id=1, source_target_pairs={{127,0},{120,1},{121,2},{122,3},{123,4},{124,5},{125,6},{126,7},{7... | collective-permute-start | bytes 147464 | tf_op jit(solution)/shard_map/ppermute | solution.py:601
  28.9 9.7 %copy-start.8 = (bf16[576,352]{1,0:T(8,128)(2,1)S(1)}, bf16[576,352]{1,0:T(8,128)(2,1)}, u32[]{:S(2)}) copy-start(bf16[576,352]{1,0:T(8,128)(2,1)} %constant.16.clone.returned_ref) | copy-start | bytes 1216516
  44.2 2.6 %collective-permute-start.6 = (bf16[1856,128]{1,0:T(8,128)(2,1)S(1)}, bf16[1856,128]{1,0:T(8,128)(2,1)S(1)}, u32[]{:S(2)}, u32[]{:S(2)}) collective-permute-start(bf16[1856,128]{1,0:T(8,128)(2,1)S(1)} %get-tuple-element.136), channel_id=1, source_target_pairs={{8,0},{9,1},{10,2},{11,3},{12,4},{13,5},{14,6},{15,7},{0,8},{1,9},... | collective-permute-start | bytes 1425416 | tf_op jit(solution)/shard_map/ppermute | solution.py:627
  44.3 2.5 %collective-permute-start.7 = (bf16[1728,128]{1,0:T(8,128)(2,1)S(1)}, bf16[1728,128]{1,0:T(8,128)(2,1)S(1)}, u32[]{:S(2)}, u32[]{:S(2)}) collective-permute-start(bf16[1728,128]{1,0:T(8,128)(2,1)S(1)} %get-tuple-element.138), channel_id=1, source_target_pairs={{8,0},{9,1},{10,2},{11,3},{12,4},{13,5},{14,6},{15,7},{0,8},{1,9},... | collective-permute-start | bytes 1327112 | tf_op jit(solution)/shard_map/ppermute | solution.py:627
  47.9 20.8 %all-to-all-start = ((bf16[16,224,128]{2,1,0:T(8,128)(2,1)}), bf16[16,224,128]{2,1,0:T(8,128)(2,1)S(1)}, u32[]{:S(2)}, u32[]{:S(2)}) async-start(bf16[16,224,128]{2,1,0:T(8,128)(2,1)} %bitcast.6), calls=%async_computation | async-start | bytes 1835008 | tf_op jit(solution)/shard_map/all_to_all | solution.py:644
  68.8 4.2 %collective-permute-start.8 = (bf16[224,128]{1,0:T(8,128)(2,1)S(1)}, bf16[224,128]{1,0:T(8,128)(2,1)S(1)}, u32[]{:S(2)}, u32[]{:S(2)}) collective-permute-start(bf16[224,128]{1,0:T(8,128)(2,1)S(1)} %shard_map.207.refs_0_), channel_id=1, source_target_pairs={{2,0},{3,1},{4,2},{5,3},{6,4},{7,5},{0,6},{1,7},{10,8},{11,9},{12,... | collective-permute-start | bytes 172040 | tf_op jit(solution)/shard_map/ppermute | solution.py:627
  70.1 5.8 %collective-permute-start.9 = (bf16[224,128]{1,0:T(8,128)(2,1)S(1)}, bf16[224,128]{1,0:T(8,128)(2,1)S(1)}, u32[]{:S(2)}, u32[]{:S(2)}) collective-permute-start(bf16[224,128]{1,0:T(8,128)(2,1)S(1)} %shard_map.207.refs_0_), channel_id=1, source_target_pairs={{4,0},{5,1},{6,2},{7,3},{0,4},{1,5},{2,6},{3,7},{12,8},{13,9},{14,... | collective-permute-start | bytes 172040 | tf_op jit(solution)/shard_map/ppermute | solution.py:627
  70.1 6.2 %collective-permute-start.10 = (bf16[224,128]{1,0:T(8,128)(2,1)S(1)}, bf16[224,128]{1,0:T(8,128)(2,1)S(1)}, u32[]{:S(2)}, u32[]{:S(2)}) collective-permute-start(bf16[224,128]{1,0:T(8,128)(2,1)S(1)} %shard_map.207.refs_0_), channel_id=1, source_target_pairs={{6,0},{7,1},{0,2},{1,3},{2,4},{3,5},{4,6},{5,7},{14,8},{15,9},{8,1... | collective-permute-start | bytes 172040 | tf_op jit(solution)/shard_map/ppermute | solution.py:627
  71.1 6.2 %collective-permute-start.11 = (bf16[416,128]{1,0:T(8,128)(2,1)S(1)}, bf16[416,128]{1,0:T(8,128)(2,1)S(1)}, u32[]{:S(2)}, u32[]{:S(2)}) collective-permute-start(bf16[416,128]{1,0:T(8,128)(2,1)S(1)} %get-tuple-element.152.mine_ref), channel_id=1, source_target_pairs={{1,0},{0,1},{3,2},{2,3},{5,4},{4,5},{7,6},{6,7},{9,8},{8,9},{11,10... | collective-permute-start | bytes 319496 | tf_op jit(solution)/shard_map/ppermute | solution.py:627
  77.3 17.9 %all-to-all-start.1 = ((bf16[16,224,128]{2,1,0:T(8,128)(2,1)}), bf16[16,224,128]{2,1,0:T(8,128)(2,1)S(1)}, u32[]{:S(2)}, u32[]{:S(2)}) async-start(bf16[16,224,128]{2,1,0:T(8,128)(2,1)} %shard_map.208), calls=%async_computation.1 | async-start | bytes 1835008 | tf_op jit(solution)/shard_map/all_to_all | solution.py:652
  81.0 4.8 %collective-permute-start.12 = (bf16[416,128]{1,0:T(8,128)(2,1)S(1)}, bf16[416,128]{1,0:T(8,128)(2,1)S(1)}, u32[]{:S(2)}, u32[]{:S(2)}) collective-permute-start(bf16[416,128]{1,0:T(8,128)(2,1)S(1)} %shard_map.209.t0_ref), channel_id=1, source_target_pairs={{2,0},{3,1},{4,2},{5,3},{6,4},{7,5},{0,6},{1,7},{10,8},{11,9},{12,... | collective-permute-start | bytes 319496 | tf_op jit(solution)/shard_map/ppermute | solution.py:627
  82.5 6.2 %collective-permute-start.13 = (bf16[416,128]{1,0:T(8,128)(2,1)S(1)}, bf16[416,128]{1,0:T(8,128)(2,1)S(1)}, u32[]{:S(2)}, u32[]{:S(2)}) collective-permute-start(bf16[416,128]{1,0:T(8,128)(2,1)S(1)} %shard_map.209.t0_ref), channel_id=1, source_target_pairs={{4,0},{5,1},{6,2},{7,3},{0,4},{1,5},{2,6},{3,7},{12,8},{13,9},{14,... | collective-permute-start | bytes 319496 | tf_op jit(solution)/shard_map/ppermute | solution.py:627
  84.2 5.9 %collective-permute-start.14 = (bf16[416,128]{1,0:T(8,128)(2,1)S(1)}, bf16[416,128]{1,0:T(8,128)(2,1)S(1)}, u32[]{:S(2)}, u32[]{:S(2)}) collective-permute-start(bf16[416,128]{1,0:T(8,128)(2,1)S(1)} %shard_map.209.t0_ref), channel_id=1, source_target_pairs={{6,0},{7,1},{0,2},{1,3},{2,4},{3,5},{4,6},{5,7},{14,8},{15,9},{8,1... | collective-permute-start | bytes 319496 | tf_op jit(solution)/shard_map/ppermute | solution.py:627
  95.3 2.5 %collective-permute-start.15 = (bf16[3584,128]{1,0:T(8,128)(2,1)S(1)}, bf16[3584,128]{1,0:T(8,128)(2,1)S(1)}, u32[]{:S(2)}, u32[]{:S(2)}) collective-permute-start(bf16[3584,128]{1,0:T(8,128)(2,1)S(1)} %bitcast.10), channel_id=1, source_target_pairs={{8,0},{9,1},{10,2},{11,3},{12,4},{13,5},{14,6},{15,7},{0,8},{1,9},... | collective-permute-start | bytes 2752520 | tf_op jit(solution)/shard_map/ppermute | solution.py:627
